TPU v7x, 128 devices: a whole 4x4x4 slice. The times are simulated.
128 devices in a mesh: space: 8 (over z, core), dp: 16 (over x, y).
Axes of the slice: x: 4, y: 4, z: 4, core: 2. Of those that a mesh axis runs over, the one named last changes fastest.
Arguments:
- features: bfloat16 [32, 96, 100, 176], P('dp', 'space'), may hold values from -15 to 15
- w_expand: bfloat16 [176, 1056], P(None, 'dp'), may hold values from -0.4375 to 0.4375
- w_depth: bfloat16 [5, 5, 1056], P(None, None, 'dp'), may hold values from -1.25 to 1.25
- w_reduce: bfloat16 [1056, 44], P('dp'), may hold values from -0.375 to 0.375
- b_reduce: bfloat16 [44], replicated, may hold values from -4 to 4
- w_excite: bfloat16 [44, 1056], P(None, 'dp'), may hold values from -1.75 to 1.75
- b_excite: bfloat16 [1056], P('dp'), may hold values from -4 to 4
- w_project: bfloat16 [1056, 176], P('dp'), may hold values from -0.375 to 0.375
- cotangent: bfloat16 [32, 96, 100, 176], P('dp', 'space'), may hold values from -6 to 6
Outputs:
- output: bfloat16 [32, 96, 100, 176], P('dp', 'space')
- grad_features: bfloat16 [32, 96, 100, 176], P('dp', 'space')
- grad_expand: float32 [176, 1056], P(None, 'dp')
- grad_depth: float32 [5, 5, 1056], P(None, None, 'dp')
- grad_reduce: float32 [1056, 44], P('dp')
- grad_excite: float32 [44, 1056], P(None, 'dp')
- grad_bexcite: float32 [1056], P('dp')
- grad_project: float32 [1056, 176], P('dp')
- grad_breduce: float32 [44], replicated
All inputs are finite; a program needn't handle non-finite values.
Results may differ from a plain program's by a relative error of at most 0.0062.
Values may be sent and summed in bfloat16 or wider, within the bound.
A program may use at most 128 MiB of HBM per device.

v0:
```python
import jax
import jax.numpy as jnp
from jax import lax
from jax.sharding import PartitionSpec as P


def padded_2(cells, sides, width):
    for axis, dim in sides:
        count = lax.axis_size(axis)
        ends = count - 1
        head = lax.slice_in_dim(cells, 0, width, axis=dim)
        tail = lax.slice_in_dim(cells, cells.shape[dim] - width, cells.shape[dim], axis=dim)
        cells = jnp.concatenate(
            [
                lax.ppermute(tail, axis, [(i, (i + 1) % count) for i in range(ends)]),
                cells,
                lax.ppermute(head, axis, [((i + 1) % count, i) for i in range(ends)]),
            ],
            axis=dim,
        )
    return cells


def swish(value):
    return value * jax.nn.sigmoid(value)


def swish_grad(value):
    sig = jax.nn.sigmoid(value)
    return sig * (1.0 + value * (1.0 - sig))


def depthwise(padded, kernel, rows, cols):
    total = jnp.zeros((padded.shape[0], rows, cols, padded.shape[3]), jnp.float32)
    for i in range(5):
        for j in range(5):
            total = total + padded[:, i : i + rows, j : j + cols, :].astype(jnp.float32) * kernel[
                i, j
            ].astype(jnp.float32)
    return total


def depthwise_back(padded, kernel, rows, cols):
    total = jnp.zeros((padded.shape[0], rows, cols, padded.shape[3]), jnp.float32)
    for i in range(5):
        for j in range(5):
            total = total + padded[:, 4 - i : 4 - i + rows, 4 - j : 4 - j + cols, :].astype(
                jnp.float32
            ) * kernel[i, j].astype(jnp.float32)
    return total


def kernel_grad(ddepth, padded, rows, cols):
    parts = []
    for i in range(5):
        row_parts = []
        for j in range(5):
            row_parts.append(
                jnp.sum(
                    ddepth.astype(jnp.float32)
                    * padded[:, i : i + rows, j : j + cols, :].astype(jnp.float32),
                    axis=(0, 1, 2),
                )
            )
        parts.append(jnp.stack(row_parts))
    return jnp.stack(parts)


def hdot(left, right):
    return jnp.dot(left, right, precision=lax.Precision.HIGHEST)


def own_slice(array, dim, count, index):
    width = array.shape[dim] // count
    return lax.dynamic_slice_in_dim(array, index * width, width, dim)


def on_device(
    features, w_expand, w_depth, w_reduce, b_reduce, w_excite, b_excite, w_project, cotangent
):
    full_expand, full_depth, full_reduce, full_excite, full_bexcite, full_project = (
        lax.all_gather(w_expand, "dp", axis=1, tiled=True),
        lax.all_gather(w_depth, "dp", axis=2, tiled=True),
        lax.all_gather(w_reduce, "dp", axis=0, tiled=True),
        lax.all_gather(w_excite, "dp", axis=1, tiled=True),
        lax.all_gather(b_excite, "dp", axis=0, tiled=True),
        lax.all_gather(w_project, "dp", axis=0, tiled=True),
    )
    batch, rows, cols, chans = features.shape
    wide = full_expand.shape[1]
    flat = features.reshape(-1, chans)
    pre = jnp.dot(flat, full_expand, preferred_element_type=jnp.float32).reshape(
        batch, rows, cols, wide
    )
    expanded = swish(pre).astype(jnp.bfloat16)
    ext_rows = padded_2(expanded, (("space", 1),), 2)
    padded = jnp.pad(ext_rows, ((0, 0), (0, 0), (2, 2), (0, 0)))
    depth = depthwise(padded, full_depth, rows, cols)
    act = swish(depth)
    area = rows * lax.axis_size("space") * cols
    pooled = lax.psum(jnp.sum(act, axis=(1, 2)), "space") / area
    wr = full_reduce.astype(jnp.float32)
    wx = full_excite.astype(jnp.float32)
    squeeze_pre = hdot(pooled, wr) + b_reduce.astype(jnp.float32)
    squeeze = swish(squeeze_pre)
    gate = jax.nn.sigmoid(hdot(squeeze, wx) + full_bexcite.astype(jnp.float32))
    gated = (act * gate[:, None, None, :]).astype(jnp.bfloat16)
    gflat = gated.reshape(-1, wide)
    output = (
        features.astype(jnp.float32)
        + jnp.dot(gflat, full_project, preferred_element_type=jnp.float32).reshape(features.shape)
    ).astype(jnp.bfloat16)
    dflat = cotangent.reshape(-1, chans)
    dgated = jnp.dot(dflat, full_project.T, preferred_element_type=jnp.float32).reshape(
        batch, rows, cols, wide
    )
    g_project = jnp.dot(gflat.T, dflat, preferred_element_type=jnp.float32)
    dgate = lax.psum(jnp.sum(dgated * act, axis=(1, 2)), "space")
    dlogit = dgate * gate * (1.0 - gate)
    leader = (lax.axis_index("space") == 0).astype(jnp.float32)
    g_excite = hdot(squeeze.T, dlogit) * leader
    g_bexcite = jnp.sum(dlogit, axis=0) * leader
    dsq_pre = hdot(dlogit, wx.T) * swish_grad(squeeze_pre)
    g_reduce = hdot(pooled.T, dsq_pre) * leader
    g_breduce = jnp.sum(dsq_pre, axis=0) * leader
    dpooled = hdot(dsq_pre, wr.T)
    ddepth = (
        (dgated * gate[:, None, None, :] + dpooled[:, None, None, :] / area) * swish_grad(depth)
    ).astype(jnp.bfloat16)
    g_depth = kernel_grad(ddepth, padded, rows, cols)
    drimmed = padded_2(ddepth, (("space", 1),), 2)
    dpadded = jnp.pad(drimmed, ((0, 0), (0, 0), (2, 2), (0, 0)))
    dexp = depthwise_back(dpadded, full_depth, rows, cols)
    dpre = (dexp * swish_grad(pre)).astype(jnp.bfloat16)
    pflat = dpre.reshape(-1, wide)
    grad_features = (
        cotangent.astype(jnp.float32)
        + jnp.dot(pflat, full_expand.T, preferred_element_type=jnp.float32).reshape(features.shape)
    ).astype(jnp.bfloat16)
    g_expand = jnp.dot(flat.T, pflat, preferred_element_type=jnp.float32)
    t_expand, t_depth, t_reduce, t_excite, t_bexcite, t_project, s_breduce = lax.psum(
        (g_expand, g_depth, g_reduce, g_excite, g_bexcite, g_project, g_breduce), ("space", "dp")
    )
    count = lax.axis_size("dp")
    index = lax.axis_index("dp")
    s_expand = own_slice(t_expand, 1, count, index)
    s_depth = own_slice(t_depth, 2, count, index)
    s_reduce = own_slice(t_reduce, 0, count, index)
    s_excite = own_slice(t_excite, 1, count, index)
    s_bexcite = own_slice(t_bexcite, 0, count, index)
    s_project = own_slice(t_project, 0, count, index)
    return (
        output,
        grad_features,
        s_expand,
        s_depth,
        s_reduce,
        s_excite,
        s_bexcite,
        s_project,
        s_breduce,
    )


def solution(mesh):
    return jax.shard_map(
        on_device,
        mesh=mesh,
        in_specs=(
            P("dp", "space", None, None),
            P(None, "dp"),
            P(None, None, "dp"),
            P("dp", None),
            P(),
            P(None, "dp"),
            P("dp"),
            P("dp", None),
            P("dp", "space", None, None),
        ),
        out_specs=(
            P("dp", "space", None, None),
            P("dp", "space", None, None),
            P(None, "dp"),
            P(None, None, "dp"),
            P("dp", None),
            P(None, "dp"),
            P("dp"),
            P("dp", None),
            P(),
        ),
        check_vma=False,
    )
```

profile of v0, /device:TPU:1, one launch (start us, length us, event | category | flops | bytes accessed | tf_op | source)
XLA Modules:
  0.0 734.2 jit_solution(4624606730477053963)
XLA Ops:
  7.2 20.1 %all-gather = bf16[16,66,176]{2,1,0:T(8,128)(2,1)S(1)} all-gather(bf16[1,66,176]{2,1,0:T(8,128)(2,1)} %bitcast.65), channel_id=1, replica_groups=mesh['space'=8,'dp'=16] {'dp'}, dimensions={0}, use_global_device_ids=true | all-gather | bytes 394944 | tf_op jit(solution)/shard_map/all_gather | solution.py:82
  27.6 8.3 %multiply_convert_fusion.2 = (bf16[2,12,100,1056]{3,2,1,0:T(8,128)(2,1)S(1)}, f32[2,12,100,1056]{3,2,1,0:T(8,128)}) fusion(bf16[2,12,100,176]{2,3,1,0:T(8,128)(2,1)} %param.9, bf16[1056,176]{1,0:T(8,128)(2,1)S(1)} %reshape.256), kind=kOutput, calls=%fused_computation.122 | convolution fusion | flops 904780800 | bytes 16422912 | tf_op jit(solution)/shard_map/dot_general | solution.py:92
  35.9 2.5 copy-done
  38.6 1.6 copy.46
  40.2 7.7 %collective-permute-start.1 = (bf16[2,2,100,1056]{3,1,2,0:T(2,128)(2,1)}, bf16[2,2,100,1056]{3,1,2,0:T(2,128)(2,1)}, u32[]{:S(2)}, u32[]{:S(2)}) collective-permute-start(bf16[2,2,100,1056]{3,1,2,0:T(2,128)(2,1)} %copy.46), channel_id=1, source_target_pairs={{16,0},{32,16},{48,32},{64,48},{80,64},{96,80},{112,96},{17,1},{33... | collective-permute-start | bytes 2534408 | tf_op jit(solution)/shard_map/ppermute | solution.py:17
  47.9 1.6 copy.45
  49.6 3.4 collective-permute-start
  53.2 22.8 %all_gather.19 = bf16[5,5,1056]{1,0,2:T(8,128)(2,1)S(1)} all-gather(bf16[5,5,66]{1,0,2:T(8,128)(2,1)S(1)} %copy.49), channel_id=1, replica_groups=mesh['space'=8,'dp'=16] {'dp'}, dimensions={2}, use_global_device_ids=true | all-gather | bytes 56100 | tf_op jit(solution)/shard_map/all_gather | solution.py:83
  76.0 67.0 %fusion.100 = (f32[1056]{0:T(1024)S(1)}, f32[1056]{0:T(1024)S(1)}, f32[1056]{0:T(1024)S(1)}, f32[1056]{0:T(1024)S(1)}, f32[1056]{0:T(1024)S(1)}, /*index=5*/f32[...) fusion(bf16[5,5,1056]{1,0,2:T(8,128)(2,1)S(1)} %all_gather.19), kind=kLoop, calls=%fused_computation.210 | loop fusion | flops 20064 | bytes 120384 | tf_op jit(solution)/shard_map/convert_element_type | solution.py:39
  145.0 30.9 %all-reduce.2 = bf16[1056]{0:T(1024)(128)(2,1)S(1)} all-reduce(bf16[1056]{0:T(1024)(128)(2,1)S(1)} %dynamic-update-slice), channel_id=1, replica_groups=mesh['space'=8,'dp'=16] {'dp'}, use_global_device_ids=true, to_apply=%add.2 | all-reduce | flops 1056 | bytes 4224
  175.9 0.6 convert_element_type.591
  176.5 15.9 %all-gather.1 = bf16[16,66,44]{1,2,0:T(8,128)(2,1)S(1)} all-gather(bf16[1,66,44]{1,2,0:T(8,128)(2,1)S(1)} %bitcast.67), channel_id=1, replica_groups=mesh['space'=8,'dp'=16] {'dp'}, dimensions={0}, use_global_device_ids=true | all-gather | bytes 98736 | tf_op jit(solution)/shard_map/all_gather | solution.py:84
  192.7 18.8 %all-gather.2 = bf16[16,66,44]{1,2,0:T(8,128)(2,1)S(1)} all-gather(bf16[1,66,44]{1,2,0:T(8,128)(2,1)S(1)} %bitcast.68), channel_id=1, replica_groups=mesh['space'=8,'dp'=16] {'dp'}, dimensions={0}, use_global_device_ids=true | all-gather | bytes 98736 | tf_op jit(solution)/shard_map/all_gather | solution.py:85
  211.8 16.2 %all-gather.3 = bf16[16,66,176]{2,1,0:T(8,128)(2,1)S(1)} all-gather(bf16[1,66,176]{2,1,0:T(8,128)(2,1)S(1)} %bitcast.66), channel_id=1, replica_groups=mesh['space'=8,'dp'=16] {'dp'}, dimensions={0}, use_global_device_ids=true | all-gather | bytes 394944 | tf_op jit(solution)/shard_map/all_gather | solution.py:87
  228.1 1.0 reshape.257
  229.1 17.8 %fusion.99 = (f32[1056]{0:T(1024)S(1)}, f32[1056]{0:T(1024)S(1)}, f32[1056]{0:T(1024)S(1)}, f32[1056]{0:T(1024)S(1)}, f32[1056]{0:T(1024)S(1)}, /*index=5*/f32[1056]{0:T(1024)S(1)}) fusion(bf16[5,5,1056]{1,0,2:T(8,128)(2,1)S(1)} %all_gather.19), kind=kLoop, calls=%fused_computation.208 | loop fusion | flops 6336 | bytes 38016 | tf_op jit(solution)/shard_map/convert_element_type | solution.py:39
  246.9 1.3 copy.48
  248.3 1.3 copy.47
  249.6 9.7 %select_maximum_fusion.2 = bf16[2,16,104,1056]{3,2,1,0:T(8,128)(2,1)} fusion(bf16[2,2,100,1056]{3,2,1,0:T(8,128)(2,1)S(1)} %copy.48, bf16[2,12,100,1056]{3,2,1,0:T(8,128)(2,1)} %copy-done, bf16[2,2,100,1056]{3,2,1,0:T(8,128)(2,1)S(1)} %copy.47), kind=kLoop, calls=%fused_computation.127 | loop fusion | flops 42172416 | bytes 13787136 | tf_op jit(solution)/shard_map/concatenate | solution.py:13
  259.3 74.7 %multiply_reduce_fusion = (f32[2,1056]{1,0:T(2,128)S(1)}, f32[2,1056]{1,0:T(2,128)S(1)}, f32[2,12,100,1056]{3,2,1,0:T(8,128)}, f32[2,12,100,1056]{3,2,1,0:T(8,128)}) fusion(f32[1056]{0:T(1024)S(1)} %get-tuple-element.77, bf16[2,16,104,1056]{3,2,1,0:T(8,128)(2,1)} %select_maximum_fusion.2, f32[1056]{0:T(1024)S(1)} %get-tuple-element.78, ...), kind=kOutput, calls=%fused_computation.118 | convolution fusion | flops 1107528704 | bytes 129748608 | tf_op jit(solution)/shard_map/dot_general | solution.py:114
  334.0 48.3 %all-reduce.5 = (f32[2,1056]{1,0:T(2,128)S(1)}, f32[2,1056]{1,0:T(2,128)S(1)}) all-reduce(f32[2,1056]{1,0:T(2,128)S(1)} %get-tuple-element.73, f32[2,1056]{1,0:T(2,128)S(1)} %get-tuple-element.72), channel_id=1, replica_groups=mesh['space'=8,'dp'=16] {'space'}, use_global_device_ids=true, to_apply=%region_1.2 | all-reduce | flops 4224 | bytes 33792 | tf_op jit(solution)/shard_map/psum | solution.py:101
  382.5 0.8 fusion.115
  383.3 0.7 fusion.122
  384.2 1.1 convolution_multiply_fusion
  385.4 1.1 convolution_multiply_fusion.1
  386.4 9.5 %add_convert_fusion.1 = bf16[2,12,100,176]{2,3,1,0:T(8,128)(2,1)} fusion(bf16[2,12,100,176]{2,3,1,0:T(8,128)(2,1)} %param.9, f32[2,1056]{1,0:T(2,128)S(1)} %get-tuple-element.120, bf16[1056,176]{1,0:T(8,128)(2,1)S(1)} %copy-done.3, f32[2,12,100,1056]{3,2,1,0:T(8,128)} %get-tuple-element.111), kind=kOutput, calls=%fused_computation.158 | convolution fusion | flops 908582400 | bytes 12207360 | tf_op jit(solution)/shard_map/dot_general | solution.py:111
  396.0 5.1 convolution_bitcast_fusion
  401.0 39.0 %fusion.63 = (f32[1056]{0:T(1024)}, f32[1056]{0:T(1024)}, f32[1056]{0:T(1024)}, f32[1056]{0:T(1024)}, f32[1056]{0:T(1024)}, /*index=5*/f32[1056]{0:T(1024)}, f32...) fusion(bf16[2,16,104,1056]{3,2,1,0:T(8,128)(2,1)S(1)} %bitcast., ...), kind=kLoop, calls=%fused_computation.116 | loop fusion | flops 167251392 | bytes 116675328 | tf_op jit(solution)/shard_map/reduce_sum | solution.py:59
  440.2 16.2 %fusion.61 = (f32[1056]{0:T(1024)S(1)}, f32[1056]{0:T(1024)S(1)}, f32[1056]{0:T(1024)S(1)}, f32[1056]{0:T(1024)S(1)}, f32[1056]{0:T(1024)S(1)}, /*index=5*/f32[1056]{0:T(1024)S(1)}, f32[1056]{0:T(1024)S(1)}) fusion(bf16[2,12,100,1056]{3,2,1,0:T(8,128)(2,1)} %get-tuple-element.110, bf16[2,2,100,1056]{3,2,1,0:T(8,128)(2,1)S(1)} %copy.48, ...), kind=kLoop, calls=%fused_computation.114 | loop fusion | flops 65887008 | bytes 21994368 | tf_op jit(solution)/shard_map/reduce_sum | solution.py:59
  456.4 1.6 fusion.120
  459.2 0.6 stack.115
  461.6 0.6 stack.122
  462.8 0.6 stack.125
  465.2 0.6 stack.132
  466.4 0.6 stack.136
  470.1 0.6 bitcast_dynamic-update-slice_fusion.4
  470.7 1.6 copy.56
  472.3 0.7 copy.55
  473.0 3.6 collective-permute-start.2
  476.7 4.1 collective-permute-start.3
  480.7 0.8 stack.120
  481.5 0.6 bitcast_dynamic-update-slice_fusion.3
  482.1 0.8 stack.127
  482.9 0.6 bitcast_dynamic-update-slice_fusion.2
  483.5 0.8 stack.134
  484.3 0.8 stack.141
  485.1 0.6 bitcast_dynamic-update-slice_fusion.1
  485.7 0.6 bitcast_dynamic-update-slice_fusion
  486.3 0.7 collective-permute-done.2
  487.0 1.3 copy.57
  488.3 3.4 collective-permute-done.3
  491.7 1.3 copy.58
  493.0 8.3 %select_maximum_fusion = bf16[2,16,104,1056]{3,2,1,0:T(8,128)(2,1)S(1)} fusion(bf16[2,2,100,1056]{3,2,1,0:T(8,128)(2,1)S(1)} %copy.58, bf16[2,12,100,1056]{3,2,1,0:T(8,128)(2,1)} %get-tuple-element.110, bf16[2,2,100,1056]{3,2,1,0:T(8,128)(2,1)S(1)} %copy.57), kind=kLoop, calls=%fused_computation.125 | loop fusion | flops 42172416 | bytes 13787136 | tf_op jit(solution)/shard_map/concatenate | solution.py:13
  501.3 61.6 %fusion.65 = bf16[2,12,100,1056]{3,2,1,0:T(8,128)(2,1)} fusion(f32[2,12,100,1056]{3,2,1,0:T(8,128)} %get-tuple-element.117, bf16[2,12,100,1056]{3,2,1,0:T(8,128)(2,1)S(1)} %bitcast.62, bf16[2,2,100,1056]{3,2,1,0:T(8,128)(2,1)S(1)} %copy.57, bf16[2,2,100,1056]{3,2,1,0:T(8,128)(2,1)S(1)} %copy.58, bf16[2,16,104,1056]{3,2,1,0:T(8,128)(2,1)S(1)} %select_maximum_fusion, ...), kind=kLoop, calls=%fused_computation.124 | loop fusion | flops 220492800 | bytes 123446400 | tf_op jit(solution)/shard_map/convert_element_type | solution.py:134
  563.0 5.3 convolution_bitcast_fusion.1
  568.3 64.9 %all-reduce.3 = (f32[1056]{0:T(1024)S(1)}, f32[44]{0:T(128)}) all-reduce(f32[1056]{0:T(1024)S(1)} %broadcast_multiply_fusion, f32[44]{0:T(128)S(1)} %broadcast_multiply_fusion.1), channel_id=1, replica_groups=mesh['space'=8,'dp'=16] {'space','dp'}, use_global_device_ids=true, to_apply=%region_34.35 | all-reduce | flops 1100 | bytes 8800 | tf_op jit(solution)/shard_map/psum | solution.py:141
  633.8 6.1 add_convert_fusion
  640.0 79.5 %all-reduce.8.cloned.1.call-done = (f32[176,1056]{1,0:T(8,128)}, f32[5,5,1056]{2,1,0:T(8,128)}, f32[1056,44]{0,1:T(8,128)}, f32[44,1056]{1,0:T(8,128)}, f32[1056,176]{1,0:T(8,128)}) async-done(((f32[176,1056]{1,0:T(8,128)}, f32[5,5,1056]{2,1,0:T(8,128)}, f32[1056,44]{0,1:T(8,128)}, f32[44,1056]{1,0:T(8,128)}, f32[1056,176]{1,0:T(8,128)}), (f32[176,1056]{1,0:T(8,128)}, f32[5,5,1056]{2,1,0:T(8,128)}, ...) | async-done | bytes 1964176 | tf_op jit(solution)/shard_map/psum | solution.py:141
  719.5 1.0 constant_dynamic-slice_fusion.4
  720.5 0.7 copy.61
  721.3 1.5 constant_dynamic-slice_fusion.3
  722.7 1.5 constant_dynamic-slice_fusion.2
  724.2 1.5 constant_dynamic-slice_fusion.1
  725.7 1.5 constant_dynamic-slice_fusion
  (129 shorter events, 12.6 us)
Async XLA Ops:
  7.2 712.3 %all-reduce.8.cloned.1.call-start = ((), (), s32[]{:S(2)}) async-start(), calls=%async_computation | async-start | bytes 5038080 | tf_op jit(solution)/shard_map/psum | solution.py:141
  27.6 8.3 %copy-start.1 = (bf16[1056,176]{1,0:T(8,128)(2,1)}, bf16[1056,176]{1,0:T(8,128)(2,1)S(1)}, u32[]{:S(2)}) copy-start(bf16[1056,176]{1,0:T(8,128)(2,1)S(1)} %reshape.256) | copy-start | bytes 1115140
  27.6 25.4 %copy-start.26 = (bf16[5,5,66]{2,1,0:T(8,128)(2,1)S(1)}, bf16[5,5,66]{2,1,0:T(8,128)(2,1)}, u32[]{:S(2)}) copy-start(bf16[5,5,66]{2,1,0:T(8,128)(2,1)} %param.11) | copy-start | bytes 9904
  35.9 2.5 copy-start
  35.9 107.1 %copy-start.31 = (bf16[44]{0:T(256)(128)(2,1)S(1)}, bf16[44]{0:T(256)(128)(2,1)}, u32[]{:S(2)}) copy-start(bf16[44]{0:T(256)(128)(2,1)} %param.13) | copy-start | bytes 268
  35.9 107.6 %copy-start.34 = (u32[128]{0:T(128)S(1)}, u32[128]{0:T(128)}, u32[]{:S(2)}) copy-start(u32[128]{0:T(128)} %constant.42) | copy-start | bytes 1540
  35.9 108.9 %copy-start.32 = (bf16[66]{0:T(256)(128)(2,1)S(1)}, bf16[66]{0:T(256)(128)(2,1)}, u32[]{:S(2)}) copy-start(bf16[66]{0:T(256)(128)(2,1)} %param.15) | copy-start | bytes 400
  35.9 140.6 %copy-start.24 = (bf16[66,44]{0,1:T(8,128)(2,1)S(1)}, bf16[66,44]{0,1:T(8,128)(2,1)}, u32[]{:S(2)}) copy-start(bf16[66,44]{0,1:T(8,128)(2,1)} %param.12) | copy-start | bytes 17428
  35.9 156.8 %copy-start.25 = (bf16[44,66]{1,0:T(8,128)(2,1)S(1)}, bf16[44,66]{1,0:T(8,128)(2,1)}, u32[]{:S(2)}) copy-start(bf16[44,66]{1,0:T(8,128)(2,1)} %param.14) | copy-start | bytes 17428
  35.9 175.9 %copy-start.4 = (bf16[66,176]{1,0:T(8,128)(2,1)S(1)}, bf16[66,176]{1,0:T(8,128)(2,1)}, u32[]{:S(2)}) copy-start(bf16[66,176]{1,0:T(8,128)(2,1)} %param.16) | copy-start | bytes 69700
  40.2 206.7 %collective-permute-start.1 = (bf16[2,2,100,1056]{3,1,2,0:T(2,128)(2,1)}, bf16[2,2,100,1056]{3,1,2,0:T(2,128)(2,1)}, u32[]{:S(2)}, u32[]{:S(2)}) collective-permute-start(bf16[2,2,100,1056]{3,1,2,0:T(2,128)(2,1)} %copy.46), channel_id=1, source_target_pairs={{16,0},{32,16},{48,32},{64,48},{80,64},{96,80},{112,96},{17,1},{33... | collective-permute-start | bytes 2534408 | tf_op jit(solution)/shard_map/ppermute | solution.py:17
  49.6 198.7 %collective-permute-start = (bf16[2,2,100,1056]{3,1,2,0:T(2,128)(2,1)}, bf16[2,2,100,1056]{3,1,2,0:T(2,128)(2,1)}, u32[]{:S(2)}, u32[]{:S(2)}) collective-permute-start(bf16[2,2,100,1056]{3,1,2,0:T(2,128)(2,1)} %copy.45), channel_id=1, source_target_pairs={{0,16},{16,32},{32,48},{48,64},{64,80},{80,96},{96,112},{1,17},{17... | collective-permute-start | bytes 2534408 | tf_op jit(solution)/shard_map/ppermute | solution.py:15
  143.0 116.3 %copy-start.5 = (f32[1056]{0:T(1024)}, f32[1056]{0:T(1024)S(1)}, u32[]{:S(2)}) copy-start(f32[1056]{0:T(1024)S(1)} %get-tuple-element.80) | copy-start | bytes 12676
  246.9 12.4 %copy-start.3 = (bf16[1056,176]{1,0:T(8,128)(2,1)S(1)}, bf16[1056,176]{1,0:T(8,128)(2,1)}, u32[]{:S(2)}) copy-start(bf16[1056,176]{1,0:T(8,128)(2,1)} %reshape.257) | copy-start | bytes 1115140
  259.3 123.0 %copy-start.35 = (f32[44]{0:T(128)S(1)}, f32[44]{0:T(128)}, u32[]{:S(2)}) copy-start(f32[44]{0:T(128)} %convert_element_type.590) | copy-start | bytes 532
  259.3 123.2 %copy-start.27 = (f32[1056]{0:T(1024)S(1)}, f32[1056]{0:T(1024)}, u32[]{:S(2)}) copy-start(f32[1056]{0:T(1024)} %convert_element_type.591) | copy-start | bytes 12676
  384.1 11.9 %slice-start.4 = ((s8[11501568]{0:T(1024)(128)(4,1)}), s8[4194304]{0:T(1024)(128)(4,1)S(1)}, s32[]{:S(2)}) async-start(s8[11501568]{0:T(1024)(128)(4,1)} %bitcast.63), calls=%async_computation.5 | async-start | bytes 8388608
  386.4 9.5 %slice-start.5 = ((s8[11501568]{0:T(1024)(128)(4,1)}), s8[4194304]{0:T(1024)(128)(4,1)S(1)}, s32[]{:S(2)}) async-start(s8[11501568]{0:T(1024)(128)(4,1)} %bitcast.63), calls=%async_computation.6 | async-start | bytes 8388608
  386.4 9.5 %slice-start.6 = ((s8[11501568]{0:T(1024)(128)(4,1)}), s8[3112960]{0:T(1024)(128)(4,1)S(1)}, s32[]{:S(2)}) async-start(s8[11501568]{0:T(1024)(128)(4,1)} %bitcast.63), calls=%async_computation.7 | async-start | bytes 6225920
  386.4 9.5 %copy-start.29 = (bf16[2,12,100,176]{2,3,1,0:T(8,128)(2,1)S(1)}, bf16[2,12,100,176]{2,3,1,0:T(8,128)(2,1)}, u32[]{:S(2)}) copy-start(bf16[2,12,100,176]{2,3,1,0:T(8,128)(2,1)} %param.17) | copy-start | bytes 2534404
  386.4 14.6 %slice-start = ((s8[7667712]{0:T(1024)(128)(4,1)}), s8[4194304]{0:T(1024)(128)(4,1)S(1)}, s32[]{:S(2)}) async-start(s8[7667712]{0:T(1024)(128)(4,1)} %bitcast.59), calls=%async_computation.1 | async-start | bytes 8388608
  396.0 5.1 slice-start.1
  440.1 18.6 %copy-start.23 = (f32[1056]{0:T(1024)S(1)}, f32[1056]{0:T(1024)}, u32[]{:S(2)}) copy-start(f32[1056]{0:T(1024)} %get-tuple-element.45) | copy-start | bytes 12676
  440.1 19.2 %copy-start.22 = (f32[1056]{0:T(1024)S(1)}, f32[1056]{0:T(1024)}, u32[]{:S(2)}) copy-start(f32[1056]{0:T(1024)} %get-tuple-element.46) | copy-start | bytes 12676
  440.1 19.2 %copy-start.21 = (f32[1056]{0:T(1024)S(1)}, f32[1056]{0:T(1024)}, u32[]{:S(2)}) copy-start(f32[1056]{0:T(1024)} %get-tuple-element.47) | copy-start | bytes 12676
  440.1 19.8 %copy-start.20 = (f32[1056]{0:T(1024)S(1)}, f32[1056]{0:T(1024)}, u32[]{:S(2)}) copy-start(f32[1056]{0:T(1024)} %get-tuple-element.48) | copy-start | bytes 12676
  440.1 20.4 %copy-start.19 = (f32[1056]{0:T(1024)S(1)}, f32[1056]{0:T(1024)}, u32[]{:S(2)}) copy-start(f32[1056]{0:T(1024)} %get-tuple-element.49) | copy-start | bytes 12676
  440.1 21.0 %copy-start.18 = (f32[1056]{0:T(1024)S(1)}, f32[1056]{0:T(1024)}, u32[]{:S(2)}) copy-start(f32[1056]{0:T(1024)} %get-tuple-element.50) | copy-start | bytes 12676
  440.1 21.5 %copy-start.17 = (f32[1056]{0:T(1024)S(1)}, f32[1056]{0:T(1024)}, u32[]{:S(2)}) copy-start(f32[1056]{0:T(1024)} %get-tuple-element.51) | copy-start | bytes 12676
  440.1 22.1 %copy-start.16 = (f32[1056]{0:T(1024)S(1)}, f32[1056]{0:T(1024)}, u32[]{:S(2)}) copy-start(f32[1056]{0:T(1024)} %get-tuple-element.52) | copy-start | bytes 12676
  440.1 22.7 %copy-start.15 = (f32[1056]{0:T(1024)S(1)}, f32[1056]{0:T(1024)}, u32[]{:S(2)}) copy-start(f32[1056]{0:T(1024)} %get-tuple-element.53) | copy-start | bytes 12676
  440.1 23.3 %copy-start.14 = (f32[1056]{0:T(1024)S(1)}, f32[1056]{0:T(1024)}, u32[]{:S(2)}) copy-start(f32[1056]{0:T(1024)} %get-tuple-element.54) | copy-start | bytes 12676
  440.1 23.9 %copy-start.13 = (f32[1056]{0:T(1024)S(1)}, f32[1056]{0:T(1024)}, u32[]{:S(2)}) copy-start(f32[1056]{0:T(1024)} %get-tuple-element.55) | copy-start | bytes 12676
  440.1 24.5 %copy-start.12 = (f32[1056]{0:T(1024)S(1)}, f32[1056]{0:T(1024)}, u32[]{:S(2)}) copy-start(f32[1056]{0:T(1024)} %get-tuple-element.56) | copy-start | bytes 12676
  440.1 25.1 %copy-start.11 = (f32[1056]{0:T(1024)S(1)}, f32[1056]{0:T(1024)}, u32[]{:S(2)}) copy-start(f32[1056]{0:T(1024)} %get-tuple-element.57) | copy-start | bytes 12676
  440.1 25.7 %copy-start.10 = (f32[1056]{0:T(1024)S(1)}, f32[1056]{0:T(1024)}, u32[]{:S(2)}) copy-start(f32[1056]{0:T(1024)} %get-tuple-element.58) | copy-start | bytes 12676
  440.2 26.2 %copy-start.9 = (f32[1056]{0:T(1024)S(1)}, f32[1056]{0:T(1024)}, u32[]{:S(2)}) copy-start(f32[1056]{0:T(1024)} %get-tuple-element.59) | copy-start | bytes 12676
  440.2 26.8 %copy-start.8 = (f32[1056]{0:T(1024)S(1)}, f32[1056]{0:T(1024)}, u32[]{:S(2)}) copy-start(f32[1056]{0:T(1024)} %get-tuple-element.60) | copy-start | bytes 12676
  440.2 27.4 %copy-start.7 = (f32[1056]{0:T(1024)S(1)}, f32[1056]{0:T(1024)}, u32[]{:S(2)}) copy-start(f32[1056]{0:T(1024)} %get-tuple-element.61) | copy-start | bytes 12676
  440.2 28.0 %copy-start.6 = (f32[1056]{0:T(1024)S(1)}, f32[1056]{0:T(1024)}, u32[]{:S(2)}) copy-start(f32[1056]{0:T(1024)} %get-tuple-element.62) | copy-start | bytes 12676
  470.7 30.6 %slice-start.2 = ((s8[5750784]{0:T(1024)(128)(4,1)}), s8[1556480]{0:T(1024)(128)(4,1)S(1)}, s32[]{:S(2)}) async-start(s8[5750784]{0:T(1024)(128)(4,1)} %bitcast.61), calls=%async_computation.3 | async-start | bytes 3112960
  473.0 14.0 %collective-permute-start.2 = (bf16[2,2,100,1056]{3,1,2,0:T(2,128)(2,1)S(1)}, bf16[2,2,100,1056]{3,1,2,0:T(2,128)(2,1)}, u32[]{:S(2)}, u32[]{:S(2)}) collective-permute-start(bf16[2,2,100,1056]{3,1,2,0:T(2,128)(2,1)S(1)} %copy.55), channel_id=1, source_target_pairs={{0,16},{16,32},{32,48},{48,64},{64,80},{80,96},{96,112},{1,17},{17... | collective-permute-start | bytes 2534408 | tf_op jit(solution)/shard_map/ppermute | solution.py:15
  476.7 15.1 %collective-permute-start.3 = (bf16[2,2,100,1056]{3,1,2,0:T(2,128)(2,1)}, bf16[2,2,100,1056]{3,1,2,0:T(2,128)(2,1)}, u32[]{:S(2)}, u32[]{:S(2)}) collective-permute-start(bf16[2,2,100,1056]{3,1,2,0:T(2,128)(2,1)} %copy.56), channel_id=1, source_target_pairs={{16,0},{32,16},{48,32},{64,48},{80,64},{96,80},{112,96},{17,1},{33... | collective-permute-start | bytes 2534408 | tf_op jit(solution)/shard_map/ppermute | solution.py:17
  493.0 8.3 %slice-start.3 = ((s8[5750784]{0:T(1024)(128)(4,1)}), s8[4194304]{0:T(1024)(128)(4,1)S(1)}, s32[]{:S(2)}) async-start(s8[5750784]{0:T(1024)(128)(4,1)} %bitcast.61), calls=%async_computation.4 | async-start | bytes 8388608
  562.9 5.4 copy-start.33
  562.9 5.4 copy-start.28
  562.9 70.9 %copy-start.2 = (bf16[1056,176]{1,0:T(8,128)(2,1)S(1)}, bf16[1056,176]{1,0:T(8,128)(2,1)}, u32[]{:S(2)}) copy-start(bf16[1056,176]{1,0:T(8,128)(2,1)} %copy-done.1) | copy-start | bytes 1115140
  562.9 70.9 %copy-start.30 = (bf16[2,12,100,176]{2,3,1,0:T(8,128)(2,1)S(1)}, bf16[2,12,100,176]{2,3,1,0:T(8,128)(2,1)}, u32[]{:S(2)}) copy-start(bf16[2,12,100,176]{2,3,1,0:T(8,128)(2,1)} %param.17) | copy-start | bytes 2534404
Sparse Core Ops, SparseCore 0:
  568.4 151.0 all-reduce.7
where the time goes:
time: 739 us; the launch traced here: 734 us
  blocking collectives  238 us (32%)
  other arithmetic  221 us (30%)
  matrix products  113 us (15%)
  waiting for transfers between devices  83.6 us (11%)
  local copies, waits for them, and re-layouts  44.6 us (6%)
  starting transfers between devices  18.9 us (3%)
  between operations  15.4 us (2%)
    convert_element_type x2, other arithmetic, depthwise(): total = total + padded[:, i:i + rows, j:j + cols, :].astype(jnp.float32)...  84.8 us
    psum x1, waiting for transfers between devices, on_device(): lax.psum((g_expand, g_depth, g_reduce, g_excite, g_bexcite, g_project, g_...  79.5 us
    dot_general x1, matrix products, on_device(): jnp.dot(dflat, full_project.T, preferred_element_type=jnp.float32)  74.7 us
    psum x1, blocking collectives, on_device(): lax.psum((g_expand, g_depth, g_reduce, g_excite, g_bexcite, g_project, g_...  64.9 us
    convert_element_type x1, other arithmetic, on_device(): dpre = (dexp * swish_grad(pre)).astype(jnp.bfloat16)  61.6 us
    reduce_sum x2, other arithmetic, kernel_grad(): jnp.sum(ddepth.astype(jnp.float32) * padded[:, i:i + rows, j:j + cols, :]...  55.2 us
    psum x1, blocking collectives, on_device(): pooled = lax.psum(jnp.sum(act, axis=(1, 2)), 'space') / area  48.3 us
    unnamed x1, blocking collectives  30.9 us
  transfers between devices with their start and end apart: 5, of which 3 were waited for; matrix products, arithmetic and copies ran while one was open for 14% of the time, Pallas kernels for 0%

commit v1 on v0

v1 whole, which is shorter than its diff:
```python
import functools

import jax
import jax.numpy as jnp
from jax import lax
from jax.experimental import pallas as pl
from jax.experimental.pallas import tpu as pltpu
from jax.sharding import PartitionSpec as P

F32 = jnp.float32
BF16 = jnp.bfloat16
MESH = pl.DeviceIdType.MESH
HIGH = lax.Precision.HIGHEST

IMGS, ROWS, COLS, C, SE = 2, 12, 100, 176, 44
BLOCK, SUB = 13, 16
PIX = BLOCK * SUB
WIDE = BLOCK + 4
HROWS = ROWS + 4
PART, SLOT = 66, 72
CP = 16 * SLOT
TILES = CP // 128
AREA = 9600.0
NS, ND = 8, 16

VMEM = pl.BlockSpec(memory_space=pltpu.VMEM)
ANY = pl.BlockSpec(memory_space=pl.ANY)


def sigmoid(value):
    return 0.5 * jnp.tanh(0.5 * value) + 0.5


def swish(value):
    return value * sigmoid(value)


def swish_grad(value):
    sig = sigmoid(value)
    act = value * sig
    return sig + act - act * sig


def dot_nt(left, right, precision=None):
    return lax.dot_general(
        left, right, (((1,), (1,)), ((), ())), precision=precision, preferred_element_type=F32
    )


def dot_tn(left, right, precision=None):
    return lax.dot_general(
        left, right, (((0,), (0,)), ((), ())), precision=precision, preferred_element_type=F32
    )


def dot_nn(left, right, precision=None):
    return lax.dot_general(
        left, right, (((1,), (0,)), ((), ())), precision=precision, preferred_element_type=F32
    )


def greet(space_peers, dp_peers):
    me_s, me_d = lax.axis_index("space"), lax.axis_index("dp")
    barrier = pltpu.get_barrier_semaphore()
    for k in space_peers:
        pl.semaphore_signal(
            barrier, inc=1, device_id=(lax.rem(me_s + k, NS), me_d), device_id_type=MESH
        )
    for k in dp_peers:
        pl.semaphore_signal(
            barrier, inc=1, device_id=(me_s, lax.rem(me_d + k, ND)), device_id_type=MESH
        )
    pl.semaphore_wait(barrier, len(space_peers) + len(dp_peers))


def gather_kernel(
    pack, feats, full, top, bottom, send, recv, halo_send, halo_recv, mate_send, mate_recv, own
):
    me_s, me_d = lax.axis_index("space"), lax.axis_index("dp")
    core = lax.rem(me_s, 2)
    mate = me_s + 1 - 2 * core
    barrier = pltpu.get_barrier_semaphore()
    for k in (1, NS - 1):
        pl.semaphore_signal(
            barrier, inc=1, device_id=(lax.rem(me_s + k, NS), me_d), device_id_type=MESH
        )
    for k in range(1, ND):
        pl.semaphore_signal(
            barrier, inc=1, device_id=(me_s, lax.rem(me_d + k, ND)), device_id_type=MESH
        )
    pl.semaphore_wait(barrier, ND + 1)
    copies = []
    for k in range(1, ND):
        copy = pltpu.make_async_remote_copy(
            src_ref=pack.at[core],
            dst_ref=full.at[core, me_d],
            send_sem=send.at[k],
            recv_sem=recv.at[k],
            device_id=(me_s, lax.rem(me_d + k, ND)),
            device_id_type=MESH,
        )
        copy.start()
        copies.append(copy)
    down = pltpu.make_async_remote_copy(
        src_ref=feats.at[:, pl.ds(ROWS - 2, 2)],
        dst_ref=top,
        send_sem=halo_send.at[0],
        recv_sem=halo_recv.at[0],
        device_id=(lax.rem(me_s + 1, NS), me_d),
        device_id_type=MESH,
    )
    up = pltpu.make_async_remote_copy(
        src_ref=feats.at[:, pl.ds(0, 2)],
        dst_ref=bottom,
        send_sem=halo_send.at[1],
        recv_sem=halo_recv.at[1],
        device_id=(lax.rem(me_s + NS - 1, NS), me_d),
        device_id_type=MESH,
    )
    down.start()
    up.start()
    mine = pltpu.make_async_copy(pack.at[core], full.at[core, me_d], own)
    mine.start()
    mine.wait()
    for copy in copies:
        copy.wait()
    share = pltpu.make_async_remote_copy(
        src_ref=full.at[core],
        dst_ref=full.at[core],
        send_sem=mate_send,
        recv_sem=mate_recv,
        device_id=(mate, me_d),
        device_id_type=MESH,
    )
    share.start()
    down.wait()
    up.wait()
    share.wait()


def gather(pack, features):
    return pl.pallas_call(
        gather_kernel,
        out_shape=(
            jax.ShapeDtypeStruct((2, ND, 80, 256), BF16),
            jax.ShapeDtypeStruct((IMGS, 2, COLS, C), BF16),
            jax.ShapeDtypeStruct((IMGS, 2, COLS, C), BF16),
        ),
        in_specs=[ANY, ANY],
        out_specs=(ANY, ANY, ANY),
        scratch_shapes=[
            pltpu.SemaphoreType.DMA((ND,)),
            pltpu.SemaphoreType.DMA((ND,)),
            pltpu.SemaphoreType.DMA((2,)),
            pltpu.SemaphoreType.DMA((2,)),
            pltpu.SemaphoreType.DMA,
            pltpu.SemaphoreType.DMA,
            pltpu.SemaphoreType.DMA,
        ],
        compiler_params=pltpu.CompilerParams(collective_id=0, has_side_effects=True),
        name="gather_weights",
    )(pack, features)


def one_hot(img, transposed):
    shape = (COLS, PIX) if transposed else (PIX, COLS)
    place = lax.broadcasted_iota(jnp.int32, shape, 1 if transposed else 0)
    col = lax.broadcasted_iota(jnp.int32, shape, 0 if transposed else 1)
    wanted = (col % BLOCK) * SUB + img * 8 + col // BLOCK
    return jnp.where(place == wanted, 1.0, 0.0).astype(BF16)


def prep_kernel(
    full, top, bottom, feats, cot, fp, cp, fpt, cpt, we, wp, misc, flat
):
    me_s = lax.axis_index("space")
    for half, out in ((0, we), (1, wp)):
        for d in range(ND):
            flat[d * SLOT : (d + 1) * SLOT, :] = full[half, d, 0:SLOT, :].astype(F32)
        valid = lax.broadcasted_iota(jnp.int32, (CP, 256), 0) % SLOT < PART
        whole = jnp.where(valid, flat[...], 0.0)
        out[...] = whole[:, 0:C].astype(BF16)
        turned = whole[:, 128:256].T
        if half == 0:
            misc[0:32, :] = turned[48:80, :]
            misc[32:80, :] = turned[80:128, :]
        else:
            misc[80:128, :] = turned[48:96, :]
            misc[128:136, :] = turned[96:104, :]
    spread = (one_hot(0, False), one_hot(1, False))
    gather_t = (one_hot(0, True), one_hot(1, True))
    has_top = jnp.where(me_s > 0, 1.0, 0.0)
    has_bottom = jnp.where(me_s < NS - 1, 1.0, 0.0)
    for r in range(2):
        value = dot_nn(spread[0], top[0, r]) + dot_nn(spread[1], top[1, r])
        fp[r] = (value * has_top).astype(BF16)
        value = dot_nn(spread[0], bottom[0, r]) + dot_nn(spread[1], bottom[1, r])
        fp[ROWS + 2 + r] = (value * has_bottom).astype(BF16)

    def row(r, carry):
        for src, dst, shift, dst_t in ((feats, fp, 2, fpt), (cot, cp, 0, cpt)):
            a, b = src[0, r], src[1, r]
            dst[r + shift] = (dot_nn(spread[0], a) + dot_nn(spread[1], b)).astype(BF16)
            dst_t[r] = (dot_tn(a, gather_t[0]) + dot_tn(b, gather_t[1])).astype(BF16)
        return carry

    lax.fori_loop(0, ROWS, row, 0)


def prep(full, top, bottom, features, cotangent):
    return pl.pallas_call(
        prep_kernel,
        out_shape=(
            jax.ShapeDtypeStruct((HROWS, PIX, C), BF16),
            jax.ShapeDtypeStruct((ROWS, PIX, C), BF16),
            jax.ShapeDtypeStruct((ROWS, C, PIX), BF16),
            jax.ShapeDtypeStruct((ROWS, C, PIX), BF16),
            jax.ShapeDtypeStruct((CP, C), BF16),
            jax.ShapeDtypeStruct((CP, C), BF16),
            jax.ShapeDtypeStruct((136, CP), F32),
        ),
        in_specs=[VMEM] * 5,
        out_specs=(VMEM,) * 7,
        scratch_shapes=[pltpu.VMEM((CP, 256), F32)],
        compiler_params=pltpu.CompilerParams(vmem_limit_bytes=56 * 2**20),
        name="prep",
    )(full, top, bottom, features, cotangent)


def spread_taps(taps, wide_taps):
    for k in range(25):
        wide_taps[k] = jnp.broadcast_to(taps[k : k + 1, :], (8, 128))


def edge_columns(value):
    split = value.reshape(BLOCK, 2, 8, 128)
    block = lax.broadcasted_iota(jnp.int32, (2, 2, 8, 128), 2)
    left = jnp.where(block > 0, pltpu.roll(split[BLOCK - 2 :], 1, 2), 0.0)
    right = jnp.where(block < 7, pltpu.roll(split[:2], 7, 2), 0.0)
    return left.reshape(2, SUB, 128), right.reshape(2, SUB, 128)


def store_row(ref, r, value):
    left, right = edge_columns(value)
    ref[r, 0:2] = left
    ref[r, 2 : 2 + BLOCK] = value
    ref[r, 2 + BLOCK :] = right


def conv_row(ref, r, h, wide_taps, flip):
    total = jnp.zeros((BLOCK, 8, 128), F32)
    for i in range(5):
        source = ref[r + i, :, 8 * h : 8 * h + 8, :]
        for j in range(5):
            k = (4 - i) * 5 + 4 - j if flip else i * 5 + j
            total = total + source[j : j + BLOCK] * wide_taps[k][None]
    return total


def pad_mask():
    block = lax.broadcasted_iota(jnp.int32, (4, 8, 128), 1)
    return jnp.where(block < 7, 1.0, 0.0)


def first_kernel(fp, cp, we, wp, misc, ex, depth, sums, wide_taps):
    spread_taps(misc, wide_taps)
    keep = pad_mask()

    def expand(r, carry):
        pre = dot_nt(fp[r], we[...])
        store_row(ex.at[0], r, swish(pre).astype(BF16).astype(F32).reshape(BLOCK, SUB, 128))
        return carry

    lax.fori_loop(0, HROWS, expand, 0)

    def conv(r, carry):
        pools, grads = list(carry[:2]), list(carry[2:])
        dgated = dot_nt(cp[r], wp[...]).reshape(BLOCK, SUB, 128)
        for h in range(2):
            total = conv_row(ex.at[0], r, h, wide_taps, False)
            depth[0, r, :, 8 * h : 8 * h + 8, :] = total
            act = swish(total)
            grads[h] = grads[h] + jnp.sum(act * dgated[:, 8 * h : 8 * h + 8, :], axis=0)
            pools[h] = pools[h] + jnp.sum(act[:9], axis=0) + jnp.sum(act[9:] * keep, axis=0)
        return (*pools, *grads)

    zero = jnp.zeros((8, 128), F32)
    parts = lax.fori_loop(0, ROWS, conv, (zero,) * 4)
    for k in range(4):
        sums[0, k : k + 1, :] = jnp.sum(parts[k], axis=0, keepdims=True)
    sums[0, 4:8, :] = jnp.zeros((4, 128), F32)


def tile_spec(*shape):
    zeros = (0,) * len(shape)
    return pl.BlockSpec((1, *shape), lambda t: (t, *zeros))


def whole_spec(*shape):
    zeros = (0,) * len(shape)
    return pl.BlockSpec(shape, lambda t: zeros)


def first(fp, cp, we, wp, misc):
    return pl.pallas_call(
        first_kernel,
        grid=(TILES,),
        out_shape=(
            jax.ShapeDtypeStruct((TILES, HROWS, WIDE, SUB, 128), F32),
            jax.ShapeDtypeStruct((TILES, ROWS, BLOCK, SUB, 128), F32),
            jax.ShapeDtypeStruct((TILES, 8, 128), F32),
        ),
        in_specs=[
            whole_spec(HROWS, PIX, C),
            whole_spec(ROWS, PIX, C),
            pl.BlockSpec((128, C), lambda t: (t, 0)),
            pl.BlockSpec((128, C), lambda t: (t, 0)),
            pl.BlockSpec((32, 128), lambda t: (0, t)),
        ],
        out_specs=(
            tile_spec(HROWS, WIDE, SUB, 128),
            tile_spec(ROWS, BLOCK, SUB, 128),
            tile_spec(8, 128),
        ),
        scratch_shapes=[pltpu.VMEM((25, 8, 128), F32)],
        compiler_params=pltpu.CompilerParams(vmem_limit_bytes=56 * 2**20),
        name="phase_a",
    )(fp, cp, we, wp, misc)


def mid_kernel(
    sums, misc, breduce, gates, greduce, gexcite, gbias, landed, msgs, got, lanes, vecs,
    send, recv, msend, mrecv,
):
    me_s, me_d = lax.axis_index("space"), lax.axis_index("dp")
    greet(range(1, NS), range(1, ND))
    copies = []
    for k in range(1, NS):
        copy = pltpu.make_async_remote_copy(
            src_ref=sums,
            dst_ref=landed.at[k],
            send_sem=send.at[k],
            recv_sem=recv.at[k],
            device_id=(lax.rem(me_s + k, NS), me_d),
            device_id_type=MESH,
        )
        copy.start()
        copies.append(copy)
    landed[0] = sums[...]
    for copy in copies:
        copy.wait()
    total = landed[lax.rem(me_s, NS)]
    for s in range(1, NS):
        total = total + landed[lax.rem(me_s + NS - s, NS)]
    for t in range(TILES):
        lanes[0:8, 128 * t : 128 * (t + 1)] = total[t]
    lanes[:, CP:] = jnp.zeros((8, 128), F32)
    allsum = lanes[:, 0:CP]
    wr = misc[32 : 32 + SE, :]
    wx = misc[80 : 80 + SE, :]
    bexcite = misc[128:129, :]
    pooled = allsum[0:2] / AREA
    dgate = allsum[2:4]
    squeeze_pre = dot_nt(pooled, wr, HIGH) + breduce[...].astype(F32)
    squeeze = swish(squeeze_pre)
    gate = sigmoid(dot_nn(squeeze, wx, HIGH) + bexcite)
    dlogit = dgate * gate * (1.0 - gate)
    dsq = dot_nt(dlogit, wx, HIGH) * swish_grad(squeeze_pre)
    dpooled = dot_nn(dsq, wr, HIGH)
    gates[0:2, :] = gate
    gates[2:4, :] = dpooled / AREA
    gates[4:8, :] = jnp.zeros((4, CP), F32)
    lanes[0:2, 0:CP] = pooled
    lanes[2:4, 0:CP] = dlogit
    vecs[...] = jnp.zeros((8, 128), F32)
    vecs[4:6, 0:SE] = squeeze
    vecs[6:8, 0:SE] = dsq
    for d in range(ND):
        msgs[d, 0:4, :] = lanes[0:4, SLOT * d : SLOT * d + 128]
        msgs[d, 4:8, :] = vecs[4:8, :]
    copies = []
    for k in range(1, ND):
        target = lax.rem(me_d + k, ND)
        copy = pltpu.make_async_remote_copy(
            src_ref=msgs.at[target],
            dst_ref=got.at[k],
            send_sem=msend.at[k],
            recv_sem=mrecv.at[k],
            device_id=(me_s, target),
            device_id_type=MESH,
        )
        copy.start()
        copies.append(copy)
    got[0] = msgs[me_d]
    for copy in copies:
        copy.wait()
    rows = [got[lax.rem(me_d + ND - d, ND)] for d in range(ND)]
    pool_all = jnp.concatenate([row[0:2] for row in rows], axis=0)
    dlog_all = jnp.concatenate([row[2:4] for row in rows], axis=0)
    sq_all = jnp.concatenate([row[4:6] for row in rows], axis=0)
    dsq_all = jnp.concatenate([row[6:8] for row in rows], axis=0)
    greduce[...] = dot_tn(pool_all, dsq_all, HIGH)
    gexcite[...] = dot_tn(sq_all, dlog_all, HIGH)
    gbias[0:1, :] = jnp.sum(dlog_all, axis=0, keepdims=True)
    gbias[1:2, :] = jnp.sum(dsq_all, axis=0, keepdims=True)
    gbias[2:8, :] = jnp.zeros((6, 128), F32)


def mid(sums, misc, breduce):
    return pl.pallas_call(
        mid_kernel,
        out_shape=(
            jax.ShapeDtypeStruct((8, CP), F32),
            jax.ShapeDtypeStruct((128, 128), F32),
            jax.ShapeDtypeStruct((128, 128), F32),
            jax.ShapeDtypeStruct((8, 128), F32),
        ),
        in_specs=[VMEM] * 3,
        out_specs=(VMEM,) * 4,
        scratch_shapes=[
            pltpu.VMEM((NS, TILES, 8, 128), F32),
            pltpu.VMEM((ND, 8, 128), F32),
            pltpu.VMEM((ND, 8, 128), F32),
            pltpu.VMEM((8, CP + 128), F32),
            pltpu.VMEM((8, 128), F32),
            pltpu.SemaphoreType.DMA((NS,)),
            pltpu.SemaphoreType.DMA((NS,)),
            pltpu.SemaphoreType.DMA((ND,)),
            pltpu.SemaphoreType.DMA((ND,)),
        ],
        compiler_params=pltpu.CompilerParams(
            collective_id=1, has_side_effects=True, vmem_limit_bytes=56 * 2**20
        ),
        name="squeeze_excite",
    )(sums, misc, breduce)


def gate_row(depth, dgated, gates, h, keep):
    gate = gates[h : h + 1, :][None]
    pull = gates[2 + h : 3 + h, :][None]
    sig = sigmoid(depth)
    act = depth * sig
    gated = act * gate
    ddepth = (dgated * gate + pull) * (sig + act - act * sig)
    ddepth = jnp.concatenate([ddepth[:9], ddepth[9:] * keep], axis=0)
    return gated, ddepth


def edge_kernel(depth, cp, wp, gates, edge):
    keep = pad_mask()
    for n, r in enumerate((0, 1, ROWS - 2, ROWS - 1)):
        dgated = dot_nt(cp[r], wp[...]).reshape(BLOCK, SUB, 128)
        both = []
        for h in range(2):
            rows = slice(8 * h, 8 * h + 8)
            _, ddepth = gate_row(depth[0, r, :, rows, :], dgated[:, rows, :], gates, h, keep)
            both.append(ddepth)
        edge[0, n] = jnp.concatenate(both, axis=1).astype(BF16)


def edges(depth, cp, wp, gates):
    return pl.pallas_call(
        edge_kernel,
        grid=(TILES,),
        out_shape=jax.ShapeDtypeStruct((TILES, 4, BLOCK, SUB, 128), BF16),
        in_specs=[
            tile_spec(ROWS, BLOCK, SUB, 128),
            whole_spec(ROWS, PIX, C),
            pl.BlockSpec((128, C), lambda t: (t, 0)),
            pl.BlockSpec((8, 128), lambda t: (0, t)),
        ],
        out_specs=tile_spec(4, BLOCK, SUB, 128),
        compiler_params=pltpu.CompilerParams(vmem_limit_bytes=56 * 2**20),
        name="edge_rows",
    )(depth, cp, wp, gates)


def unpermute(value, out, r, back):
    for img in range(2):
        out[img, r] = dot_nn(back[img], value).astype(BF16)


def second_kernel(
    ex, depth, fp, cp, cpt, wp, gates, dd, out, gproj, gdepth, gated_rows, total, acc
):
    keep = pad_mask()
    t = pl.program_id(0)

    def pointwise(r, carry):
        dgated = dot_nt(cp[r], wp[...]).reshape(BLOCK, SUB, 128)
        both, gates_both = [], []
        for h in range(2):
            rows = slice(8 * h, 8 * h + 8)
            gated, ddepth = gate_row(depth[0, r, :, rows, :], dgated[:, rows, :], gates, h, keep)
            both.append(ddepth)
            gates_both.append(gated)
        value = jnp.concatenate(both, axis=1).astype(BF16).astype(F32)
        store_row(dd.at[0], r, value)
        gated_rows[r] = jnp.concatenate(gates_both, axis=1).reshape(PIX, 128).astype(BF16)
        return carry

    lax.fori_loop(0, ROWS, pointwise, 0)

    @pl.when(t == 0)
    def _():
        total[...] = jnp.zeros_like(total)

    def matmuls(r, grad):
        total[r] = total[r] + dot_nn(gated_rows[r], wp[...])
        return grad + dot_nn(cpt[r], gated_rows[r])

    gproj[0] = lax.fori_loop(0, ROWS, matmuls, jnp.zeros((C, 128), F32))

    acc[...] = jnp.zeros_like(acc)

    def taps(r, carry):
        for h in range(2):
            rows = slice(8 * h, 8 * h + 8)
            mine = dd[0, r, 2 : 2 + BLOCK, rows, :]
            for i in range(5):
                source = ex[0, r + i, :, rows, :]
                for j in range(5):
                    k = 5 * i + j
                    acc[k] = acc[k] + jnp.sum(mine * source[j : j + BLOCK], axis=0)
        return carry

    lax.fori_loop(0, ROWS, taps, 0)
    for k in range(25):
        gdepth[0, k : k + 1, :] = jnp.sum(acc[k], axis=0, keepdims=True)
    gdepth[0, 25:32, :] = jnp.zeros((7, 128), F32)

    @pl.when(t == TILES - 1)
    def _():
        back = (one_hot(0, True), one_hot(1, True))

        def finish(r, carry):
            value = (total[r] + fp[r + 2].astype(F32)).astype(BF16)
            unpermute(value, out, r, back)
            return carry

        lax.fori_loop(0, ROWS, finish, 0)


def second(ex, depth, fp, cp, cpt, wp, gates):
    return pl.pallas_call(
        second_kernel,
        grid=(TILES,),
        out_shape=(
            jax.ShapeDtypeStruct((TILES, ROWS, WIDE, SUB, 128), F32),
            jax.ShapeDtypeStruct((IMGS, ROWS, COLS, C), BF16),
            jax.ShapeDtypeStruct((TILES, C, 128), F32),
            jax.ShapeDtypeStruct((TILES, 32, 128), F32),
        ),
        in_specs=[
            tile_spec(HROWS, WIDE, SUB, 128),
            tile_spec(ROWS, BLOCK, SUB, 128),
            whole_spec(HROWS, PIX, C),
            whole_spec(ROWS, PIX, C),
            whole_spec(ROWS, C, PIX),
            pl.BlockSpec((128, C), lambda t: (t, 0)),
            pl.BlockSpec((8, 128), lambda t: (0, t)),
        ],
        out_specs=(
            tile_spec(ROWS, WIDE, SUB, 128),
            whole_spec(IMGS, ROWS, COLS, C),
            tile_spec(C, 128),
            tile_spec(32, 128),
        ),
        scratch_shapes=[
            pltpu.VMEM((ROWS, PIX, 128), BF16),
            pltpu.VMEM((ROWS, PIX, C), F32),
            pltpu.VMEM((25, 8, 128), F32),
        ],
        compiler_params=pltpu.CompilerParams(vmem_limit_bytes=56 * 2**20),
        cost_estimate=pl.CostEstimate(
            flops=4 * 10**9, bytes_accessed=50 * 10**6, transcendentals=3 * 10**6
        ),
        name="phase_b",
    )(ex, depth, fp, cp, cpt, wp, gates)


def third_kernel(dd, above, below, fp, cp, fpt, we, misc, out, gexp, wide_taps, rows_in, dpre, total):
    t = pl.program_id(0)
    spread_taps(misc, wide_taps)
    for n in range(2):
        store_row(rows_in, n, above[0, n].astype(F32))
        store_row(rows_in, ROWS + 2 + n, below[0, n].astype(F32))

    def move(r, carry):
        rows_in[r + 2] = dd[0, r]
        return carry

    lax.fori_loop(0, ROWS, move, 0)

    @pl.when(t == 0)
    def _():
        total[...] = jnp.zeros_like(total)

    def conv(r, carry):
        slope = swish_grad(dot_nt(fp[r + 2], we[...])).reshape(BLOCK, SUB, 128)
        both = []
        for h in range(2):
            both.append(conv_row(rows_in, r, h, wide_taps, True) * slope[:, 8 * h : 8 * h + 8, :])
        dpre[r] = jnp.concatenate(both, axis=1).reshape(PIX, 128).astype(BF16)
        return carry

    lax.fori_loop(0, ROWS, conv, 0)

    def matmuls(r, grad):
        total[r] = total[r] + dot_nn(dpre[r], we[...])
        return grad + dot_nn(fpt[r], dpre[r])

    gexp[0] = lax.fori_loop(0, ROWS, matmuls, jnp.zeros((C, 128), F32))

    @pl.when(t == TILES - 1)
    def _():
        back = (one_hot(0, True), one_hot(1, True))

        def finish(r, carry):
            value = (total[r] + cp[r].astype(F32)).astype(BF16)
            unpermute(value, out, r, back)
            return carry

        lax.fori_loop(0, ROWS, finish, 0)


def third(dd, above, below, fp, cp, fpt, we, misc):
    return pl.pallas_call(
        third_kernel,
        grid=(TILES,),
        out_shape=(
            jax.ShapeDtypeStruct((IMGS, ROWS, COLS, C), BF16),
            jax.ShapeDtypeStruct((TILES, C, 128), F32),
        ),
        in_specs=[
            tile_spec(ROWS, WIDE, SUB, 128),
            tile_spec(2, BLOCK, SUB, 128),
            tile_spec(2, BLOCK, SUB, 128),
            whole_spec(HROWS, PIX, C),
            whole_spec(ROWS, PIX, C),
            whole_spec(ROWS, C, PIX),
            pl.BlockSpec((128, C), lambda t: (t, 0)),
            pl.BlockSpec((32, 128), lambda t: (0, t)),
        ],
        out_specs=(whole_spec(IMGS, ROWS, COLS, C), tile_spec(C, 128)),
        scratch_shapes=[
            pltpu.VMEM((25, 8, 128), F32),
            pltpu.VMEM((HROWS, WIDE, SUB, 128), F32),
            pltpu.VMEM((ROWS, PIX, 128), BF16),
            pltpu.VMEM((ROWS, PIX, C), F32),
        ],
        compiler_params=pltpu.CompilerParams(vmem_limit_bytes=56 * 2**20),
        name="phase_c",
    )(dd, above, below, fp, cp, fpt, we, misc)


CHUNK = 48


def reduce_kernel(
    gexp, gproj, gdepth, out, stack, packed, landed, part, pieces, got, final,
    send, recv, dsend, drecv, fsend, frecv,
):
    me_s, me_d = lax.axis_index("space"), lax.axis_index("dp")
    greet(range(1, NS), range(1, ND))
    for t in range(TILES):
        lanes = slice(128 * t, 128 * (t + 1))
        stack[0:C, lanes] = gexp[t]
        stack[C : 2 * C, lanes] = gproj[t]
        stack[2 * C :, lanes] = gdepth[t]
    packed[...] = stack[...].reshape(NS, CHUNK, CP).astype(BF16)
    copies = []
    for k in range(1, NS):
        target = lax.rem(me_s + k, NS)
        copy = pltpu.make_async_remote_copy(
            src_ref=packed.at[target],
            dst_ref=landed.at[k],
            send_sem=send.at[k],
            recv_sem=recv.at[k],
            device_id=(target, me_d),
            device_id_type=MESH,
        )
        copy.start()
        copies.append(copy)
    start = pl.multiple_of(me_s * CHUNK, CHUNK)
    part[:, 0:CP] = stack[pl.ds(start, CHUNK), :]
    part[:, CP:] = jnp.zeros((CHUNK, 128), F32)
    for k, copy in enumerate(copies):
        copy.wait()
        part[:, 0:CP] = part[:, 0:CP] + landed[k + 1].astype(F32)
    for d in range(ND):
        pieces[d] = part[:, SLOT * d : SLOT * d + 128].astype(BF16)
    copies = []
    for k in range(1, ND):
        target = lax.rem(me_d + k, ND)
        copy = pltpu.make_async_remote_copy(
            src_ref=pieces.at[target],
            dst_ref=got.at[k],
            send_sem=dsend.at[k],
            recv_sem=drecv.at[k],
            device_id=(me_s, target),
            device_id_type=MESH,
        )
        copy.start()
        copies.append(copy)
    total = pieces[me_d].astype(F32)
    for k, copy in enumerate(copies):
        copy.wait()
        total = total + got[k + 1].astype(F32)
    final[me_s] = total
    copies = []
    for k in range(1, NS):
        copy = pltpu.make_async_remote_copy(
            src_ref=final.at[me_s],
            dst_ref=final.at[me_s],
            send_sem=fsend.at[k],
            recv_sem=frecv.at[k],
            device_id=(lax.rem(me_s + k, NS), me_d),
            device_id_type=MESH,
        )
        copy.start()
        copies.append(copy)
    for copy in copies:
        copy.wait()
    out[...] = final[...]


def reduce_grads(gexp, gproj, gdepth):
    return pl.pallas_call(
        reduce_kernel,
        out_shape=jax.ShapeDtypeStruct((NS, CHUNK, 128), F32),
        in_specs=[VMEM] * 3,
        out_specs=VMEM,
        scratch_shapes=[
            pltpu.VMEM((NS * CHUNK, CP), F32),
            pltpu.VMEM((NS, CHUNK, CP), BF16),
            pltpu.VMEM((NS, CHUNK, CP), BF16),
            pltpu.VMEM((CHUNK, CP + 128), F32),
            pltpu.VMEM((ND, CHUNK, 128), BF16),
            pltpu.VMEM((ND, CHUNK, 128), BF16),
            pltpu.VMEM((NS, CHUNK, 128), F32),
            pltpu.SemaphoreType.DMA((NS,)),
            pltpu.SemaphoreType.DMA((NS,)),
            pltpu.SemaphoreType.DMA((ND,)),
            pltpu.SemaphoreType.DMA((ND,)),
            pltpu.SemaphoreType.DMA((NS,)),
            pltpu.SemaphoreType.DMA((NS,)),
        ],
        compiler_params=pltpu.CompilerParams(
            collective_id=2, has_side_effects=True, vmem_limit_bytes=56 * 2**20
        ),
        name="reduce_grads",
    )(gexp, gproj, gdepth)


def on_device(
    features, w_expand, w_depth, w_reduce, b_reduce, w_excite, b_excite, w_project, cotangent
):
    def blank(count):
        return jnp.zeros((PART, count), BF16)

    first_half = jnp.concatenate(
        [w_expand.T, w_depth.reshape(25, PART).T, blank(7), w_reduce, blank(4)], axis=1
    )
    second_half = jnp.concatenate(
        [w_project, w_excite.T, blank(4), b_excite[:, None], blank(31)], axis=1
    )
    pack = jnp.pad(jnp.stack([first_half, second_half]), ((0, 0), (0, 80 - PART), (0, 0)))
    full, top, bottom = gather(pack, features)
    fp, cp, fpt, cpt, we, wp, misc = prep(full, top, bottom, features, cotangent)
    ex, depth, sums = first(fp, cp, we, wp, misc)
    gates, greduce, gexcite, gbias = mid(sums, misc, b_reduce[None, :])
    edge = edges(depth, cp, wp, gates)
    above = lax.ppermute(edge[:, 2:4], "space", [(i, i + 1) for i in range(NS - 1)])
    below = lax.ppermute(edge[:, 0:2], "space", [(i + 1, i) for i in range(NS - 1)])
    dd, output, gproj, gdepth = second(ex, depth, fp, cp, cpt, wp, gates)
    grad_features, gexp = third(dd, above, below, fp, cp, fpt, we, misc)
    grads = reduce_grads(gexp, gproj, gdepth).reshape(NS * CHUNK, 128)
    return (
        output,
        grad_features,
        grads[0:C, 0:PART],
        grads[2 * C : 2 * C + 25, 0:PART].reshape(5, 5, PART),
        greduce[0:PART, 0:SE],
        gexcite[0:SE, 0:PART],
        gbias[0, 0:PART],
        grads[C : 2 * C, 0:PART].T,
        gbias[1, 0:SE],
    )


def solution(mesh):
    return jax.shard_map(
        on_device,
        mesh=mesh,
        in_specs=(
            P("dp", "space", None, None),
            P(None, "dp"),
            P(None, None, "dp"),
            P("dp", None),
            P(),
            P(None, "dp"),
            P("dp"),
            P("dp", None),
            P("dp", "space", None, None),
        ),
        out_specs=(
            P("dp", "space", None, None),
            P("dp", "space", None, None),
            P(None, "dp"),
            P(None, None, "dp"),
            P("dp", None),
            P(None, "dp"),
            P("dp"),
            P("dp", None),
            P(),
        ),
        check_vma=False,
    )
```

time: 739 us -> 327 us (0.44)
  Pallas kernels: 0 us -> 296 us
  blocking collectives: 238 us -> 0 us
  other arithmetic: 221 us -> 0.65 us
  matrix products: 113 us -> 0 us
  waiting for transfers between devices: 83.6 us -> 0.01 us
  local copies, waits for them, and re-layouts: 44.6 us -> 24 us
  between operations: 15.4 us -> 0.78 us
  starting transfers between devices: 18.9 us -> 5.55 us
    pallas_call x0 -> x8, Pallas kernels: none -> 296 us  [the longest x1 70.9 us: second(): pl.pallas_call(second_kernel, grid=(TILES,), out_shape=(jax.ShapeDtypeStr...]
    convert_element_type x5 -> x0, other arithmetic: 147 us -> none  [the longest x2 84.8 us: depthwise(): total = total + padded[:, i:i + rows, j:j + cols, :].astype(jnp.float32)...]
    psum x2 -> x0, blocking collectives: 113 us -> none  [the longest x1 64.9 us: on_device(): lax.psum((g_expand, g_depth, g_reduce, g_excite, g_bexcite, g_project, g_...]
    dot_general x12 -> x0, matrix products: 113 us -> none  [the longest x1 74.7 us: on_device(): jnp.dot(dflat, full_project.T, preferred_element_type=jnp.float32)]
    all_gather x5 -> x0, blocking collectives: 93.9 us -> none  [the longest x1 22.8 us: on_device(): lax.all_gather(w_depth, 'dp', axis=2, tiled=True)]
    psum x1 -> x0, waiting for transfers between devices: 79.5 us -> none  [on_device(): lax.psum((g_expand, g_depth, g_reduce, g_excite, g_bexcite, g_project, g_...]
    reduce_sum x2 -> x0, other arithmetic: 55.2 us -> none  [kernel_grad(): jnp.sum(ddepth.astype(jnp.float32) * padded[:, i:i + rows, j:j + cols, :]...]
    unnamed x1 -> x0, blocking collectives: 30.9 us -> none
  transfers between devices with their start and end apart: 5 -> 2, of which waited for: 3 -> 0; matrix products, arithmetic and copies ran while one was open for 14% -> 2% of each run, Pallas kernels for 0% -> 22%
where the time goes in v1:
time: 327 us; the launch traced here: 326 us
  Pallas kernels  296 us (91%)
  local copies, waits for them, and re-layouts  24 us (7%)
  starting transfers between devices  5.55 us (2%)
    pallas_call x1, Pallas kernels, second(): pl.pallas_call(second_kernel, grid=(TILES,), out_shape=(jax.ShapeDtypeStr...  70.9 us
    pallas_call x1, Pallas kernels, first(): pl.pallas_call(first_kernel, grid=(TILES,), out_shape=(jax.ShapeDtypeStru...  69.5 us
    pallas_call x1, Pallas kernels, third(): pl.pallas_call(third_kernel, grid=(TILES,), out_shape=(jax.ShapeDtypeStru...  69.5 us
    pallas_call x1, Pallas kernels, reduce_grads(): pl.pallas_call(reduce_kernel, out_shape=jax.ShapeDtypeStruct((NS, CHUNK,...  26.6 us
    pallas_call x1, Pallas kernels, mid(): pl.pallas_call(mid_kernel, out_shape=(jax.ShapeDtypeStruct((8, CP), F32),...  20.2 us
    pallas_call x1, Pallas kernels, gather(): pl.pallas_call(gather_kernel, out_shape=(jax.ShapeDtypeStruct((2, ND, 80,...  18.7 us
    unnamed x23, local copies, waits for them, and re-layouts  13.3 us
    pallas_call x1, Pallas kernels, prep(): pl.pallas_call(prep_kernel, out_shape=(jax.ShapeDtypeStruct((HROWS, PIX,...  10.2 us
  transfers between devices with their start and end apart: 2, of which 0 were waited for; matrix products, arithmetic and copies ran while one was open for 2% of the time, Pallas kernels for 22%

profile of v1, /device:TPU:1, one launch (start us, length us, event | category | flops | bytes accessed | tf_op | source)
XLA Modules:
  0.0 326.5 jit_solution(484046537495449529)
XLA Ops:
  0.6 0.0 copy-start.1
  0.7 0.8 reshape.27
  1.5 0.1 copy.30
  1.6 0.8 copy.31
  2.4 0.8 copy.32
  3.2 0.8 copy.33
  4.0 2.6 copy.34.feats
  6.6 0.0 copy-done.1
  6.6 0.0 copy-start.4
  6.6 0.0 copy-start.5
  6.6 1.6 copy.36.cot
  8.2 0.0 copy-done.4
  8.2 0.1 concatenate.7
  8.3 0.0 copy-done.5
  8.4 0.1 concatenate.6
  8.5 0.6 fusion.2.pack
  9.1 18.7 %gather_weights.1 = (bf16[2,16,80,256]{3,2,1,0:T(8,128)(2,1)}, bf16[2,2,100,176]{3,2,1,0:T(8,128)(2,1)}, bf16[2,2,100,176]{3,2,1,0:T(8,128)(2,1)}) custom-call(bf16[2,80,256]{2,1,0:T(8,128)(2,1)} %fusion.2.pack, bf16[2,12,100,176]{3,2,1,0:T(8,128)(2,1)} %copy.34.feats), custom_call_target="tpu_custom_call" | custom-call | tf_op jit(solution)/shard_map/gather_weights/pallas_call | solution.py:142
  27.8 10.2 %prep.1 = (bf16[16,208,176]{2,1,0:T(8,128)(2,1)}, bf16[12,208,176]{2,1,0:T(8,128)(2,1)}, bf16[12,176,208]{2,1,0:T(8,128)(2,1)}, bf16[12,176,208]{2,1,0:T(8,128)(...) custom-call(bf16[2,16,80,256]{3,2,1,0:T(8,128)(2,1)} %get-tuple-element.32.full, ...), custom_call_target="tpu_custom_call" | custom-call | tf_op jit(solution)/shard_map/prep/pallas_call | solution.py:211
  38.0 69.5 %phase_a.1 = (f32[9,16,17,16,128]{4,3,2,1,0:T(8,128)}, f32[9,12,13,16,128]{4,3,2,1,0:T(8,128)}, f32[9,8,128]{2,1,0:T(8,128)}) custom-call(bf16[16,208,176]{2,1,0:T(8,128)(2,1)} %get-tuple-element.35.fp, bf16[12,208,176]{2,1,0:T(8,128)(2,1)} %get-tuple-element.36.cp, bf16[1152,176]{1,0:T(8,128)(2,1)} %get-tuple-element.37.we, ...), custom_call_target="tpu_custom_call" | custom-call | tf_op jit(solution)/shard_map/phase_a/pallas_call | solution.py:305
  107.5 20.2 %squeeze_excite.1 = (f32[8,1152]{1,0:T(8,128)}, f32[128,128]{1,0:T(8,128)}, f32[128,128]{1,0:T(8,128)}, f32[8,128]{1,0:T(8,128)}) custom-call(f32[9,8,128]{2,1,0:T(8,128)} %get-tuple-element.43.sums, f32[136,1152]{1,0:T(8,128)} %get-tuple-element.39.misc, bf16[1,44]{1,0:T(2,128)(2,1)} %bitcast.21), custom_call_target="tpu_custom_call" | custom-call | tf_op jit(solution)/shard_map/squeeze_excite/pallas_call | solution.py:410
  127.7 9.9 %edge_rows.1 = bf16[9,4,13,16,128]{4,3,2,1,0:T(8,128)(2,1)} custom-call(f32[9,12,13,16,128]{4,3,2,1,0:T(8,128)} %get-tuple-element.41.depth, bf16[12,208,176]{2,1,0:T(8,128)(2,1)} %get-tuple-element.36.cp, bf16[1152,176]{1,0:T(8,128)(2,1)} %get-tuple-element.38.wp, f32[8,1152]{1,0:T(8,128)} %get-tuple-element.44.gates), custom_call_target="tpu_custom_call" | custom-call | tf_op jit(solution)/shard_map/edge_rows/pallas_call | solution.py:462
  137.6 2.8 fusion.3
  140.4 2.9 collective-permute-start.1
  143.3 2.7 collective-permute-start
  146.0 70.9 %phase_b.1 = (f32[9,12,17,16,128]{4,3,2,1,0:T(8,128)}, bf16[2,12,100,176]{3,2,1,0:T(8,128)(2,1)}, f32[9,176,128]{2,1,0:T(8,128)}, f32[9,32,128]{2,1,0:T(8,128)}) custom-call(f32[9,16,17,16,128]{4,3,2,1,0:T(8,128)} %get-tuple-element.40.ex, f32[9,12,13,16,128]{4,3,2,1,0:T(8,128)} %get-tuple-element.41.depth, bf16[16,208,176]{2,1,0:T(8,128)(2,1)} %get-tuple-element.35.fp, ...), custom_call_target="tpu_custom_call" | custom-call | flops 4000000000 | bytes 50000000 | tf_op jit(solution)/shard_map/phase_b/pallas_call | solution.py:545
  216.9 0.0 copy-start.6
  216.9 2.5 copy.39
  219.4 0.0 copy-done.6
  219.4 0.7 copy.41
  220.1 1.3 slice.32
  221.5 1.2 slice_bitcast_fusion
  222.7 1.2 slice_bitcast_fusion.1
  223.9 0.0 collective-permute-done.1.below
  223.9 0.0 copy-start.2
  223.9 0.0 collective-permute-done.above
  223.9 0.0 copy-start.3
  223.9 0.9 copy-done.2
  224.8 0.3 copy-done.3
  225.1 69.5 %phase_c.1 = (bf16[2,12,100,176]{3,2,1,0:T(8,128)(2,1)}, f32[9,176,128]{2,1,0:T(8,128)}) custom-call(f32[9,12,17,16,128]{4,3,2,1,0:T(8,128)} %get-tuple-element.46.dd, bf16[9,2,13,16,128]{4,3,2,1,0:T(8,128)(2,1)} %copy-done.3, bf16[9,2,13,16,128]{4,3,2,1,0:T(8,128)(2,1)} %copy-done.2, bf16[16,208,176]{2,1,0:T(8,128)(2,1)} %get-tuple-element.35.fp, ...), custom_call_target="tpu_custom_call" | custom-call | tf_op jit(solution)/shard_map/phase_c/pallas_call | solution.py:628
  294.6 0.0 copy-start
  294.6 26.6 %reduce_grads.1 = f32[8,48,128]{2,1,0:T(8,128)} custom-call(f32[9,176,128]{2,1,0:T(8,128)} %get-tuple-element.49.gexp, f32[9,176,128]{2,1,0:T(8,128)} %get-tuple-element.50.gproj, f32[9,32,128]{2,1,0:T(8,128)} %get-tuple-element.51.gdepth), custom_call_target="tpu_custom_call" | custom-call | tf_op jit(solution)/shard_map/reduce_grads/pallas_call | solution.py:729
  321.2 0.7 slice.39
  321.9 0.9 fusion.4
  322.9 0.0 copy-done
  322.9 1.5 copy.40
  324.4 0.7 copy.43
  325.1 0.6 reshape.29
  325.7 0.7 copy.42
  (4 shorter events, 0.0 us)
Async XLA Ops:
  0.6 5.9 %copy-start.1 = (bf16[2,12,100,176]{2,3,1,0:T(8,128)(2,1)S(1)}, bf16[2,12,100,176]{2,3,1,0:T(8,128)(2,1)}, u32[]{:S(2)}) copy-start(bf16[2,12,100,176]{2,3,1,0:T(8,128)(2,1)} %param.17) | copy-start | bytes 2534404
  6.6 1.6 copy-start.4
  6.6 1.8 copy-start.5
  140.4 83.4 %collective-permute-start.1 = (bf16[9,2,13,16,128]{4,3,2,1,0:T(8,128)(2,1)}, bf16[9,2,13,16,128]{4,3,2,1,0:T(8,128)(2,1)S(1)}, u32[]{:S(2)}, u32[]{:S(2)}) collective-permute-start(bf16[9,2,13,16,128]{4,3,2,1,0:T(8,128)(2,1)} %get-tuple-element.73), channel_id=1, source_target_pairs={{16,0},{32,16},{48,32},{64,48},{80,64},{96,80},{112,96},{17,1},{33... | collective-permute-start | bytes 2875400 | tf_op jit(solution)/shard_map/ppermute | solution.py:775
  143.3 80.5 %collective-permute-start = (bf16[9,2,13,16,128]{4,3,2,1,0:T(8,128)(2,1)S(1)}, bf16[9,2,13,16,128]{4,3,2,1,0:T(8,128)(2,1)S(1)}, u32[]{:S(2)}, u32[]{:S(2)}) collective-permute-start(bf16[9,2,13,16,128]{4,3,2,1,0:T(8,128)(2,1)S(1)} %get-tuple-element.74), channel_id=1, source_target_pairs={{0,16},{16,32},{32,48},{48,64},{64,80},{80,96},{96,112},{1,17},{17... | collective-permute-start | bytes 2875400 | tf_op jit(solution)/shard_map/ppermute | solution.py:774
  216.9 2.5 copy-start.6
  223.9 0.9 copy-start.2
  223.9 1.3 copy-start.3
  294.6 28.3 %copy-start = (bf16[2,12,100,176]{3,2,1,0:T(8,128)(2,1)S(1)}, bf16[2,12,100,176]{3,2,1,0:T(8,128)(2,1)}, u32[]{:S(2)}) copy-start(bf16[2,12,100,176]{3,2,1,0:T(8,128)(2,1)} %get-tuple-element.65) | copy-start | bytes 2534404

commit v2 on v1

--- a/solution.py
+++ b/solution.py
@@ -262,26 +262,37 @@
     return jnp.where(block < 7, 1.0, 0.0)
 
 
-def first_kernel(fp, cp, we, wp, misc, ex, depth, sums, wide_taps):
+def first_kernel(fp, cp, we, wp, misc, ex, depth, sums, wide_taps, pres, dgs):
     spread_taps(misc, wide_taps)
     keep = pad_mask()
 
-    def expand(r, carry):
-        pre = dot_nt(fp[r], we[...])
-        store_row(ex.at[0], r, swish(pre).astype(BF16).astype(F32).reshape(BLOCK, SUB, 128))
+    def expand(slot, r):
+        store_row(ex.at[0], r, swish(pres[slot]).astype(BF16).astype(F32).reshape(BLOCK, SUB, 128))
+
+    head = fp[0:6].reshape(6 * PIX, C)
+    pres[...] = dot_nt(head, we[...]).reshape(6, PIX, 128)
+    dgs[0] = dot_nt(cp[0], wp[...])
+
+    def start(r, carry):
+        expand(r, r)
         return carry
 
-    lax.fori_loop(0, HROWS, expand, 0)
+    lax.fori_loop(0, 5, start, 0)
+    pres[1] = pres[5]
 
     def conv(r, carry):
         pools, grads = list(carry[:2]), list(carry[2:])
-        dgated = dot_nt(cp[r], wp[...]).reshape(BLOCK, SUB, 128)
+        later = lax.rem(r + 1, 2)
         for h in range(2):
             total = conv_row(ex.at[0], r, h, wide_taps, False)
             depth[0, r, :, 8 * h : 8 * h + 8, :] = total
             act = swish(total)
-            grads[h] = grads[h] + jnp.sum(act * dgated[:, 8 * h : 8 * h + 8, :], axis=0)
+            dgated = dgs[lax.rem(r, 2)].reshape(BLOCK, SUB, 128)[:, 8 * h : 8 * h + 8, :]
+            grads[h] = grads[h] + jnp.sum(act * dgated, axis=0)
             pools[h] = pools[h] + jnp.sum(act[:9], axis=0) + jnp.sum(act[9:] * keep, axis=0)
+        expand(later, jnp.minimum(r + 5, HROWS - 1))
+        pres[lax.rem(r, 2)] = dot_nt(fp[jnp.minimum(r + 6, HROWS - 1)], we[...])
+        dgs[later] = dot_nt(cp[jnp.minimum(r + 1, ROWS - 1)], wp[...])
         return (*pools, *grads)
 
     zero = jnp.zeros((8, 128), F32)
@@ -322,7 +333,11 @@
             tile_spec(ROWS, BLOCK, SUB, 128),
             tile_spec(8, 128),
         ),
-        scratch_shapes=[pltpu.VMEM((25, 8, 128), F32)],
+        scratch_shapes=[
+            pltpu.VMEM((25, 8, 128), F32),
+            pltpu.VMEM((6, PIX, 128), F32),
+            pltpu.VMEM((2, PIX, 128), F32),
+        ],
         compiler_params=pltpu.CompilerParams(vmem_limit_bytes=56 * 2**20),
         name="phase_a",
     )(fp, cp, we, wp, misc)
@@ -481,13 +496,13 @@
 
 
 def second_kernel(
-    ex, depth, fp, cp, cpt, wp, gates, dd, out, gproj, gdepth, gated_rows, total, acc
+    ex, depth, fp, cp, cpt, wp, gates, dd, out, gproj, gdepth, gated_rows, total, acc, dgs
 ):
     keep = pad_mask()
     t = pl.program_id(0)
 
-    def pointwise(r, carry):
-        dgated = dot_nt(cp[r], wp[...]).reshape(BLOCK, SUB, 128)
+    def pointwise(slot, r):
+        dgated = dgs[slot].reshape(BLOCK, SUB, 128)
         both, gates_both = [], []
         for h in range(2):
             rows = slice(8 * h, 8 * h + 8)
@@ -497,21 +512,15 @@
         value = jnp.concatenate(both, axis=1).astype(BF16).astype(F32)
         store_row(dd.at[0], r, value)
         gated_rows[r] = jnp.concatenate(gates_both, axis=1).reshape(PIX, 128).astype(BF16)
-        return carry
-
-    lax.fori_loop(0, ROWS, pointwise, 0)
 
     @pl.when(t == 0)
     def _():
         total[...] = jnp.zeros_like(total)
 
-    def matmuls(r, grad):
-        total[r] = total[r] + dot_nn(gated_rows[r], wp[...])
-        return grad + dot_nn(cpt[r], gated_rows[r])
-
-    gproj[0] = lax.fori_loop(0, ROWS, matmuls, jnp.zeros((C, 128), F32))
-
     acc[...] = jnp.zeros_like(acc)
+    gproj[...] = jnp.zeros_like(gproj)
+    dgs[...] = dot_nt(cp[0:2].reshape(2 * PIX, C), wp[...]).reshape(2, PIX, 128)
+    pointwise(0, 0)
 
     def taps(r, carry):
         for h in range(2):
@@ -522,6 +531,10 @@
                 for j in range(5):
                     k = 5 * i + j
                     acc[k] = acc[k] + jnp.sum(mine * source[j : j + BLOCK], axis=0)
+        total[r] = total[r] + dot_nn(gated_rows[r], wp[...])
+        gproj[0] = gproj[0] + dot_nn(cpt[r], gated_rows[r])
+        pointwise(lax.rem(r + 1, 2), jnp.minimum(r + 1, ROWS - 1))
+        dgs[lax.rem(r, 2)] = dot_nt(cp[jnp.minimum(r + 2, ROWS - 1)], wp[...])
         return carry
 
     lax.fori_loop(0, ROWS, taps, 0)
@@ -570,6 +583,7 @@
             pltpu.VMEM((ROWS, PIX, 128), BF16),
             pltpu.VMEM((ROWS, PIX, C), F32),
             pltpu.VMEM((25, 8, 128), F32),
+            pltpu.VMEM((2, PIX, 128), F32),
         ],
         compiler_params=pltpu.CompilerParams(vmem_limit_bytes=56 * 2**20),
         cost_estimate=pl.CostEstimate(
@@ -579,38 +593,44 @@
     )(ex, depth, fp, cp, cpt, wp, gates)
 
 
-def third_kernel(dd, above, below, fp, cp, fpt, we, misc, out, gexp, wide_taps, rows_in, dpre, total):
+def third_kernel(
+    dd, above, below, fp, cp, fpt, we, misc, out, gexp, wide_taps, rows_in, dpre, total, pres
+):
     t = pl.program_id(0)
     spread_taps(misc, wide_taps)
     for n in range(2):
         store_row(rows_in, n, above[0, n].astype(F32))
         store_row(rows_in, ROWS + 2 + n, below[0, n].astype(F32))
-
-    def move(r, carry):
-        rows_in[r + 2] = dd[0, r]
-        return carry
-
-    lax.fori_loop(0, ROWS, move, 0)
+    for n in range(3):
+        rows_in[n + 2] = dd[0, n]
 
     @pl.when(t == 0)
     def _():
         total[...] = jnp.zeros_like(total)
 
+    gexp[...] = jnp.zeros_like(gexp)
+    dpre[0] = jnp.zeros((PIX, 128), BF16)
+    pres[0] = dot_nt(fp[2], we[...])
+
+    def matmuls(n, r):
+        total[r] = total[r] + dot_nn(dpre[n], we[...])
+        gexp[0] = gexp[0] + dot_nn(fpt[r], dpre[n])
+
     def conv(r, carry):
-        slope = swish_grad(dot_nt(fp[r + 2], we[...])).reshape(BLOCK, SUB, 128)
         both = []
         for h in range(2):
-            both.append(conv_row(rows_in, r, h, wide_taps, True) * slope[:, 8 * h : 8 * h + 8, :])
-        dpre[r] = jnp.concatenate(both, axis=1).reshape(PIX, 128).astype(BF16)
+            rows = slice(8 * h, 8 * h + 8)
+            slope = swish_grad(pres[lax.rem(r, 2)].reshape(BLOCK, SUB, 128)[:, rows, :])
+            both.append(conv_row(rows_in, r, h, wide_taps, True) * slope)
+        matmuls(r, jnp.maximum(r - 1, 0))
+        dpre[r + 1] = jnp.concatenate(both, axis=1).reshape(PIX, 128).astype(BF16)
+        pres[lax.rem(r + 1, 2)] = dot_nt(fp[jnp.minimum(r + 3, ROWS + 1)], we[...])
+        later = jnp.minimum(r + 3, ROWS - 1)
+        rows_in[later + 2] = dd[0, later]
         return carry
 
     lax.fori_loop(0, ROWS, conv, 0)
-
-    def matmuls(r, grad):
-        total[r] = total[r] + dot_nn(dpre[r], we[...])
-        return grad + dot_nn(fpt[r], dpre[r])
-
-    gexp[0] = lax.fori_loop(0, ROWS, matmuls, jnp.zeros((C, 128), F32))
+    matmuls(ROWS, ROWS - 1)
 
     @pl.when(t == TILES - 1)
     def _():
@@ -646,8 +666,9 @@
         scratch_shapes=[
             pltpu.VMEM((25, 8, 128), F32),
             pltpu.VMEM((HROWS, WIDE, SUB, 128), F32),
-            pltpu.VMEM((ROWS, PIX, 128), BF16),
+            pltpu.VMEM((ROWS + 1, PIX, 128), BF16),
             pltpu.VMEM((ROWS, PIX, C), F32),
+            pltpu.VMEM((2, PIX, 128), F32),
         ],
         compiler_params=pltpu.CompilerParams(vmem_limit_bytes=56 * 2**20),
         name="phase_c",

time: 327 us -> 283 us (0.87)
  Pallas kernels: 296 us -> 251 us
    pallas_call x1, Pallas kernels: 69.5 us -> 52.3 us  [first(): pl.pallas_call(first_kernel, grid=(TILES,), out_shape=(jax.ShapeDtypeStru...]
    pallas_call x1, Pallas kernels: 70.9 us -> 55.1 us  [second(): pl.pallas_call(second_kernel, grid=(TILES,), out_shape=(jax.ShapeDtypeStr...]
    pallas_call x1, Pallas kernels: 69.5 us -> 58.3 us  [third(): pl.pallas_call(third_kernel, grid=(TILES,), out_shape=(jax.ShapeDtypeStru...]
  transfers between devices with their start and end apart: 2 -> 2, of which waited for: 0 -> 0; matrix products, arithmetic and copies ran while one was open for 2% -> 2% of each run, Pallas kernels for 22% -> 20%
where the time goes in v2:
time: 283 us; the launch traced here: 282 us
  Pallas kernels  251 us (89%)
  local copies, waits for them, and re-layouts  24 us (8%)
  starting transfers between devices  5.55 us (2%)
    pallas_call x1, Pallas kernels, third(): pl.pallas_call(third_kernel, grid=(TILES,), out_shape=(jax.ShapeDtypeStru...  58.3 us
    pallas_call x1, Pallas kernels, second(): pl.pallas_call(second_kernel, grid=(TILES,), out_shape=(jax.ShapeDtypeStr...  55.1 us
    pallas_call x1, Pallas kernels, first(): pl.pallas_call(first_kernel, grid=(TILES,), out_shape=(jax.ShapeDtypeStru...  52.3 us
    pallas_call x1, Pallas kernels, reduce_grads(): pl.pallas_call(reduce_kernel, out_shape=jax.ShapeDtypeStruct((NS, CHUNK,...  26.6 us
    pallas_call x1, Pallas kernels, mid(): pl.pallas_call(mid_kernel, out_shape=(jax.ShapeDtypeStruct((8, CP), F32),...  20.2 us
    pallas_call x1, Pallas kernels, gather(): pl.pallas_call(gather_kernel, out_shape=(jax.ShapeDtypeStruct((2, ND, 80,...  18.7 us
    unnamed x23, local copies, waits for them, and re-layouts  13.3 us
    pallas_call x1, Pallas kernels, prep(): pl.pallas_call(prep_kernel, out_shape=(jax.ShapeDtypeStruct((HROWS, PIX,...  10.2 us
  transfers between devices with their start and end apart: 2, of which 0 were waited for; matrix products, arithmetic and copies ran while one was open for 2% of the time, Pallas kernels for 20%

profile of v2, /device:TPU:1, one launch (start us, length us, event | category | flops | bytes accessed | tf_op | source)
XLA Modules:
  0.0 282.2 jit_solution(9189385196559721390)
XLA Ops:
  0.6 0.0 copy-start.1
  0.7 0.8 reshape.27
  1.5 0.1 copy.30
  1.6 0.8 copy.31
  2.4 0.8 copy.32
  3.2 0.8 copy.33
  4.0 2.6 copy.34.feats
  6.6 0.0 copy-done.1
  6.6 0.0 copy-start.4
  6.6 0.0 copy-start.5
  6.6 1.6 copy.36.cot
  8.2 0.0 copy-done.4
  8.2 0.1 concatenate.7
  8.3 0.0 copy-done.5
  8.4 0.1 concatenate.6
  8.5 0.6 fusion.2.pack
  9.1 18.7 %gather_weights.1 = (bf16[2,16,80,256]{3,2,1,0:T(8,128)(2,1)}, bf16[2,2,100,176]{3,2,1,0:T(8,128)(2,1)}, bf16[2,2,100,176]{3,2,1,0:T(8,128)(2,1)}) custom-call(bf16[2,80,256]{2,1,0:T(8,128)(2,1)} %fusion.2.pack, bf16[2,12,100,176]{3,2,1,0:T(8,128)(2,1)} %copy.34.feats), custom_call_target="tpu_custom_call" | custom-call | tf_op jit(solution)/shard_map/gather_weights/pallas_call | solution.py:142
  27.8 10.2 %prep.1 = (bf16[16,208,176]{2,1,0:T(8,128)(2,1)}, bf16[12,208,176]{2,1,0:T(8,128)(2,1)}, bf16[12,176,208]{2,1,0:T(8,128)(2,1)}, bf16[12,176,208]{2,1,0:T(8,128)(...) custom-call(bf16[2,16,80,256]{3,2,1,0:T(8,128)(2,1)} %get-tuple-element.32.full, ...), custom_call_target="tpu_custom_call" | custom-call | tf_op jit(solution)/shard_map/prep/pallas_call | solution.py:211
  38.0 52.3 %phase_a.1 = (f32[9,16,17,16,128]{4,3,2,1,0:T(8,128)}, f32[9,12,13,16,128]{4,3,2,1,0:T(8,128)}, f32[9,8,128]{2,1,0:T(8,128)}) custom-call(bf16[16,208,176]{2,1,0:T(8,128)(2,1)} %get-tuple-element.35.fp, bf16[12,208,176]{2,1,0:T(8,128)(2,1)} %get-tuple-element.36.cp, bf16[1152,176]{1,0:T(8,128)(2,1)} %get-tuple-element.37.we, ...), custom_call_target="tpu_custom_call" | custom-call | tf_op jit(solution)/shard_map/phase_a/pallas_call | solution.py:316
  90.3 20.2 %squeeze_excite.1 = (f32[8,1152]{1,0:T(8,128)}, f32[128,128]{1,0:T(8,128)}, f32[128,128]{1,0:T(8,128)}, f32[8,128]{1,0:T(8,128)}) custom-call(f32[9,8,128]{2,1,0:T(8,128)} %get-tuple-element.43.sums, f32[136,1152]{1,0:T(8,128)} %get-tuple-element.39.misc, bf16[1,44]{1,0:T(2,128)(2,1)} %bitcast.21), custom_call_target="tpu_custom_call" | custom-call | tf_op jit(solution)/shard_map/squeeze_excite/pallas_call | solution.py:425
  110.5 9.9 %edge_rows.1 = bf16[9,4,13,16,128]{4,3,2,1,0:T(8,128)(2,1)} custom-call(f32[9,12,13,16,128]{4,3,2,1,0:T(8,128)} %get-tuple-element.41.depth, bf16[12,208,176]{2,1,0:T(8,128)(2,1)} %get-tuple-element.36.cp, bf16[1152,176]{1,0:T(8,128)(2,1)} %get-tuple-element.38.wp, f32[8,1152]{1,0:T(8,128)} %get-tuple-element.44.gates), custom_call_target="tpu_custom_call" | custom-call | tf_op jit(solution)/shard_map/edge_rows/pallas_call | solution.py:477
  120.4 2.8 fusion.3
  123.2 2.9 %collective-permute-start.1 = (bf16[9,2,13,16,128]{4,3,2,1,0:T(8,128)(2,1)}, bf16[9,2,13,16,128]{4,3,2,1,0:T(8,128)(2,1)S(1)}, u32[]{:S(2)}, u32[]{:S(2)}) collective-permute-start(bf16[9,2,13,16,128]{4,3,2,1,0:T(8,128)(2,1)} %get-tuple-element.73), channel_id=1, source_target_pairs={{16,0},{32,16},{48,32},{64,48},{80,64},{96,80},{112,96},{17,1},{33... | collective-permute-start | bytes 2875400 | tf_op jit(solution)/shard_map/ppermute | solution.py:796
  126.1 2.7 collective-permute-start
  128.8 55.1 %phase_b.1 = (f32[9,12,17,16,128]{4,3,2,1,0:T(8,128)}, bf16[2,12,100,176]{3,2,1,0:T(8,128)(2,1)}, f32[9,176,128]{2,1,0:T(8,128)}, f32[9,32,128]{2,1,0:T(8,128)}) custom-call(f32[9,16,17,16,128]{4,3,2,1,0:T(8,128)} %get-tuple-element.40.ex, f32[9,12,13,16,128]{4,3,2,1,0:T(8,128)} %get-tuple-element.41.depth, bf16[16,208,176]{2,1,0:T(8,128)(2,1)} %get-tuple-element.35.fp, ...), custom_call_target="tpu_custom_call" | custom-call | flops 4000000000 | bytes 50000000 | tf_op jit(solution)/shard_map/phase_b/pallas_call | solution.py:558
  183.8 0.0 copy-start.6
  183.8 2.5 copy.39
  186.3 0.0 copy-done.6
  186.3 0.7 copy.41
  187.0 1.3 slice.32
  188.4 1.2 slice_bitcast_fusion
  189.6 1.2 slice_bitcast_fusion.1
  190.8 0.0 collective-permute-done.1.below
  190.8 0.0 copy-start.2
  190.8 0.0 collective-permute-done.above
  190.8 0.0 copy-start.3
  190.8 0.9 copy-done.2
  191.7 0.3 copy-done.3
  192.0 58.3 %phase_c.1 = (bf16[2,12,100,176]{3,2,1,0:T(8,128)(2,1)}, f32[9,176,128]{2,1,0:T(8,128)}) custom-call(f32[9,12,17,16,128]{4,3,2,1,0:T(8,128)} %get-tuple-element.46.dd, bf16[9,2,13,16,128]{4,3,2,1,0:T(8,128)(2,1)} %copy-done.3, bf16[9,2,13,16,128]{4,3,2,1,0:T(8,128)(2,1)} %copy-done.2, bf16[16,208,176]{2,1,0:T(8,128)(2,1)} %get-tuple-element.35.fp, ...), custom_call_target="tpu_custom_call" | custom-call | tf_op jit(solution)/shard_map/phase_c/pallas_call | solution.py:648
  250.3 0.0 copy-start
  250.3 26.6 %reduce_grads.1 = f32[8,48,128]{2,1,0:T(8,128)} custom-call(f32[9,176,128]{2,1,0:T(8,128)} %get-tuple-element.49.gexp, f32[9,176,128]{2,1,0:T(8,128)} %get-tuple-element.50.gproj, f32[9,32,128]{2,1,0:T(8,128)} %get-tuple-element.51.gdepth), custom_call_target="tpu_custom_call" | custom-call | tf_op jit(solution)/shard_map/reduce_grads/pallas_call | solution.py:750
  276.9 0.7 slice.39
  277.7 0.9 fusion.4
  278.6 0.0 copy-done
  278.6 1.5 copy.40
  280.1 0.7 copy.43
  280.9 0.6 reshape.29
  281.5 0.7 copy.42
  (4 shorter events, 0.0 us)
Async XLA Ops:
  0.6 5.9 %copy-start.1 = (bf16[2,12,100,176]{2,3,1,0:T(8,128)(2,1)S(1)}, bf16[2,12,100,176]{2,3,1,0:T(8,128)(2,1)}, u32[]{:S(2)}) copy-start(bf16[2,12,100,176]{2,3,1,0:T(8,128)(2,1)} %param.17) | copy-start | bytes 2534404
  6.6 1.6 copy-start.4
  6.6 1.8 copy-start.5
  123.2 67.6 %collective-permute-start.1 = (bf16[9,2,13,16,128]{4,3,2,1,0:T(8,128)(2,1)}, bf16[9,2,13,16,128]{4,3,2,1,0:T(8,128)(2,1)S(1)}, u32[]{:S(2)}, u32[]{:S(2)}) collective-permute-start(bf16[9,2,13,16,128]{4,3,2,1,0:T(8,128)(2,1)} %get-tuple-element.73), channel_id=1, source_target_pairs={{16,0},{32,16},{48,32},{64,48},{80,64},{96,80},{112,96},{17,1},{33... | collective-permute-start | bytes 2875400 | tf_op jit(solution)/shard_map/ppermute | solution.py:796
  126.1 64.7 %collective-permute-start = (bf16[9,2,13,16,128]{4,3,2,1,0:T(8,128)(2,1)S(1)}, bf16[9,2,13,16,128]{4,3,2,1,0:T(8,128)(2,1)S(1)}, u32[]{:S(2)}, u32[]{:S(2)}) collective-permute-start(bf16[9,2,13,16,128]{4,3,2,1,0:T(8,128)(2,1)S(1)} %get-tuple-element.74), channel_id=1, source_target_pairs={{0,16},{16,32},{32,48},{48,64},{64,80},{80,96},{96,112},{1,17},{17... | collective-permute-start | bytes 2875400 | tf_op jit(solution)/shard_map/ppermute | solution.py:795
  183.8 2.5 copy-start.6
  190.8 0.9 copy-start.2
  190.8 1.3 copy-start.3
  250.3 28.3 %copy-start = (bf16[2,12,100,176]{3,2,1,0:T(8,128)(2,1)S(1)}, bf16[2,12,100,176]{3,2,1,0:T(8,128)(2,1)}, u32[]{:S(2)}) copy-start(bf16[2,12,100,176]{3,2,1,0:T(8,128)(2,1)} %get-tuple-element.65) | copy-start | bytes 2534404

commit v3 on v1

v3 whole, which is shorter than its diff:
```python
import functools

import jax
import jax.numpy as jnp
from jax import lax
from jax.experimental import pallas as pl
from jax.experimental.pallas import tpu as pltpu
from jax.sharding import PartitionSpec as P

F32 = jnp.float32
BF16 = jnp.bfloat16
MESH = pl.DeviceIdType.MESH
HIGH = lax.Precision.HIGHEST

IMGS, ROWS, COLS, C, SE = 2, 12, 100, 176, 44
BLOCK, SUB = 13, 16
PIX = BLOCK * SUB
WIDE = BLOCK + 4
HROWS = ROWS + 4
PART, SLOT = 66, 72
CP = 16 * SLOT
TILES = CP // 128
AREA = 9600.0
NS, ND = 8, 16

VMEM = pl.BlockSpec(memory_space=pltpu.VMEM)
ANY = pl.BlockSpec(memory_space=pl.ANY)


def sigmoid(value):
    return 0.5 * jnp.tanh(0.5 * value) + 0.5


def swish(value):
    return value * sigmoid(value)


def swish_grad(value):
    sig = sigmoid(value)
    act = value * sig
    return sig + act - act * sig


def dot_nt(left, right, precision=None):
    return lax.dot_general(
        left, right, (((1,), (1,)), ((), ())), precision=precision, preferred_element_type=F32
    )


def dot_tn(left, right, precision=None):
    return lax.dot_general(
        left, right, (((0,), (0,)), ((), ())), precision=precision, preferred_element_type=F32
    )


def dot_nn(left, right, precision=None):
    return lax.dot_general(
        left, right, (((1,), (0,)), ((), ())), precision=precision, preferred_element_type=F32
    )


def greet(space_peers, dp_peers):
    me_s, me_d = lax.axis_index("space"), lax.axis_index("dp")
    barrier = pltpu.get_barrier_semaphore()
    for k in space_peers:
        pl.semaphore_signal(
            barrier, inc=1, device_id=(lax.rem(me_s + k, NS), me_d), device_id_type=MESH
        )
    for k in dp_peers:
        pl.semaphore_signal(
            barrier, inc=1, device_id=(me_s, lax.rem(me_d + k, ND)), device_id_type=MESH
        )
    pl.semaphore_wait(barrier, len(space_peers) + len(dp_peers))


def one_hot(img, transposed):
    shape = (COLS, PIX) if transposed else (PIX, COLS)
    place = lax.broadcasted_iota(jnp.int32, shape, 1 if transposed else 0)
    col = lax.broadcasted_iota(jnp.int32, shape, 0 if transposed else 1)
    wanted = (col % BLOCK) * SUB + img * 8 + col // BLOCK
    return jnp.where(place == wanted, 1.0, 0.0).astype(BF16)


def gather_kernel(
    wet, wpr, taps, wrt, wx, bex, feats, cot,
    fp, cp, fpt, cpt, we, wp, misc,
    stage, pack, full, top, bottom, flat,
    send, recv, halo_send, halo_recv, mate_send, mate_recv,
):
    me_s, me_d = lax.axis_index("space"), lax.axis_index("dp")
    core = lax.rem(me_s, 2)
    mate = me_s + 1 - 2 * core
    barrier = pltpu.get_barrier_semaphore()
    for k in (1, NS - 1):
        pl.semaphore_signal(
            barrier, inc=1, device_id=(lax.rem(me_s + k, NS), me_d), device_id_type=MESH
        )
    for k in range(1, ND):
        pl.semaphore_signal(
            barrier, inc=1, device_id=(me_s, lax.rem(me_d + k, ND)), device_id_type=MESH
        )
    stage[...] = jnp.zeros_like(stage)
    stage[0, 0:PART, 0:C] = wet[...].astype(F32)
    stage[1, 0:PART, 0:C] = wpr[...].astype(F32)
    side = slice(C, C + PART)
    stage[0, 0:25, side] = taps[...].astype(F32)
    stage[0, 32 : 32 + SE, side] = wrt[...].astype(F32)
    stage[1, 0:SE, side] = wx[...].astype(F32)
    stage[1, 48:49, side] = bex[...].astype(F32)
    pack[...] = stage[...].astype(BF16)
    pl.semaphore_wait(barrier, ND + 1)
    copies = []
    for k in range(1, ND):
        copy = pltpu.make_async_remote_copy(
            src_ref=pack.at[core],
            dst_ref=full.at[core, me_d],
            send_sem=send.at[k],
            recv_sem=recv.at[k],
            device_id=(me_s, lax.rem(me_d + k, ND)),
            device_id_type=MESH,
        )
        copy.start()
        copies.append(copy)
    down = pltpu.make_async_remote_copy(
        src_ref=feats.at[:, pl.ds(ROWS - 2, 2)],
        dst_ref=top,
        send_sem=halo_send.at[0],
        recv_sem=halo_recv.at[0],
        device_id=(lax.rem(me_s + 1, NS), me_d),
        device_id_type=MESH,
    )
    up = pltpu.make_async_remote_copy(
        src_ref=feats.at[:, pl.ds(0, 2)],
        dst_ref=bottom,
        send_sem=halo_send.at[1],
        recv_sem=halo_recv.at[1],
        device_id=(lax.rem(me_s + NS - 1, NS), me_d),
        device_id_type=MESH,
    )
    down.start()
    up.start()
    full[core, me_d] = pack[core]
    spread = (one_hot(0, False), one_hot(1, False))
    gather_t = (one_hot(0, True), one_hot(1, True))

    def row(r, carry):
        for src, dst, shift in ((feats, fp, 2), (cot, cp, 0)):
            a, b = src[0, r], src[1, r]
            dst[r + shift] = (dot_nt(spread[0], a) + dot_nt(spread[1], b)).astype(BF16)
        return carry

    lax.fori_loop(0, ROWS, row, 0)
    for r in range(ROWS):
        for src, dst in ((feats, fpt), (cot, cpt)):
            value = dot_nn(src[0, r], gather_t[0]) + dot_nn(src[1, r], gather_t[1])
            dst[:, PIX * r : PIX * (r + 1)] = value.astype(BF16)
    for copy in copies:
        copy.wait()
    share = pltpu.make_async_remote_copy(
        src_ref=full.at[core],
        dst_ref=full.at[core],
        send_sem=mate_send,
        recv_sem=mate_recv,
        device_id=(mate, me_d),
        device_id_type=MESH,
    )
    share.start()
    down.wait()
    up.wait()
    has_top = jnp.where(me_s > 0, 1.0, 0.0)
    has_bottom = jnp.where(me_s < NS - 1, 1.0, 0.0)
    for r in range(2):
        value = dot_nt(spread[0], top[0, r]) + dot_nt(spread[1], top[1, r])
        fp[r] = (value * has_top).astype(BF16)
        value = dot_nt(spread[0], bottom[0, r]) + dot_nt(spread[1], bottom[1, r])
        fp[ROWS + 2 + r] = (value * has_bottom).astype(BF16)
    share.wait()
    for half, out in ((0, we), (1, wp)):
        for d in range(ND):
            part = full[half, d].astype(F32)
            flat[d * SLOT : (d + 1) * SLOT, :] = part[0:SLOT, 0:C]
            lanes = slice(d * SLOT, (d + 1) * SLOT)
            if half == 0:
                misc[0:80, lanes] = part[:, C : C + SLOT]
            else:
                misc[80:136, lanes] = part[0:56, C : C + SLOT]
        out[...] = flat[...].astype(BF16)


def gather(wet, wpr, taps, wrt, wx, bex, feats, cot):
    return pl.pallas_call(
        gather_kernel,
        out_shape=(
            jax.ShapeDtypeStruct((HROWS, PIX, C), BF16),
            jax.ShapeDtypeStruct((ROWS, PIX, C), BF16),
            jax.ShapeDtypeStruct((C, ROWS * PIX), BF16),
            jax.ShapeDtypeStruct((C, ROWS * PIX), BF16),
            jax.ShapeDtypeStruct((CP, C), BF16),
            jax.ShapeDtypeStruct((CP, C), BF16),
            jax.ShapeDtypeStruct((136, CP), F32),
        ),
        in_specs=[VMEM] * 8,
        out_specs=(VMEM,) * 7,
        scratch_shapes=[
            pltpu.VMEM((2, 80, 256), F32),
            pltpu.VMEM((2, 80, 256), BF16),
            pltpu.VMEM((2, ND, 80, 256), BF16),
            pltpu.VMEM((IMGS, 2, C, COLS), BF16),
            pltpu.VMEM((IMGS, 2, C, COLS), BF16),
            pltpu.VMEM((CP, C), F32),
            pltpu.SemaphoreType.DMA((ND,)),
            pltpu.SemaphoreType.DMA((ND,)),
            pltpu.SemaphoreType.DMA((2,)),
            pltpu.SemaphoreType.DMA((2,)),
            pltpu.SemaphoreType.DMA,
            pltpu.SemaphoreType.DMA,
        ],
        compiler_params=pltpu.CompilerParams(
            collective_id=0, has_side_effects=True, vmem_limit_bytes=56 * 2**20
        ),
        name="gather_weights",
    )(wet, wpr, taps, wrt, wx, bex, feats, cot)


def spread_taps(taps, wide_taps):
    for k in range(25):
        wide_taps[k] = jnp.broadcast_to(taps[k : k + 1, :], (8, 128))


def edge_columns(value):
    split = value.reshape(BLOCK, 2, 8, 128)
    block = lax.broadcasted_iota(jnp.int32, (2, 2, 8, 128), 2)
    left = jnp.where(block > 0, pltpu.roll(split[BLOCK - 2 :], 1, 2), 0.0)
    right = jnp.where(block < 7, pltpu.roll(split[:2], 7, 2), 0.0)
    return left.reshape(2, SUB, 128), right.reshape(2, SUB, 128)


def store_row(ref, r, value):
    left, right = edge_columns(value)
    ref[r, 0:2] = left
    ref[r, 2 : 2 + BLOCK] = value
    ref[r, 2 + BLOCK :] = right


def conv_row(ref, r, h, wide_taps, flip):
    total = jnp.zeros((BLOCK, 8, 128), F32)
    for i in range(5):
        source = ref[r + i, :, 8 * h : 8 * h + 8, :]
        for j in range(5):
            k = (4 - i) * 5 + 4 - j if flip else i * 5 + j
            total = total + source[j : j + BLOCK] * wide_taps[k][None]
    return total


def pad_mask():
    block = lax.broadcasted_iota(jnp.int32, (4, 8, 128), 1)
    return jnp.where(block < 7, 1.0, 0.0)


def first_kernel(fp, cp, we, wp, misc, saved, depth, sums, wide_taps, ex, dgs):
    spread_taps(misc, wide_taps)
    keep = pad_mask()

    def expand(q, carry):
        pre = dot_nt(fp[pl.ds(8 * q, 8)].reshape(8 * PIX, C), we[...])
        value = swish(pre).astype(BF16).astype(F32).reshape(8, BLOCK, SUB, 128)
        for n in range(8):
            store_row(ex, 8 * q + n, value[n])
        return carry

    lax.fori_loop(0, 2, expand, 0)
    cot_matmul(cp, wp, dgs)

    def conv(r, carry):
        pools, grads = list(carry[:2]), list(carry[2:])
        for h in range(2):
            total = conv_row(ex, r, h, wide_taps, False)
            depth[0, r, :, 8 * h : 8 * h + 8, :] = total
            act = swish(total)
            dgated = dgs[r, :, 8 * h : 8 * h + 8, :]
            grads[h] = grads[h] + jnp.sum(act * dgated, axis=0)
            pools[h] = pools[h] + jnp.sum(act[:9], axis=0) + jnp.sum(act[9:] * keep, axis=0)
        saved[0, r] = ex[r].astype(BF16)
        return (*pools, *grads)

    zero = jnp.zeros((8, 128), F32)
    parts = lax.fori_loop(0, ROWS, conv, (zero,) * 4)
    for r in range(ROWS, HROWS):
        saved[0, r] = ex[r].astype(BF16)
    for k in range(4):
        sums[0, k : k + 1, :] = jnp.sum(parts[k], axis=0, keepdims=True)
    sums[0, 4:8, :] = jnp.zeros((4, 128), F32)


def cot_matmul(cp, wp, dgs):
    def chunk(q, carry):
        rows = pl.ds(6 * q, 6)
        dgs[rows] = dot_nt(cp[rows].reshape(6 * PIX, C), wp[...]).reshape(6, BLOCK, SUB, 128)
        return carry

    lax.fori_loop(0, 2, chunk, 0)


def tile_spec(*shape):
    zeros = (0,) * len(shape)
    return pl.BlockSpec((1, *shape), lambda t: (t, *zeros))


def whole_spec(*shape):
    zeros = (0,) * len(shape)
    return pl.BlockSpec(shape, lambda t: zeros)


def first(fp, cp, we, wp, misc):
    return pl.pallas_call(
        first_kernel,
        grid=(TILES,),
        out_shape=(
            jax.ShapeDtypeStruct((TILES, HROWS, WIDE, SUB, 128), BF16),
            jax.ShapeDtypeStruct((TILES, ROWS, BLOCK, SUB, 128), F32),
            jax.ShapeDtypeStruct((TILES, 8, 128), F32),
        ),
        in_specs=[
            whole_spec(HROWS, PIX, C),
            whole_spec(ROWS, PIX, C),
            pl.BlockSpec((128, C), lambda t: (t, 0)),
            pl.BlockSpec((128, C), lambda t: (t, 0)),
            pl.BlockSpec((32, 128), lambda t: (0, t)),
        ],
        out_specs=(
            tile_spec(HROWS, WIDE, SUB, 128),
            tile_spec(ROWS, BLOCK, SUB, 128),
            tile_spec(8, 128),
        ),
        scratch_shapes=[
            pltpu.VMEM((25, 8, 128), F32),
            pltpu.VMEM((HROWS, WIDE, SUB, 128), F32),
            pltpu.VMEM((ROWS, BLOCK, SUB, 128), F32),
        ],
        compiler_params=pltpu.CompilerParams(vmem_limit_bytes=56 * 2**20),
        name="phase_a",
    )(fp, cp, we, wp, misc)


def mid_kernel(sums, misc, breduce, gates, msgs, packed, landed, lanes, vecs, send, recv):
    me_s, me_d = lax.axis_index("space"), lax.axis_index("dp")
    greet(range(1, NS), ())
    packed[...] = jnp.zeros_like(packed)
    for t in range(TILES):
        packed[t // 2, 4 * (t % 2) : 4 * (t % 2) + 4, :] = sums[t, 0:4, :]
    copies = []
    for k in range(1, NS):
        copy = pltpu.make_async_remote_copy(
            src_ref=packed,
            dst_ref=landed.at[k],
            send_sem=send.at[k],
            recv_sem=recv.at[k],
            device_id=(lax.rem(me_s + k, NS), me_d),
            device_id_type=MESH,
        )
        copy.start()
        copies.append(copy)
    landed[0] = packed[...]
    for copy in copies:
        copy.wait()
    total = landed[lax.rem(me_s, NS)]
    for s in range(1, NS):
        total = total + landed[lax.rem(me_s + NS - s, NS)]
    for t in range(TILES):
        lanes[0:4, 128 * t : 128 * (t + 1)] = total[t // 2, 4 * (t % 2) : 4 * (t % 2) + 4]
    lanes[:, CP:] = jnp.zeros((8, 128), F32)
    wr = misc[32 : 32 + SE, :]
    wx = misc[80 : 80 + SE, :]
    bexcite = misc[128:129, :]
    pooled = lanes[0:2, 0:CP] / AREA
    dgate = lanes[2:4, 0:CP]
    squeeze_pre = dot_nt(pooled, wr, HIGH) + breduce[...].astype(F32)
    squeeze = swish(squeeze_pre)
    gate = sigmoid(dot_nn(squeeze, wx, HIGH) + bexcite)
    dlogit = dgate * gate * (1.0 - gate)
    dsq = dot_nt(dlogit, wx, HIGH) * swish_grad(squeeze_pre)
    dpooled = dot_nn(dsq, wr, HIGH)
    gates[0:2, :] = gate
    gates[2:4, :] = dpooled / AREA
    gates[4:8, :] = jnp.zeros((4, CP), F32)
    lanes[0:2, 0:CP] = pooled
    lanes[2:4, 0:CP] = dlogit
    vecs[...] = jnp.zeros((8, 128), F32)
    vecs[4:6, 0:SE] = squeeze
    vecs[6:8, 0:SE] = dsq
    for d in range(ND):
        msgs[d, 0:4, :] = lanes[0:4, SLOT * d : SLOT * d + 128]
        msgs[d, 4:8, :] = vecs[4:8, :]


def mid(sums, misc, breduce):
    return pl.pallas_call(
        mid_kernel,
        out_shape=(
            jax.ShapeDtypeStruct((8, CP), F32),
            jax.ShapeDtypeStruct((ND, 8, 128), F32),
        ),
        in_specs=[VMEM] * 3,
        out_specs=(VMEM,) * 2,
        scratch_shapes=[
            pltpu.VMEM((5, 8, 128), F32),
            pltpu.VMEM((NS, 5, 8, 128), F32),
            pltpu.VMEM((8, CP + 128), F32),
            pltpu.VMEM((8, 128), F32),
            pltpu.SemaphoreType.DMA((NS,)),
            pltpu.SemaphoreType.DMA((NS,)),
        ],
        compiler_params=pltpu.CompilerParams(
            collective_id=1, has_side_effects=True, vmem_limit_bytes=56 * 2**20
        ),
        name="squeeze_excite",
    )(sums, misc, breduce)


def gate_row(depth, dgated, gates, h, keep):
    gate = gates[h : h + 1, :][None]
    pull = gates[2 + h : 3 + h, :][None]
    sig = sigmoid(depth)
    act = depth * sig
    gated = act * gate
    ddepth = (dgated * gate + pull) * (sig + act - act * sig)
    ddepth = jnp.concatenate([ddepth[:9], ddepth[9:] * keep], axis=0)
    return gated, ddepth


def unpermute(value, out, r):
    for img in range(2):
        out[img, r] = dot_tn(value, one_hot(img, False)).astype(BF16)


def all_channels(rows_in, weights, base, shift, turned, out, grad):
    def chunk(q, carry):
        block = rows_in[pl.ds(pl.multiple_of(4 * PIX * q, 4 * PIX), 4 * PIX), :]
        product = dot_nn(block, weights[...]).reshape(4, PIX, C)
        for n in range(4):
            value = product[n] + base[4 * q + n + shift].astype(F32)
            unpermute(value.astype(BF16), out, 4 * q + n)
        return carry

    lax.fori_loop(0, 3, chunk, 0)

    def lanes(q, carry):
        span = pl.ds(pl.multiple_of(384 * q, 128), 384)
        grad[:, span] = dot_nn(turned[...], rows_in[:, span])
        return carry

    lax.fori_loop(0, 3, lanes, 0)


def second_kernel(
    depth, fp, cp, cpt, wp, gates, dd, upper, lower, out, gproj, gated_rows, dgs
):
    keep = pad_mask()
    t = pl.program_id(0)
    lane = pl.ds(pl.multiple_of(128 * t, 128), 128)
    cot_matmul(cp, wp.at[lane], dgs)

    def pointwise(r, carry):
        both, gates_both = [], []
        for h in range(2):
            rows = slice(8 * h, 8 * h + 8)
            gated, ddepth = gate_row(depth[0, r, :, rows, :], dgs[r, :, rows, :], gates, h, keep)
            both.append(ddepth)
            gates_both.append(gated)
        dd[0, r] = jnp.concatenate(both, axis=1).astype(BF16)
        gated_rows[pl.ds(pl.multiple_of(r * PIX, PIX), PIX), lane] = (
            jnp.concatenate(gates_both, axis=1).reshape(PIX, 128).astype(BF16)
        )
        return carry

    lax.fori_loop(0, ROWS, pointwise, 0)
    upper[0] = dd[0, 0:2]
    lower[0] = dd[0, ROWS - 2 :]

    @pl.when(t == TILES - 1)
    def _():
        all_channels(gated_rows, wp, fp, 2, cpt, out, gproj)


def second(depth, fp, cp, cpt, wp, gates):
    return pl.pallas_call(
        second_kernel,
        grid=(TILES,),
        out_shape=(
            jax.ShapeDtypeStruct((TILES, ROWS, BLOCK, SUB, 128), BF16),
            jax.ShapeDtypeStruct((TILES, 2, BLOCK, SUB, 128), BF16),
            jax.ShapeDtypeStruct((TILES, 2, BLOCK, SUB, 128), BF16),
            jax.ShapeDtypeStruct((IMGS, ROWS, C, COLS), BF16),
            jax.ShapeDtypeStruct((C, CP), F32),
        ),
        in_specs=[
            tile_spec(ROWS, BLOCK, SUB, 128),
            whole_spec(HROWS, PIX, C),
            whole_spec(ROWS, PIX, C),
            whole_spec(C, ROWS * PIX),
            whole_spec(CP, C),
            pl.BlockSpec((8, 128), lambda t: (0, t)),
        ],
        out_specs=(
            tile_spec(ROWS, BLOCK, SUB, 128),
            tile_spec(2, BLOCK, SUB, 128),
            tile_spec(2, BLOCK, SUB, 128),
            whole_spec(IMGS, ROWS, C, COLS),
            whole_spec(C, CP),
        ),
        scratch_shapes=[
            pltpu.VMEM((ROWS * PIX, CP), BF16),
            pltpu.VMEM((ROWS, BLOCK, SUB, 128), F32),
        ],
        compiler_params=pltpu.CompilerParams(vmem_limit_bytes=56 * 2**20),
        name="phase_b",
    )(depth, fp, cp, cpt, wp, gates)


def tap_kernel(ex, dd, gdepth, acc):
    acc[...] = jnp.zeros_like(acc)

    def taps(r, carry):
        for h in range(2):
            rows = slice(8 * h, 8 * h + 8)
            mine = dd[0, r, :, :, :].astype(F32)[:, rows, :]
            for i in range(5):
                source = ex[0, r + i].astype(F32)[:, rows, :]
                for j in range(5):
                    k = 5 * i + j
                    acc[k] = acc[k] + jnp.sum(mine * source[j : j + BLOCK], axis=0)
        return carry

    lax.fori_loop(0, ROWS, taps, 0)
    for k in range(25):
        gdepth[0, k : k + 1, :] = jnp.sum(acc[k], axis=0, keepdims=True)
    gdepth[0, 25:32, :] = jnp.zeros((7, 128), F32)


def tap_grads(ex, dd):
    return pl.pallas_call(
        tap_kernel,
        grid=(TILES,),
        out_shape=jax.ShapeDtypeStruct((TILES, 32, 128), F32),
        in_specs=[tile_spec(HROWS, WIDE, SUB, 128), tile_spec(ROWS, BLOCK, SUB, 128)],
        out_specs=tile_spec(32, 128),
        scratch_shapes=[pltpu.VMEM((25, 8, 128), F32)],
        compiler_params=pltpu.CompilerParams(vmem_limit_bytes=56 * 2**20),
        cost_estimate=pl.CostEstimate(
            flops=4 * 10**9, bytes_accessed=50 * 10**6, transcendentals=3 * 10**6
        ),
        name="tap_grads",
    )(ex, dd)


def third_kernel(
    dd, above, below, fp, cp, fpt, we, misc, out, gexp, wide_taps, rows_in, dpre, pres
):
    t = pl.program_id(0)
    lane = pl.ds(pl.multiple_of(128 * t, 128), 128)
    spread_taps(misc, wide_taps)
    for n in range(2):
        store_row(rows_in, n, above[0, n].astype(F32))
        store_row(rows_in, ROWS + 2 + n, below[0, n].astype(F32))

    def spread(r, carry):
        store_row(rows_in, r + 2, dd[0, r].astype(F32))
        return carry

    lax.fori_loop(0, ROWS, spread, 0)

    def chunk(q, carry):
        pre = dot_nt(fp[pl.ds(6 * q + 2, 6)].reshape(6 * PIX, C), we[lane, :])
        pres[pl.ds(6 * q, 6)] = swish_grad(pre).reshape(6, BLOCK, SUB, 128)
        return carry

    lax.fori_loop(0, 2, chunk, 0)

    def conv(r, carry):
        both = []
        for h in range(2):
            slope = pres[r, :, 8 * h : 8 * h + 8, :]
            both.append(conv_row(rows_in, r, h, wide_taps, True) * slope)
        dpre[pl.ds(pl.multiple_of(r * PIX, PIX), PIX), lane] = (
            jnp.concatenate(both, axis=1).reshape(PIX, 128).astype(BF16)
        )
        return carry

    lax.fori_loop(0, ROWS, conv, 0)

    @pl.when(t == TILES - 1)
    def _():
        all_channels(dpre, we, cp, 0, fpt, out, gexp)


def third(dd, above, below, fp, cp, fpt, we, misc):
    return pl.pallas_call(
        third_kernel,
        grid=(TILES,),
        out_shape=(
            jax.ShapeDtypeStruct((IMGS, ROWS, C, COLS), BF16),
            jax.ShapeDtypeStruct((C, CP), F32),
        ),
        in_specs=[
            tile_spec(ROWS, BLOCK, SUB, 128),
            tile_spec(2, BLOCK, SUB, 128),
            tile_spec(2, BLOCK, SUB, 128),
            whole_spec(HROWS, PIX, C),
            whole_spec(ROWS, PIX, C),
            whole_spec(C, ROWS * PIX),
            whole_spec(CP, C),
            pl.BlockSpec((32, 128), lambda t: (0, t)),
        ],
        out_specs=(whole_spec(IMGS, ROWS, C, COLS), whole_spec(C, CP)),
        scratch_shapes=[
            pltpu.VMEM((25, 8, 128), F32),
            pltpu.VMEM((HROWS, WIDE, SUB, 128), F32),
            pltpu.VMEM((ROWS * PIX, CP), BF16),
            pltpu.VMEM((ROWS, BLOCK, SUB, 128), F32),
        ],
        compiler_params=pltpu.CompilerParams(vmem_limit_bytes=56 * 2**20),
        name="phase_c",
    )(dd, above, below, fp, cp, fpt, we, misc)


CHUNK = 48


def reduce_kernel(
    gexp, gproj, gdepth, msgs, final, mail, stack, packed, landed, part, pieces, got,
    send, recv, dsend, drecv, fsend, frecv, msend, mrecv,
):
    me_s, me_d = lax.axis_index("space"), lax.axis_index("dp")
    greet(range(1, NS), range(1, ND))
    small = []
    for k in range(1, ND):
        target = lax.rem(me_d + k, ND)
        copy = pltpu.make_async_remote_copy(
            src_ref=msgs.at[target],
            dst_ref=mail.at[me_d],
            send_sem=msend.at[k],
            recv_sem=mrecv.at[k],
            device_id=(me_s, target),
            device_id_type=MESH,
        )
        copy.start()
        small.append(copy)
    mail[me_d] = msgs[me_d]
    stack[0:C, :] = gexp[...]
    stack[C : 2 * C, :] = gproj[...]
    for t in range(TILES):
        stack[2 * C :, 128 * t : 128 * (t + 1)] = gdepth[t]
    packed[...] = stack[...].reshape(NS, CHUNK, CP).astype(BF16)
    copies = []
    for k in range(1, NS):
        target = lax.rem(me_s + k, NS)
        copy = pltpu.make_async_remote_copy(
            src_ref=packed.at[target],
            dst_ref=landed.at[k],
            send_sem=send.at[k],
            recv_sem=recv.at[k],
            device_id=(target, me_d),
            device_id_type=MESH,
        )
        copy.start()
        copies.append(copy)
    start = pl.multiple_of(me_s * CHUNK, CHUNK)
    part[:, 0:CP] = stack[pl.ds(start, CHUNK), :]
    part[:, CP:] = jnp.zeros((CHUNK, 128), F32)
    for k, copy in enumerate(copies):
        copy.wait()
        part[:, 0:CP] = part[:, 0:CP] + landed[k + 1].astype(F32)
    for d in range(ND):
        pieces[d] = part[:, SLOT * d : SLOT * d + 128].astype(BF16)
    copies = []
    for k in range(1, ND):
        target = lax.rem(me_d + k, ND)
        copy = pltpu.make_async_remote_copy(
            src_ref=pieces.at[target],
            dst_ref=got.at[k],
            send_sem=dsend.at[k],
            recv_sem=drecv.at[k],
            device_id=(me_s, target),
            device_id_type=MESH,
        )
        copy.start()
        copies.append(copy)
    total = pieces[me_d].astype(F32)
    for k, copy in enumerate(copies):
        copy.wait()
        total = total + got[k + 1].astype(F32)
    final[me_s] = total
    copies = []
    for k in range(1, NS):
        copy = pltpu.make_async_remote_copy(
            src_ref=final.at[me_s],
            dst_ref=final.at[me_s],
            send_sem=fsend.at[k],
            recv_sem=frecv.at[k],
            device_id=(lax.rem(me_s + k, NS), me_d),
            device_id_type=MESH,
        )
        copy.start()
        copies.append(copy)
    for copy in copies:
        copy.wait()
    for copy in small:
        copy.wait()


def reduce_grads(gexp, gproj, gdepth, msgs):
    return pl.pallas_call(
        reduce_kernel,
        out_shape=(
            jax.ShapeDtypeStruct((NS, CHUNK, 128), F32),
            jax.ShapeDtypeStruct((ND, 8, 128), F32),
        ),
        in_specs=[VMEM] * 4,
        out_specs=(VMEM, VMEM),
        scratch_shapes=[
            pltpu.VMEM((NS * CHUNK, CP), F32),
            pltpu.VMEM((NS, CHUNK, CP), BF16),
            pltpu.VMEM((NS, CHUNK, CP), BF16),
            pltpu.VMEM((CHUNK, CP + 128), F32),
            pltpu.VMEM((ND, CHUNK, 128), BF16),
            pltpu.VMEM((ND, CHUNK, 128), BF16),
            pltpu.SemaphoreType.DMA((NS,)),
            pltpu.SemaphoreType.DMA((NS,)),
            pltpu.SemaphoreType.DMA((ND,)),
            pltpu.SemaphoreType.DMA((ND,)),
            pltpu.SemaphoreType.DMA((NS,)),
            pltpu.SemaphoreType.DMA((NS,)),
            pltpu.SemaphoreType.DMA((ND,)),
            pltpu.SemaphoreType.DMA((ND,)),
        ],
        compiler_params=pltpu.CompilerParams(
            collective_id=2, has_side_effects=True, vmem_limit_bytes=56 * 2**20
        ),
        name="reduce_grads",
    )(gexp, gproj, gdepth, msgs)


def finish_kernel(final, mail, gexp, gdepth, greduce, gexcite, gbex, gproj, gbred):
    grads = final[...].reshape(NS * CHUNK, 128)
    gexp[...] = grads[0:C].T[0:PART]
    gproj[...] = grads[C : 2 * C].T[0:PART]
    gdepth[...] = grads[2 * C : 2 * C + 25, 0:PART]
    rows = [mail[d] for d in range(ND)]
    pool_all = jnp.concatenate([row[0:2] for row in rows], axis=0)
    dlog_all = jnp.concatenate([row[2:4] for row in rows], axis=0)
    sq_all = jnp.concatenate([row[4:6] for row in rows], axis=0)
    dsq_all = jnp.concatenate([row[6:8] for row in rows], axis=0)
    greduce[...] = dot_tn(dsq_all, pool_all, HIGH)[0:SE, 0:PART]
    gexcite[...] = dot_tn(sq_all, dlog_all, HIGH)[0:SE, 0:PART]
    gbex[...] = jnp.sum(dlog_all, axis=0, keepdims=True)[:, 0:PART]
    gbred[...] = jnp.sum(dsq_all, axis=0, keepdims=True)[:, 0:SE]


def finish(final, mail):
    return pl.pallas_call(
        finish_kernel,
        out_shape=(
            jax.ShapeDtypeStruct((PART, C), F32),
            jax.ShapeDtypeStruct((25, PART), F32),
            jax.ShapeDtypeStruct((SE, PART), F32),
            jax.ShapeDtypeStruct((SE, PART), F32),
            jax.ShapeDtypeStruct((1, PART), F32),
            jax.ShapeDtypeStruct((PART, C), F32),
            jax.ShapeDtypeStruct((1, SE), F32),
        ),
        in_specs=[VMEM] * 2,
        out_specs=(VMEM,) * 7,
        name="finish",
    )(final, mail)


def on_device(
    features, w_expand, w_depth, w_reduce, b_reduce, w_excite, b_excite, w_project, cotangent
):
    fp, cp, fpt, cpt, we, wp, misc = gather(
        w_expand.T,
        w_project,
        w_depth.reshape(25, PART),
        w_reduce.T,
        w_excite,
        b_excite[None, :],
        features.swapaxes(2, 3),
        cotangent.swapaxes(2, 3),
    )
    ex, depth, sums = first(fp, cp, we, wp, misc)
    gates, msgs = mid(sums, misc, b_reduce[None, :])
    dd, upper, lower, output, gproj = second(depth, fp, cp, cpt, wp, gates)
    above = lax.ppermute(lower, "space", [(i, i + 1) for i in range(NS - 1)])
    below = lax.ppermute(upper, "space", [(i + 1, i) for i in range(NS - 1)])
    gdepth = tap_grads(ex, dd)
    grad_features, gexp = third(dd, above, below, fp, cp, fpt, we, misc)
    final, mail = reduce_grads(gexp, gproj, gdepth, msgs)
    s_expand, s_depth, s_reduce, s_excite, s_bexcite, s_project, s_breduce = finish(final, mail)
    return (
        output.swapaxes(2, 3),
        grad_features.swapaxes(2, 3),
        s_expand.T,
        s_depth.reshape(5, 5, PART),
        s_reduce.T,
        s_excite,
        s_bexcite[0],
        s_project,
        s_breduce[0],
    )


def solution(mesh):
    return jax.shard_map(
        on_device,
        mesh=mesh,
        in_specs=(
            P("dp", "space", None, None),
            P(None, "dp"),
            P(None, None, "dp"),
            P("dp", None),
            P(),
            P(None, "dp"),
            P("dp"),
            P("dp", None),
            P("dp", "space", None, None),
        ),
        out_specs=(
            P("dp", "space", None, None),
            P("dp", "space", None, None),
            P(None, "dp"),
            P(None, None, "dp"),
            P("dp", None),
            P(None, "dp"),
            P("dp"),
            P("dp", None),
            P(),
        ),
        check_vma=False,
    )
```

time: 327 us -> 210 us (0.64)
  Pallas kernels: 296 us -> 200 us
  local copies, waits for them, and re-layouts: 24 us -> 3.93 us
    pallas_call x1, Pallas kernels: 70.9 us -> 23 us  [second(): pl.pallas_call(second_kernel, grid=(TILES,), out_shape=(jax.ShapeDtypeStr...]
    pallas_call x1, Pallas kernels: 69.5 us -> 43.6 us  [third(): pl.pallas_call(third_kernel, grid=(TILES,), out_shape=(jax.ShapeDtypeStru...]
    pallas_call x1, Pallas kernels: 69.5 us -> 44.1 us  [first(): pl.pallas_call(first_kernel, grid=(TILES,), out_shape=(jax.ShapeDtypeStru...]
    pallas_call x4, Pallas kernels: 65.4 us -> 78.7 us  [the longest x1 29.5 us: reduce_grads(): pl.pallas_call(reduce_kernel, out_shape=(jax.ShapeDtypeStruct((NS, CHUNK,...]
    unnamed x23 -> x4, local copies, waits for them, and re-layouts: 13.3 us -> 1.28 us
    pallas_call x1, Pallas kernels: 20.2 us -> 10.9 us  [mid(): pl.pallas_call(mid_kernel, out_shape=(jax.ShapeDtypeStruct((8, CP), F32),...]
    slice x5 -> x0, local copies, waits for them, and re-layouts: 5.8 us -> none  [the longest x1 2.78 us: on_device(): edge[:, 0:2]]
  transfers between devices with their start and end apart: 2 -> 2, of which waited for: 0 -> 0; matrix products, arithmetic and copies ran while one was open for 2% -> 0% of each run, Pallas kernels for 22% -> 12%
where the time goes in v3:
time: 210 us; the launch traced here: 209 us
  Pallas kernels  200 us (95%)
  starting transfers between devices  4.38 us (2%)
  local copies, waits for them, and re-layouts  3.93 us (2%)
    pallas_call x1, Pallas kernels, first(): pl.pallas_call(first_kernel, grid=(TILES,), out_shape=(jax.ShapeDtypeStru...  44.1 us
    pallas_call x1, Pallas kernels, third(): pl.pallas_call(third_kernel, grid=(TILES,), out_shape=(jax.ShapeDtypeStru...  43.6 us
    pallas_call x1, Pallas kernels, reduce_grads(): pl.pallas_call(reduce_kernel, out_shape=(jax.ShapeDtypeStruct((NS, CHUNK,...  29.5 us
    pallas_call x1, Pallas kernels, tap_grads(): pl.pallas_call(tap_kernel, grid=(TILES,), out_shape=jax.ShapeDtypeStruct(...  24.7 us
    pallas_call x1, Pallas kernels, second(): pl.pallas_call(second_kernel, grid=(TILES,), out_shape=(jax.ShapeDtypeStr...  23 us
    pallas_call x1, Pallas kernels, gather(): pl.pallas_call(gather_kernel, out_shape=(jax.ShapeDtypeStruct((HROWS, PIX...  22.7 us
    pallas_call x1, Pallas kernels, mid(): pl.pallas_call(mid_kernel, out_shape=(jax.ShapeDtypeStruct((8, CP), F32),...  10.9 us
  transfers between devices with their start and end apart: 2, of which 0 were waited for; matrix products, arithmetic and copies ran while one was open for 0% of the time, Pallas kernels for 12%

profile of v3, /device:TPU:1, one launch (start us, length us, event | category | flops | bytes accessed | tf_op | source)
XLA Modules:
  0.0 209.3 jit_solution(2821702604263850479)
XLA Ops:
  0.6 1.3 reshape.24.taps
  2.0 22.7 %gather_weights.1 = (bf16[16,208,176]{2,1,0:T(8,128)(2,1)}, bf16[12,208,176]{2,1,0:T(8,128)(2,1)}, bf16[176,2496]{1,0:T(8,128)(2,1)}, bf16[176,2496]{1,0:T(8,128...) custom-call(bf16[66,176]{1,0:T(8,128)(2,1)} %bitcast.14, bf16[66,176]{1,0:T(8,128)(2,1)} %wpr.1, ...), custom_call_target="tpu_custom_call" | custom-call | tf_op jit(solution)/shard_map/gather_weights/pallas_call | solution.py:191
  24.7 44.1 %phase_a.1 = (bf16[9,16,17,16,128]{4,3,2,1,0:T(8,128)(2,1)}, f32[9,12,13,16,128]{4,3,2,1,0:T(8,128)}, f32[9,8,128]{2,1,0:T(8,128)}) custom-call(bf16[16,208,176]{2,1,0:T(8,128)(2,1)} %get-tuple-element.37.fp, bf16[12,208,176]{2,1,0:T(8,128)(2,1)} %get-tuple-element.38.cp, bf16[1152,176]{1,0:T(8,128)(2,1)} %get-tuple-element.39.we, ...), custom_call_target="tpu_custom_call" | custom-call | tf_op jit(solution)/shard_map/phase_a/pallas_call | solution.py:315
  68.8 10.9 %squeeze_excite.1 = (f32[8,1152]{1,0:T(8,128)}, f32[16,8,128]{2,1,0:T(8,128)}) custom-call(f32[9,8,128]{2,1,0:T(8,128)} %get-tuple-element.44.sums, f32[136,1152]{1,0:T(8,128)} %get-tuple-element.41.misc, bf16[1,44]{1,0:T(2,128)(2,1)} %bitcast.17), custom_call_target="tpu_custom_call" | custom-call | tf_op jit(solution)/shard_map/squeeze_excite/pallas_call | solution.py:397
  79.7 23.0 %phase_b.1 = (bf16[9,12,13,16,128]{4,3,2,1,0:T(8,128)(2,1)}, bf16[9,2,13,16,128]{4,3,2,1,0:T(8,128)(2,1)}, bf16[9,2,13,16,128]{4,3,2,1,0:T(8,128)(2,1)}, bf16[2,12,176,100]{3,2,1,0:T(8,128)(2,1)}, f32[176,1152]{1,0:T(8,128)}) custom-call(f32[9,12,13,16,128]{4,3,2,1,0:T(8,128)} %get-tuple-element.42.depth, bf16[16,208,176]{2,1,0:T(8,128)(2,1)} %get-tuple-element.37.fp, ...), custom_call_target="tpu_custom_call" | custom-call | tf_op jit(solution)/shard_map/phase_b/pallas_call | solution.py:486
  102.7 1.9 collective-permute-start
  104.6 2.5 %collective-permute-start.1 = (bf16[9,2,13,16,128]{4,3,2,1,0:T(8,128)(2,1)}, bf16[9,2,13,16,128]{4,3,2,1,0:T(8,128)(2,1)S(1)}, u32[]{:S(2)}, u32[]{:S(2)}) collective-permute-start(bf16[9,2,13,16,128]{4,3,2,1,0:T(8,128)(2,1)} %get-tuple-element.49), channel_id=1, source_target_pairs={{16,0},{32,16},{48,32},{64,48},{80,64},{96,80},{112,96},{17,1},{33... | collective-permute-start | bytes 2875400 | tf_op jit(solution)/shard_map/ppermute | solution.py:794
  107.1 24.7 %tap_grads.1.gdepth = f32[9,32,128]{2,1,0:T(8,128)} custom-call(bf16[9,16,17,16,128]{4,3,2,1,0:T(8,128)(2,1)} %get-tuple-element.54.ex, bf16[9,12,13,16,128]{4,3,2,1,0:T(8,128)(2,1)} %get-tuple-element.47.dd), custom_call_target="tpu_custom_call" | custom-call | flops 4000000000 | bytes 50000000 | tf_op jit(solution)/shard_map/tap_grads/pallas_call | solution.py:541
  131.8 0.0 collective-permute-done.above
  131.8 0.0 copy-start
  131.8 0.0 collective-permute-done.1.below
  131.8 0.0 copy-start.1
  131.8 0.9 copy-done
  132.7 0.3 copy-done.1
  133.1 43.6 %phase_c.1 = (bf16[2,12,176,100]{3,2,1,0:T(8,128)(2,1)}, f32[176,1152]{1,0:T(8,128)}) custom-call(bf16[9,12,13,16,128]{4,3,2,1,0:T(8,128)(2,1)} %get-tuple-element.47.dd, bf16[9,2,13,16,128]{4,3,2,1,0:T(8,128)(2,1)} %copy-done, bf16[9,2,13,16,128]{4,3,2,1,0:T(8,128)(2,1)} %copy-done.1, bf16[16,208,176]{2,1,0:T(8,128)(2,1)} %get-tuple-element.37.fp, ...), custom_call_target="tpu_custom_call" | custom-call | tf_op jit(solution)/shard_map/phase_c/pallas_call | solution.py:597
  176.7 29.5 %reduce_grads.1 = (f32[8,48,128]{2,1,0:T(8,128)}, f32[16,8,128]{2,1,0:T(8,128)}) custom-call(f32[176,1152]{1,0:T(8,128)} %get-tuple-element.52.gexp, f32[176,1152]{1,0:T(8,128)} %get-tuple-element.53.gproj, f32[9,32,128]{2,1,0:T(8,128)} %tap_grads.1.gdepth, f32[16,8,128]{2,1,0:T(8,128)} %get-tuple-element.55.msgs), custom_call_target="tpu_custom_call" | custom-call | tf_op jit(solution)/shard_map/reduce_grads/pallas_call | solution.py:712
  206.1 1.9 finish.1
  208.0 1.3 reshape.25
Async XLA Ops:
  102.7 29.1 %collective-permute-start = (bf16[9,2,13,16,128]{4,3,2,1,0:T(8,128)(2,1)}, bf16[9,2,13,16,128]{4,3,2,1,0:T(8,128)(2,1)S(1)}, u32[]{:S(2)}, u32[]{:S(2)}) collective-permute-start(bf16[9,2,13,16,128]{4,3,2,1,0:T(8,128)(2,1)} %get-tuple-element.48), channel_id=1, source_target_pairs={{0,16},{16,32},{32,48},{48,64},{64,80},{80,96},{96,112},{1,17},{17... | collective-permute-start | bytes 2875400 | tf_op jit(solution)/shard_map/ppermute | solution.py:793
  104.6 27.1 %collective-permute-start.1 = (bf16[9,2,13,16,128]{4,3,2,1,0:T(8,128)(2,1)}, bf16[9,2,13,16,128]{4,3,2,1,0:T(8,128)(2,1)S(1)}, u32[]{:S(2)}, u32[]{:S(2)}) collective-permute-start(bf16[9,2,13,16,128]{4,3,2,1,0:T(8,128)(2,1)} %get-tuple-element.49), channel_id=1, source_target_pairs={{16,0},{32,16},{48,32},{64,48},{80,64},{96,80},{112,96},{17,1},{33... | collective-permute-start | bytes 2875400 | tf_op jit(solution)/shard_map/ppermute | solution.py:794
  131.8 0.9 copy-start
  131.8 1.3 copy-start.1

commit v4 on v3

--- a/solution.py
+++ b/solution.py
@@ -433,7 +433,7 @@
         out[img, r] = dot_tn(value, one_hot(img, False)).astype(BF16)
 
 
-def all_channels(rows_in, weights, base, shift, turned, out, grad):
+def all_channels_out(rows_in, weights, base, shift, out):
     def chunk(q, carry):
         block = rows_in[pl.ds(pl.multiple_of(4 * PIX * q, 4 * PIX), 4 * PIX), :]
         product = dot_nn(block, weights[...]).reshape(4, PIX, C)
@@ -444,6 +444,8 @@
 
     lax.fori_loop(0, 3, chunk, 0)
 
+
+def all_channels_grad(rows_in, turned, grad):
     def lanes(q, carry):
         span = pl.ds(pl.multiple_of(384 * q, 128), 384)
         grad[:, span] = dot_nn(turned[...], rows_in[:, span])
@@ -479,7 +481,8 @@
 
     @pl.when(t == TILES - 1)
     def _():
-        all_channels(gated_rows, wp, fp, 2, cpt, out, gproj)
+        all_channels_out(gated_rows, wp, fp, 2, out)
+        all_channels_grad(gated_rows, cpt, gproj)
 
 
 def second(depth, fp, cp, cpt, wp, gates):
@@ -553,11 +556,77 @@
     )(ex, dd)
 
 
+EARLY = C + 32
+
+
 def third_kernel(
-    dd, above, below, fp, cp, fpt, we, misc, out, gexp, wide_taps, rows_in, dpre, pres
+    dd, above, below, fp, cp, fpt, we, misc, gproj, gdepth, msgs,
+    out, early, late, mail_out,
+    mail, wide_taps, rows_in, dpre, pres, flat, epiece, egot, espace, lpiece, lgot, lspace,
+    esend, erecv, fsend, frecv, lsend, lrecv, gsend, grecv, msend, mrecv,
 ):
     t = pl.program_id(0)
+    me_s, me_d = lax.axis_index("space"), lax.axis_index("dp")
     lane = pl.ds(pl.multiple_of(128 * t, 128), 128)
+
+    def to_dp(src, dst, send, recv, slotted):
+        copies = []
+        for k in range(1, ND):
+            target = lax.rem(me_d + k, ND)
+            copies.append(
+                pltpu.make_async_remote_copy(
+                    src_ref=src.at[target],
+                    dst_ref=dst.at[me_d] if slotted else dst.at[k],
+                    send_sem=send.at[k],
+                    recv_sem=recv.at[k],
+                    device_id=(me_s, target),
+                    device_id_type=MESH,
+                )
+            )
+        return copies
+
+    def to_space(ref, send, recv):
+        copies = []
+        for k in range(1, NS):
+            copies.append(
+                pltpu.make_async_remote_copy(
+                    src_ref=ref.at[me_s],
+                    dst_ref=ref.at[me_s],
+                    send_sem=send.at[k],
+                    recv_sem=recv.at[k],
+                    device_id=(lax.rem(me_s + k, NS), me_d),
+                    device_id_type=MESH,
+                )
+            )
+        return copies
+
+    def dp_sum(copies, piece, got):
+        total = piece[me_d].astype(F32)
+        for k, copy in enumerate(copies):
+            copy.wait()
+            total = total + got[k + 1].astype(F32)
+        return total
+
+    def space_sum(copies, ref):
+        for copy in copies:
+            copy.wait()
+        total = ref[0].astype(F32)
+        for s in range(1, NS):
+            total = total + ref[s].astype(F32)
+        return total
+
+    @pl.when(t == 0)
+    def _():
+        barrier = pltpu.get_barrier_semaphore()
+        for k in range(1, NS):
+            pl.semaphore_signal(
+                barrier, inc=1, device_id=(lax.rem(me_s + k, NS), me_d), device_id_type=MESH
+            )
+        for k in range(1, ND):
+            pl.semaphore_signal(
+                barrier, inc=1, device_id=(me_s, lax.rem(me_d + k, ND)), device_id_type=MESH
+            )
+
     spread_taps(misc, wide_taps)
     for n in range(2):
         store_row(rows_in, n, above[0, n].astype(F32))
@@ -588,18 +657,57 @@
 
     lax.fori_loop(0, ROWS, conv, 0)
 
+    @pl.when(t == 0)
+    def _():
+        pl.semaphore_wait(pltpu.get_barrier_semaphore(), NS + ND - 2)
+        flat[:, CP:] = jnp.zeros((EARLY, 128), F32)
+        flat[0:C, 0:CP] = gproj[...]
+        for n in range(TILES):
+            flat[C:, 128 * n : 128 * (n + 1)] = gdepth[n]
+        for d in range(ND):
+            epiece[d] = flat[:, SLOT * d : SLOT * d + 128].astype(BF16)
+        mail[me_d] = msgs[me_d]
+        for copy in to_dp(epiece, egot, esend, erecv, False):
+            copy.start()
+        for copy in to_dp(msgs, mail, msend, mrecv, True):
+            copy.start()
+
+    @pl.when(t == TILES // 2)
+    def _():
+        total = dp_sum(to_dp(epiece, egot, esend, erecv, False), epiece, egot)
+        espace[me_s] = total.astype(BF16)
+        for copy in to_space(espace, fsend, frecv):
+            copy.start()
+
     @pl.when(t == TILES - 1)
     def _():
-        all_channels(dpre, we, cp, 0, fpt, out, gexp)
-
-
-def third(dd, above, below, fp, cp, fpt, we, misc):
+        early[...] = space_sum(to_space(espace, fsend, frecv), espace)
+        for copy in to_dp(msgs, mail, msend, mrecv, True):
+            copy.wait()
+        mail_out[...] = mail[...]
+        all_channels_grad(dpre, fpt, flat.at[0:C])
+        for d in range(ND):
+            lpiece[d] = flat[0:C, SLOT * d : SLOT * d + 128].astype(BF16)
+        copies = to_dp(lpiece, lgot, lsend, lrecv, False)
+        for copy in copies:
+            copy.start()
+        all_channels_out(dpre, we, cp, 0, out)
+        lspace[me_s] = dp_sum(copies, lpiece, lgot).astype(BF16)
+        copies = to_space(lspace, gsend, grecv)
+        for copy in copies:
+            copy.start()
+        late[...] = space_sum(copies, lspace)
+
+
+def third(dd, above, below, fp, cp, fpt, we, misc, gproj, gdepth, msgs):
     return pl.pallas_call(
         third_kernel,
         grid=(TILES,),
         out_shape=(
             jax.ShapeDtypeStruct((IMGS, ROWS, C, COLS), BF16),
-            jax.ShapeDtypeStruct((C, CP), F32),
+            jax.ShapeDtypeStruct((EARLY, 128), F32),
+            jax.ShapeDtypeStruct((C, 128), F32),
+            jax.ShapeDtypeStruct((ND, 8, 128), F32),
         ),
         in_specs=[
             tile_spec(ROWS, BLOCK, SUB, 128),
@@ -610,141 +718,37 @@
             whole_spec(C, ROWS * PIX),
             whole_spec(CP, C),
             pl.BlockSpec((32, 128), lambda t: (0, t)),
+            VMEM,
+            VMEM,
+            VMEM,
         ],
-        out_specs=(whole_spec(IMGS, ROWS, C, COLS), whole_spec(C, CP)),
+        out_specs=(whole_spec(IMGS, ROWS, C, COLS), VMEM, VMEM, VMEM),
         scratch_shapes=[
+            pltpu.VMEM((ND, 8, 128), F32),
             pltpu.VMEM((25, 8, 128), F32),
             pltpu.VMEM((HROWS, WIDE, SUB, 128), F32),
             pltpu.VMEM((ROWS * PIX, CP), BF16),
             pltpu.VMEM((ROWS, BLOCK, SUB, 128), F32),
-        ],
-        compiler_params=pltpu.CompilerParams(vmem_limit_bytes=56 * 2**20),
-        name="phase_c",
-    )(dd, above, below, fp, cp, fpt, we, misc)
-
-
-CHUNK = 48
-
-
-def reduce_kernel(
-    gexp, gproj, gdepth, msgs, final, mail, stack, packed, landed, part, pieces, got,
-    send, recv, dsend, drecv, fsend, frecv, msend, mrecv,
-):
-    me_s, me_d = lax.axis_index("space"), lax.axis_index("dp")
-    greet(range(1, NS), range(1, ND))
-    small = []
-    for k in range(1, ND):
-        target = lax.rem(me_d + k, ND)
-        copy = pltpu.make_async_remote_copy(
-            src_ref=msgs.at[target],
-            dst_ref=mail.at[me_d],
-            send_sem=msend.at[k],
-            recv_sem=mrecv.at[k],
-            device_id=(me_s, target),
-            device_id_type=MESH,
-        )
-        copy.start()
-        small.append(copy)
-    mail[me_d] = msgs[me_d]
-    stack[0:C, :] = gexp[...]
-    stack[C : 2 * C, :] = gproj[...]
-    for t in range(TILES):
-        stack[2 * C :, 128 * t : 128 * (t + 1)] = gdepth[t]
-    packed[...] = stack[...].reshape(NS, CHUNK, CP).astype(BF16)
-    copies = []
-    for k in range(1, NS):
-        target = lax.rem(me_s + k, NS)
-        copy = pltpu.make_async_remote_copy(
-            src_ref=packed.at[target],
-            dst_ref=landed.at[k],
-            send_sem=send.at[k],
-            recv_sem=recv.at[k],
-            device_id=(target, me_d),
-            device_id_type=MESH,
-        )
-        copy.start()
-        copies.append(copy)
-    start = pl.multiple_of(me_s * CHUNK, CHUNK)
-    part[:, 0:CP] = stack[pl.ds(start, CHUNK), :]
-    part[:, CP:] = jnp.zeros((CHUNK, 128), F32)
-    for k, copy in enumerate(copies):
-        copy.wait()
-        part[:, 0:CP] = part[:, 0:CP] + landed[k + 1].astype(F32)
-    for d in range(ND):
-        pieces[d] = part[:, SLOT * d : SLOT * d + 128].astype(BF16)
-    copies = []
-    for k in range(1, ND):
-        target = lax.rem(me_d + k, ND)
-        copy = pltpu.make_async_remote_copy(
-            src_ref=pieces.at[target],
-            dst_ref=got.at[k],
-            send_sem=dsend.at[k],
-            recv_sem=drecv.at[k],
-            device_id=(me_s, target),
-            device_id_type=MESH,
-        )
-        copy.start()
-        copies.append(copy)
-    total = pieces[me_d].astype(F32)
-    for k, copy in enumerate(copies):
-        copy.wait()
-        total = total + got[k + 1].astype(F32)
-    final[me_s] = total
-    copies = []
-    for k in range(1, NS):
-        copy = pltpu.make_async_remote_copy(
-            src_ref=final.at[me_s],
-            dst_ref=final.at[me_s],
-            send_sem=fsend.at[k],
-            recv_sem=frecv.at[k],
-            device_id=(lax.rem(me_s + k, NS), me_d),
-            device_id_type=MESH,
-        )
-        copy.start()
-        copies.append(copy)
-    for copy in copies:
-        copy.wait()
-    for copy in small:
-        copy.wait()
-
-
-def reduce_grads(gexp, gproj, gdepth, msgs):
-    return pl.pallas_call(
-        reduce_kernel,
-        out_shape=(
-            jax.ShapeDtypeStruct((NS, CHUNK, 128), F32),
-            jax.ShapeDtypeStruct((ND, 8, 128), F32),
-        ),
-        in_specs=[VMEM] * 4,
-        out_specs=(VMEM, VMEM),
-        scratch_shapes=[
-            pltpu.VMEM((NS * CHUNK, CP), F32),
-            pltpu.VMEM((NS, CHUNK, CP), BF16),
-            pltpu.VMEM((NS, CHUNK, CP), BF16),
-            pltpu.VMEM((CHUNK, CP + 128), F32),
-            pltpu.VMEM((ND, CHUNK, 128), BF16),
-            pltpu.VMEM((ND, CHUNK, 128), BF16),
-            pltpu.SemaphoreType.DMA((NS,)),
-            pltpu.SemaphoreType.DMA((NS,)),
-            pltpu.SemaphoreType.DMA((ND,)),
-            pltpu.SemaphoreType.DMA((ND,)),
-            pltpu.SemaphoreType.DMA((NS,)),
-            pltpu.SemaphoreType.DMA((NS,)),
-            pltpu.SemaphoreType.DMA((ND,)),
-            pltpu.SemaphoreType.DMA((ND,)),
-        ],
+            pltpu.VMEM((EARLY, CP + 128), F32),
+            pltpu.VMEM((ND, EARLY, 128), BF16),
+            pltpu.VMEM((ND, EARLY, 128), BF16),
+            pltpu.VMEM((NS, EARLY, 128), BF16),
+            pltpu.VMEM((ND, C, 128), BF16),
+            pltpu.VMEM((ND, C, 128), BF16),
+            pltpu.VMEM((NS, C, 128), BF16),
+        ]
+        + [pltpu.SemaphoreType.DMA((n,)) for n in (ND, ND, NS, NS, ND, ND, NS, NS, ND, ND)],
         compiler_params=pltpu.CompilerParams(
             collective_id=2, has_side_effects=True, vmem_limit_bytes=56 * 2**20
         ),
-        name="reduce_grads",
-    )(gexp, gproj, gdepth, msgs)
-
-
-def finish_kernel(final, mail, gexp, gdepth, greduce, gexcite, gbex, gproj, gbred):
-    grads = final[...].reshape(NS * CHUNK, 128)
-    gexp[...] = grads[0:C].T[0:PART]
-    gproj[...] = grads[C : 2 * C].T[0:PART]
-    gdepth[...] = grads[2 * C : 2 * C + 25, 0:PART]
+        name="phase_c",
+    )(dd, above, below, fp, cp, fpt, we, misc, gproj, gdepth, msgs)
+
+
+def finish_kernel(early, late, mail, gexp, gdepth, greduce, gexcite, gbex, gproj, gbred):
+    gexp[...] = late[...].T[0:PART]
+    gproj[...] = early[0:C].T[0:PART]
+    gdepth[...] = early[C : C + 25, 0:PART]
     rows = [mail[d] for d in range(ND)]
     pool_all = jnp.concatenate([row[0:2] for row in rows], axis=0)
     dlog_all = jnp.concatenate([row[2:4] for row in rows], axis=0)
@@ -756,7 +760,7 @@
     gbred[...] = jnp.sum(dsq_all, axis=0, keepdims=True)[:, 0:SE]
 
 
-def finish(final, mail):
+def finish(early, late, mail):
     return pl.pallas_call(
         finish_kernel,
         out_shape=(
@@ -768,10 +772,10 @@
             jax.ShapeDtypeStruct((PART, C), F32),
             jax.ShapeDtypeStruct((1, SE), F32),
         ),
-        in_specs=[VMEM] * 2,
+        in_specs=[VMEM] * 3,
         out_specs=(VMEM,) * 7,
         name="finish",
-    )(final, mail)
+    )(early, late, mail)
 
 
 def on_device(
@@ -793,9 +797,12 @@
     above = lax.ppermute(lower, "space", [(i, i + 1) for i in range(NS - 1)])
     below = lax.ppermute(upper, "space", [(i + 1, i) for i in range(NS - 1)])
     gdepth = tap_grads(ex, dd)
-    grad_features, gexp = third(dd, above, below, fp, cp, fpt, we, misc)
-    final, mail = reduce_grads(gexp, gproj, gdepth, msgs)
-    s_expand, s_depth, s_reduce, s_excite, s_bexcite, s_project, s_breduce = finish(final, mail)
+    grad_features, early, late, mail = third(
+        dd, above, below, fp, cp, fpt, we, misc, gproj, gdepth, msgs
+    )
+    s_expand, s_depth, s_reduce, s_excite, s_bexcite, s_project, s_breduce = finish(
+        early, late, mail
+    )
     return (
         output.swapaxes(2, 3),
         grad_features.swapaxes(2, 3),

time: 210 us -> 200 us (0.952)
  Pallas kernels: 200 us -> 188 us
  local copies, waits for them, and re-layouts: 3.93 us -> 6.17 us
    pallas_call x1 -> x0, Pallas kernels: 29.5 us -> none  [reduce_grads(): pl.pallas_call(reduce_kernel, out_shape=(jax.ShapeDtypeStruct((NS, CHUNK,...]
    pallas_call x1, Pallas kernels: 43.6 us -> 61.2 us  [third(): pl.pallas_call(third_kernel, grid=(TILES,), out_shape=(jax.ShapeDtypeStru...]
    unnamed x4 -> x5, local copies, waits for them, and re-layouts: 1.28 us -> 3.52 us
where the time goes in v4:
time: 200 us
  Pallas kernels  188 us (94%)
  local copies, waits for them, and re-layouts  6.17 us (3%)
  starting transfers between devices  4.38 us (2%)
    pallas_call x1, Pallas kernels, third(): pl.pallas_call(third_kernel, grid=(TILES,), out_shape=(jax.ShapeDtypeStru...  61.2 us
    pallas_call x1, Pallas kernels, first(): pl.pallas_call(first_kernel, grid=(TILES,), out_shape=(jax.ShapeDtypeStru...  44.1 us
    pallas_call x1, Pallas kernels, tap_grads(): pl.pallas_call(tap_kernel, grid=(TILES,), out_shape=jax.ShapeDtypeStruct(...  24.7 us
    pallas_call x1, Pallas kernels, second(): pl.pallas_call(second_kernel, grid=(TILES,), out_shape=(jax.ShapeDtypeStr...  23 us
    pallas_call x1, Pallas kernels, gather(): pl.pallas_call(gather_kernel, out_shape=(jax.ShapeDtypeStruct((HROWS, PIX...  22.7 us
    pallas_call x1, Pallas kernels, mid(): pl.pallas_call(mid_kernel, out_shape=(jax.ShapeDtypeStruct((8, CP), F32),...  10.9 us
  transfers between devices with their start and end apart: 2, of which 0 were waited for; matrix products, arithmetic and copies ran while one was open for 0% of the time, Pallas kernels for 12%

profile of v4, /device:TPU:1, one launch (start us, length us, event | category | flops | bytes accessed | tf_op | source)
XLA Modules:
  0.0 199.6 jit_solution(8464275527615348777)
XLA Ops:
  0.6 1.3 reshape.24.taps
  2.0 22.7 %gather_weights.1 = (bf16[16,208,176]{2,1,0:T(8,128)(2,1)}, bf16[12,208,176]{2,1,0:T(8,128)(2,1)}, bf16[176,2496]{1,0:T(8,128)(2,1)}, bf16[176,2496]{1,0:T(8,128...) custom-call(bf16[66,176]{1,0:T(8,128)(2,1)} %bitcast.15, bf16[66,176]{1,0:T(8,128)(2,1)} %wpr.1, ...), custom_call_target="tpu_custom_call" | custom-call | tf_op jit(solution)/shard_map/gather_weights/pallas_call | solution.py:191
  24.7 44.1 %phase_a.1 = (bf16[9,16,17,16,128]{4,3,2,1,0:T(8,128)(2,1)}, f32[9,12,13,16,128]{4,3,2,1,0:T(8,128)}, f32[9,8,128]{2,1,0:T(8,128)}) custom-call(bf16[16,208,176]{2,1,0:T(8,128)(2,1)} %get-tuple-element.37.fp, bf16[12,208,176]{2,1,0:T(8,128)(2,1)} %get-tuple-element.38.cp, bf16[1152,176]{1,0:T(8,128)(2,1)} %get-tuple-element.39.we, ...), custom_call_target="tpu_custom_call" | custom-call | tf_op jit(solution)/shard_map/phase_a/pallas_call | solution.py:315
  68.8 10.9 %squeeze_excite.1 = (f32[8,1152]{1,0:T(8,128)}, f32[16,8,128]{2,1,0:T(8,128)}) custom-call(f32[9,8,128]{2,1,0:T(8,128)} %get-tuple-element.44.sums, f32[136,1152]{1,0:T(8,128)} %get-tuple-element.41.misc, bf16[1,44]{1,0:T(2,128)(2,1)} %bitcast.18), custom_call_target="tpu_custom_call" | custom-call | tf_op jit(solution)/shard_map/squeeze_excite/pallas_call | solution.py:397
  79.7 23.0 %phase_b.1 = (bf16[9,12,13,16,128]{4,3,2,1,0:T(8,128)(2,1)}, bf16[9,2,13,16,128]{4,3,2,1,0:T(8,128)(2,1)}, bf16[9,2,13,16,128]{4,3,2,1,0:T(8,128)(2,1)}, bf16[2,12,176,100]{3,2,1,0:T(8,128)(2,1)}, f32[176,1152]{1,0:T(8,128)}) custom-call(f32[9,12,13,16,128]{4,3,2,1,0:T(8,128)} %get-tuple-element.42.depth, bf16[16,208,176]{2,1,0:T(8,128)(2,1)} %get-tuple-element.37.fp, ...), custom_call_target="tpu_custom_call" | custom-call | tf_op jit(solution)/shard_map/phase_b/pallas_call | solution.py:489
  102.7 1.9 collective-permute-start
  104.6 2.5 %collective-permute-start.1 = (bf16[9,2,13,16,128]{4,3,2,1,0:T(8,128)(2,1)}, bf16[9,2,13,16,128]{4,3,2,1,0:T(8,128)(2,1)S(1)}, u32[]{:S(2)}, u32[]{:S(2)}) collective-permute-start(bf16[9,2,13,16,128]{4,3,2,1,0:T(8,128)(2,1)} %get-tuple-element.49), channel_id=1, source_target_pairs={{16,0},{32,16},{48,32},{64,48},{80,64},{96,80},{112,96},{17,1},{33... | collective-permute-start | bytes 2875400 | tf_op jit(solution)/shard_map/ppermute | solution.py:798
  107.1 24.7 %tap_grads.1.gdepth = f32[9,32,128]{2,1,0:T(8,128)} custom-call(bf16[9,16,17,16,128]{4,3,2,1,0:T(8,128)(2,1)} %get-tuple-element.52.ex, bf16[9,12,13,16,128]{4,3,2,1,0:T(8,128)(2,1)} %get-tuple-element.47.dd), custom_call_target="tpu_custom_call" | custom-call | flops 4000000000 | bytes 50000000 | tf_op jit(solution)/shard_map/tap_grads/pallas_call | solution.py:544
  131.7 0.0 collective-permute-done.above
  131.7 0.0 copy-start
  131.7 0.0 collective-permute-done.1.below
  131.8 0.0 copy-start.1
  131.8 1.0 copy-done
  132.7 0.3 copy-done.1
  133.0 61.2 %phase_c.1 = (bf16[2,12,176,100]{3,2,1,0:T(8,128)(2,1)}, f32[208,128]{1,0:T(8,128)}, f32[176,128]{1,0:T(8,128)}, f32[16,8,128]{2,1,0:T(8,128)}) custom-call(bf16[9,12,13,16,128]{4,3,2,1,0:T(8,128)(2,1)} %get-tuple-element.47.dd, bf16[9,2,13,16,128]{4,3,2,1,0:T(8,128)(2,1)} %copy-done, bf16[9,2,13,16,128]{4,3,2,1,0:T(8,128)(2,1)} %copy-done.1, ...), custom_call_target="tpu_custom_call" | custom-call | tf_op jit(solution)/shard_map/phase_c/pallas_call | solution.py:703
  194.2 1.9 finish.1
  196.0 1.3 reshape.25
  197.4 2.3 %copy.19 = bf16[2,12,100,176]{2,3,1,0:T(8,128)(2,1)} copy(bf16[2,12,100,176]{2,3,1,0:T(8,128)(2,1)} %bitcast.14) | data formatting | bytes 1689600
Async XLA Ops:
  102.7 29.1 %collective-permute-start = (bf16[9,2,13,16,128]{4,3,2,1,0:T(8,128)(2,1)}, bf16[9,2,13,16,128]{4,3,2,1,0:T(8,128)(2,1)S(1)}, u32[]{:S(2)}, u32[]{:S(2)}) collective-permute-start(bf16[9,2,13,16,128]{4,3,2,1,0:T(8,128)(2,1)} %get-tuple-element.48), channel_id=1, source_target_pairs={{0,16},{16,32},{32,48},{48,64},{64,80},{80,96},{96,112},{1,17},{17... | collective-permute-start | bytes 2875400 | tf_op jit(solution)/shard_map/ppermute | solution.py:797
  104.6 27.1 %collective-permute-start.1 = (bf16[9,2,13,16,128]{4,3,2,1,0:T(8,128)(2,1)}, bf16[9,2,13,16,128]{4,3,2,1,0:T(8,128)(2,1)S(1)}, u32[]{:S(2)}, u32[]{:S(2)}) collective-permute-start(bf16[9,2,13,16,128]{4,3,2,1,0:T(8,128)(2,1)} %get-tuple-element.49), channel_id=1, source_target_pairs={{16,0},{32,16},{48,32},{64,48},{80,64},{96,80},{112,96},{17,1},{33... | collective-permute-start | bytes 2875400 | tf_op jit(solution)/shard_map/ppermute | solution.py:798
  131.7 1.0 copy-start
  131.8 1.2 copy-start.1

commit v5 on v0

v5 whole, which is shorter than its diff:
```python
import functools

import jax
import jax.numpy as jnp
from jax import lax
from jax.experimental import pallas as pl
from jax.experimental.pallas import tpu as pltpu
from jax.sharding import PartitionSpec as P

F32 = jnp.float32
BF16 = jnp.bfloat16
MESH = pl.DeviceIdType.MESH
HIGH = lax.Precision.HIGHEST

IMGS, ROWS, COLS, C, SE = 2, 12, 100, 176, 44
BLOCK, SUB = 13, 16
PIX = BLOCK * SUB
WIDE = BLOCK + 4
HROWS = ROWS + 4
PART, SLOT = 66, 72
CP = 16 * SLOT
TILES = CP // 128
AREA = 9600.0
NS, ND = 8, 16

VMEM = pl.BlockSpec(memory_space=pltpu.VMEM)
ANY = pl.BlockSpec(memory_space=pl.ANY)


def sigmoid(value):
    return 0.5 * jnp.tanh(0.5 * value) + 0.5


def swish(value):
    return value * sigmoid(value)


def swish_grad(value):
    sig = sigmoid(value)
    act = value * sig
    return sig + act - act * sig


def dot_nt(left, right, precision=None):
    return lax.dot_general(
        left, right, (((1,), (1,)), ((), ())), precision=precision, preferred_element_type=F32
    )


def dot_tn(left, right, precision=None):
    return lax.dot_general(
        left, right, (((0,), (0,)), ((), ())), precision=precision, preferred_element_type=F32
    )


def dot_nn(left, right, precision=None):
    return lax.dot_general(
        left, right, (((1,), (0,)), ((), ())), precision=precision, preferred_element_type=F32
    )


def one_hot(img, transposed):
    shape = (COLS, PIX) if transposed else (PIX, COLS)
    place = lax.broadcasted_iota(jnp.int32, shape, 1 if transposed else 0)
    col = lax.broadcasted_iota(jnp.int32, shape, 0 if transposed else 1)
    wanted = (col % BLOCK) * SUB + img * 8 + col // BLOCK
    return jnp.where(place == wanted, 1.0, 0.0).astype(BF16)


def spread_taps(taps, wide_taps):
    for k in range(25):
        wide_taps[k] = jnp.broadcast_to(taps[k : k + 1, :], (8, 128))


def edge_columns(value):
    split = value.reshape(BLOCK, 2, 8, 128)
    block = lax.broadcasted_iota(jnp.int32, (2, 2, 8, 128), 2)
    left = jnp.where(block > 0, pltpu.roll(split[BLOCK - 2 :], 1, 2), 0.0)
    right = jnp.where(block < 7, pltpu.roll(split[:2], 7, 2), 0.0)
    return left.reshape(2, SUB, 128), right.reshape(2, SUB, 128)


def store_row(ref, r, value):
    left, right = edge_columns(value)
    ref[r, 0:2] = left
    ref[r, 2 : 2 + BLOCK] = value
    ref[r, 2 + BLOCK :] = right


def conv_row(ref, r, h, wide_taps, flip):
    total = jnp.zeros((BLOCK, 8, 128), F32)
    for i in range(5):
        source = ref[r + i, :, 8 * h : 8 * h + 8, :]
        for j in range(5):
            k = (4 - i) * 5 + 4 - j if flip else i * 5 + j
            total = total + source[j : j + BLOCK] * wide_taps[k][None]
    return total


def pad_mask():
    block = lax.broadcasted_iota(jnp.int32, (4, 8, 128), 1)
    return jnp.where(block < 7, 1.0, 0.0)


def gate_row(depth, dgated, gates, h, keep):
    gate = gates[h : h + 1, :][None]
    pull = gates[2 + h : 3 + h, :][None]
    sig = sigmoid(depth)
    act = depth * sig
    gated = act * gate
    ddepth = (dgated * gate + pull) * (sig + act - act * sig)
    ddepth = jnp.concatenate([ddepth[:9], ddepth[9:] * keep], axis=0)
    return gated, ddepth


def unpermute(value, out, r):
    for img in range(2):
        out[img, r] = dot_tn(value, one_hot(img, False)).astype(BF16)


def all_channels_out(rows_in, weights, base, shift, out):
    def chunk(q, carry):
        block = rows_in[pl.ds(pl.multiple_of(4 * PIX * q, 4 * PIX), 4 * PIX), :]
        product = dot_nn(block, weights[...]).reshape(4, PIX, C)
        for n in range(4):
            value = product[n] + base[4 * q + n + shift].astype(F32)
            unpermute(value.astype(BF16), out, 4 * q + n)
        return carry

    lax.fori_loop(0, 3, chunk, 0)


def all_channels_grad(rows_in, turned, grad):
    def lanes(q, carry):
        span = pl.ds(pl.multiple_of(384 * q, 128), 384)
        grad[:, span] = dot_nn(turned[...], rows_in[:, span])
        return carry

    lax.fori_loop(0, 3, lanes, 0)


def to_dp(src, dst, send, recv, by_sender=False):
    me_s, me_d = lax.axis_index("space"), lax.axis_index("dp")
    copies = []
    for k in range(1, ND):
        target = lax.rem(me_d + k, ND)
        copies.append(
            pltpu.make_async_remote_copy(
                src_ref=src.at[target],
                dst_ref=dst.at[me_d] if by_sender else dst.at[k],
                send_sem=send.at[k],
                recv_sem=recv.at[k],
                device_id=(me_s, target),
                device_id_type=MESH,
            )
        )
    return copies


def to_space(ref, send, recv):
    me_s, me_d = lax.axis_index("space"), lax.axis_index("dp")
    copies = []
    for k in range(1, NS):
        copies.append(
            pltpu.make_async_remote_copy(
                src_ref=ref.at[me_s],
                dst_ref=ref.at[me_s],
                send_sem=send.at[k],
                recv_sem=recv.at[k],
                device_id=(lax.rem(me_s + k, NS), me_d),
                device_id_type=MESH,
            )
        )
    return copies


def to_neighbours(down_src, down_dst, up_src, up_dst, send, recv):
    me_s, me_d = lax.axis_index("space"), lax.axis_index("dp")
    down = pltpu.make_async_remote_copy(
        src_ref=down_src,
        dst_ref=down_dst,
        send_sem=send[0],
        recv_sem=recv[0],
        device_id=(lax.rem(me_s + 1, NS), me_d),
        device_id_type=MESH,
    )
    up = pltpu.make_async_remote_copy(
        src_ref=up_src,
        dst_ref=up_dst,
        send_sem=send[1],
        recv_sem=recv[1],
        device_id=(lax.rem(me_s + NS - 1, NS), me_d),
        device_id_type=MESH,
    )
    return down, up


def dp_sum(copies, piece, got):
    total = piece[lax.axis_index("dp")].astype(F32)
    for k, copy in enumerate(copies):
        copy.wait()
        total = total + got[k + 1].astype(F32)
    return total


def space_sum(copies, ref):
    for copy in copies:
        copy.wait()
    total = ref[0].astype(F32)
    for s in range(1, NS):
        total = total + ref[s].astype(F32)
    return total


EARLY = C + 32


def block_kernel(
    wet, wpr, taps, wrt, wx_own, bex, bred, feats, cot,
    out, out_grad, early, late, mail_out,
    stage, pack, full, top, bottom, flatw, fp, cp, fpt, cpt, we, wp, misc,
    wide_taps, ex, dgs, saved, depth, sums, packed, landed, lanes, vecs, gates, msgs, mail,
    edge, above, below, gated, dpre, acc, flat, epiece, egot, espace, lpiece, lgot, lspace,
    wsend, wrecv, hsend, hrecv, csend, crecv, ssend, srecv, msend, mrecv,
    dsend, drecv, esend, erecv, fsend, frecv, lsend, lrecv, gsend, grecv,
):
    me_s, me_d = lax.axis_index("space"), lax.axis_index("dp")
    core = lax.rem(me_s, 2)
    barrier = pltpu.get_barrier_semaphore()
    for k in range(1, ND):
        pl.semaphore_signal(
            barrier, inc=1, device_id=(me_s, lax.rem(me_d + k, ND)), device_id_type=MESH
        )
    for k in range(1, NS):
        pl.semaphore_signal(
            barrier, inc=1, device_id=(lax.rem(me_s + k, NS), me_d), device_id_type=MESH
        )

    stage[...] = jnp.zeros_like(stage)
    stage[0, 0:PART, 0:C] = wet[...].astype(F32)
    stage[1, 0:PART, 0:C] = wpr[...].astype(F32)
    side = slice(C, C + PART)
    stage[0, 0:25, side] = taps[...].astype(F32)
    stage[0, 32 : 32 + SE, side] = wrt[...].astype(F32)
    stage[1, 0:SE, side] = wx_own[...].astype(F32)
    stage[1, 48:49, side] = bex[...].astype(F32)
    pack[...] = stage[...].astype(BF16)
    pl.semaphore_wait(barrier, NS + ND - 2)
    copies = []
    for k in range(1, ND):
        copy = pltpu.make_async_remote_copy(
            src_ref=pack.at[core],
            dst_ref=full.at[core, me_d],
            send_sem=wsend.at[k],
            recv_sem=wrecv.at[k],
            device_id=(me_s, lax.rem(me_d + k, ND)),
            device_id_type=MESH,
        )
        copy.start()
        copies.append(copy)
    halo = to_neighbours(
        feats.at[:, pl.ds(ROWS - 2, 2)],
        top,
        feats.at[:, pl.ds(0, 2)],
        bottom,
        (hsend.at[0], hsend.at[1]),
        (hrecv.at[0], hrecv.at[1]),
    )
    for copy in halo:
        copy.start()
    full[core, me_d] = pack[core]
    spread = (one_hot(0, False), one_hot(1, False))
    gather_t = (one_hot(0, True), one_hot(1, True))

    def permute(r, carry):
        for src, dst, shift in ((feats, fp, 2), (cot, cp, 0)):
            a, b = src[0, r], src[1, r]
            dst[r + shift] = (dot_nt(spread[0], a) + dot_nt(spread[1], b)).astype(BF16)
        return carry

    lax.fori_loop(0, ROWS, permute, 0)
    for r in range(ROWS):
        for src, dst in ((feats, fpt), (cot, cpt)):
            value = dot_nn(src[0, r], gather_t[0]) + dot_nn(src[1, r], gather_t[1])
            dst[:, PIX * r : PIX * (r + 1)] = value.astype(BF16)
    for copy in copies:
        copy.wait()
    share = pltpu.make_async_remote_copy(
        src_ref=full.at[core],
        dst_ref=full.at[core],
        send_sem=csend,
        recv_sem=crecv,
        device_id=(me_s + 1 - 2 * core, me_d),
        device_id_type=MESH,
    )
    share.start()
    for copy in halo:
        copy.wait()
    has_top = jnp.where(me_s > 0, 1.0, 0.0)
    has_bottom = jnp.where(me_s < NS - 1, 1.0, 0.0)
    for r in range(2):
        value = dot_nt(spread[0], top[0, r]) + dot_nt(spread[1], top[1, r])
        fp[r] = (value * has_top).astype(BF16)
        value = dot_nt(spread[0], bottom[0, r]) + dot_nt(spread[1], bottom[1, r])
        fp[ROWS + 2 + r] = (value * has_bottom).astype(BF16)
    share.wait()
    for half, whole in ((0, we), (1, wp)):
        for d in range(ND):
            part = full[half, d].astype(F32)
            flatw[d * SLOT : (d + 1) * SLOT, :] = part[0:SLOT, 0:C]
            span = slice(d * SLOT, (d + 1) * SLOT)
            if half == 0:
                misc[0:80, span] = part[:, C : C + SLOT]
            else:
                misc[80:136, span] = part[0:56, C : C + SLOT]
        whole[...] = flatw[...].astype(BF16)

    keep = pad_mask()

    def lane_of(t):
        return pl.ds(pl.multiple_of(128 * t, 128), 128)

    def cot_matmul(t):
        def chunk(q, carry):
            rows = pl.ds(6 * q, 6)
            product = dot_nt(cp[rows].reshape(6 * PIX, C), wp[lane_of(t), :])
            dgs[rows] = product.reshape(6, BLOCK, SUB, 128)
            return carry

        lax.fori_loop(0, 2, chunk, 0)

    def first(t, carry):
        spread_taps(misc[0:32, lane_of(t)], wide_taps)

        def expand(q, carry):
            pre = dot_nt(fp[pl.ds(8 * q, 8)].reshape(8 * PIX, C), we[lane_of(t), :])
            value = swish(pre).astype(BF16).astype(F32).reshape(8, BLOCK, SUB, 128)
            for n in range(8):
                store_row(ex, 8 * q + n, value[n])
            return carry

        lax.fori_loop(0, 2, expand, 0)
        cot_matmul(t)

        def conv(r, carry):
            pools, grads = list(carry[:2]), list(carry[2:])
            for h in range(2):
                total = conv_row(ex, r, h, wide_taps, False)
                depth[t, r, :, 8 * h : 8 * h + 8, :] = total
                act = swish(total)
                dgated = dgs[r, :, 8 * h : 8 * h + 8, :]
                grads[h] = grads[h] + jnp.sum(act * dgated, axis=0)
                pools[h] = pools[h] + jnp.sum(act[:9], axis=0) + jnp.sum(act[9:] * keep, axis=0)
            saved[t, r] = ex[r].astype(BF16)
            return (*pools, *grads)

        zero = jnp.zeros((8, 128), F32)
        parts = lax.fori_loop(0, ROWS, conv, (zero,) * 4)
        for r in range(ROWS, HROWS):
            saved[t, r] = ex[r].astype(BF16)
        for k in range(4):
            sums[t, k : k + 1, :] = jnp.sum(parts[k], axis=0, keepdims=True)
        return carry

    lax.fori_loop(0, TILES, first, 0)

    packed[...] = jnp.zeros_like(packed)
    for t in range(TILES):
        packed[t // 2, 4 * (t % 2) : 4 * (t % 2) + 4, :] = sums[t, 0:4, :]
    landed[me_s] = packed[...]
    copies = to_space(landed, ssend, srecv)
    for copy in copies:
        copy.start()
    total = space_sum(copies, landed)
    for t in range(TILES):
        lanes[0:4, 128 * t : 128 * (t + 1)] = total[t // 2, 4 * (t % 2) : 4 * (t % 2) + 4]
    lanes[:, CP:] = jnp.zeros((8, 128), F32)
    wr = misc[32 : 32 + SE, :]
    wx = misc[80 : 80 + SE, :]
    pooled = lanes[0:2, 0:CP] / AREA
    dgate = lanes[2:4, 0:CP]
    squeeze_pre = dot_nt(pooled, wr, HIGH) + bred[...].astype(F32)
    squeeze = swish(squeeze_pre)
    gate = sigmoid(dot_nn(squeeze, wx, HIGH) + misc[128:129, :])
    dlogit = dgate * gate * (1.0 - gate)
    dsq = dot_nt(dlogit, wx, HIGH) * swish_grad(squeeze_pre)
    dpooled = dot_nn(dsq, wr, HIGH)
    gates[0:2, :] = gate
    gates[2:4, :] = dpooled / AREA
    gates[4:8, :] = jnp.zeros((4, CP), F32)
    lanes[0:2, 0:CP] = pooled
    lanes[2:4, 0:CP] = dlogit
    vecs[...] = jnp.zeros((8, 128), F32)
    vecs[4:6, 0:SE] = squeeze
    vecs[6:8, 0:SE] = dsq
    for d in range(ND):
        msgs[d, 0:4, :] = lanes[0:4, SLOT * d : SLOT * d + 128]
        msgs[d, 4:8, :] = vecs[4:8, :]
    mail[me_d] = msgs[me_d]
    small = to_dp(msgs, mail, msend, mrecv, True)
    for copy in small:
        copy.start()

    def edge_copies(t):
        return to_neighbours(
            edge.at[t, 1],
            above.at[t],
            edge.at[t, 0],
            below.at[t],
            (dsend.at[0, t], dsend.at[1, t]),
            (drecv.at[0, t], drecv.at[1, t]),
        )

    def second(t, carry):
        cot_matmul(t)

        def pointwise(r, carry):
            both = []
            for h in range(2):
                rows = slice(8 * h, 8 * h + 8)
                value, ddepth = gate_row(
                    depth[t, r, :, rows, :], dgs[r, :, rows, :], gates.at[:, lane_of(t)], h, keep
                )
                depth[t, r, :, rows, :] = ddepth.astype(BF16).astype(F32)
                both.append(value)
            gated[pl.ds(pl.multiple_of(r * PIX, PIX), PIX), lane_of(t)] = (
                jnp.concatenate(both, axis=1).reshape(PIX, 128).astype(BF16)
            )
            return carry

        lax.fori_loop(0, ROWS, pointwise, 0)
        for n in range(2):
            edge[t, 0, n] = depth[t, n].astype(BF16)
            edge[t, 1, n] = depth[t, ROWS - 2 + n].astype(BF16)
        for copy in edge_copies(t):
            copy.start()
        return carry

    lax.fori_loop(0, TILES, second, 0)

    def tap_grads(t, carry):
        acc[...] = jnp.zeros_like(acc)

        def row(r, carry):
            for h in range(2):
                rows = slice(8 * h, 8 * h + 8)
                mine = depth[t, r, :, rows, :]
                for i in range(5):
                    source = saved[t, r + i].astype(F32)[:, rows, :]
                    for j in range(5):
                        k = 5 * i + j
                        acc[k] = acc[k] + jnp.sum(mine * source[j : j + BLOCK], axis=0)
            return carry

        lax.fori_loop(0, ROWS, row, 0)
        for k in range(25):
            flat[C + k : C + k + 1, lane_of(t)] = jnp.sum(acc[k], axis=0, keepdims=True)
        return carry

    flat[...] = jnp.zeros_like(flat)
    lax.fori_loop(0, TILES, tap_grads, 0)
    all_channels_grad(gated, cpt, flat.at[0:C])
    for d in range(ND):
        epiece[d] = flat[:, SLOT * d : SLOT * d + 128].astype(BF16)
    for copy in to_dp(epiece, egot, esend, erecv):
        copy.start()

    def third(t, carry):
        spread_taps(misc[0:32, lane_of(t)], wide_taps)

        def middle(r, carry):
            store_row(ex, r + 2, depth[t, r])
            return carry

        lax.fori_loop(0, ROWS, middle, 0)

        def chunk(q, carry):
            pre = dot_nt(fp[pl.ds(6 * q + 2, 6)].reshape(6 * PIX, C), we[lane_of(t), :])
            dgs[pl.ds(6 * q, 6)] = swish_grad(pre).reshape(6, BLOCK, SUB, 128)
            return carry

        lax.fori_loop(0, 2, chunk, 0)
        for copy in edge_copies(t):
            copy.wait()
        for n in range(2):
            store_row(ex, n, above[t, n].astype(F32) * has_top)
            store_row(ex, ROWS + 2 + n, below[t, n].astype(F32) * has_bottom)

        def conv(r, carry):
            both = []
            for h in range(2):
                slope = dgs[r, :, 8 * h : 8 * h + 8, :]
                both.append(conv_row(ex, r, h, wide_taps, True) * slope)
            dpre[pl.ds(pl.multiple_of(r * PIX, PIX), PIX), lane_of(t)] = (
                jnp.concatenate(both, axis=1).reshape(PIX, 128).astype(BF16)
            )
            return carry

        lax.fori_loop(0, ROWS, conv, 0)

        @pl.when(t == TILES // 2)
        def _():
            total = dp_sum(to_dp(epiece, egot, esend, erecv), epiece, egot)
            espace[me_s] = total.astype(BF16)
            for copy in to_space(espace, fsend, frecv):
                copy.start()

        return carry

    lax.fori_loop(0, TILES, third, 0)

    all_channels_grad(dpre, fpt, flat.at[0:C])
    for d in range(ND):
        lpiece[d] = flat[0:C, SLOT * d : SLOT * d + 128].astype(BF16)
    copies = to_dp(lpiece, lgot, lsend, lrecv)
    for copy in copies:
        copy.start()
    all_channels_out(dpre, we, cp, 0, out_grad)
    early[...] = space_sum(to_space(espace, fsend, frecv), espace)
    for copy in small:
        copy.wait()
    mail_out[...] = mail[...]
    lspace[me_s] = dp_sum(copies, lpiece, lgot).astype(BF16)
    copies = to_space(lspace, gsend, grecv)
    for copy in copies:
        copy.start()
    all_channels_out(gated, wp, fp, 2, out)
    late[...] = space_sum(copies, lspace)


def block(*args):
    def bf16(*shape):
        return pltpu.VMEM(shape, BF16)

    def f32(*shape):
        return pltpu.VMEM(shape, F32)

    def sems(*shape):
        return pltpu.SemaphoreType.DMA(shape)

    one = pltpu.SemaphoreType.DMA
    return pl.pallas_call(
        block_kernel,
        out_shape=(
            jax.ShapeDtypeStruct((IMGS, ROWS, C, COLS), BF16),
            jax.ShapeDtypeStruct((IMGS, ROWS, C, COLS), BF16),
            jax.ShapeDtypeStruct((EARLY, 128), F32),
            jax.ShapeDtypeStruct((C, 128), F32),
            jax.ShapeDtypeStruct((ND, 8, 128), F32),
        ),
        in_specs=[VMEM] * 9,
        out_specs=(VMEM,) * 5,
        scratch_shapes=[
            f32(2, 80, 256),
            bf16(2, 80, 256),
            bf16(2, ND, 80, 256),
            bf16(IMGS, 2, C, COLS),
            bf16(IMGS, 2, C, COLS),
            f32(CP, C),
            bf16(HROWS, PIX, C),
            bf16(ROWS, PIX, C),
            bf16(C, ROWS * PIX),
            bf16(C, ROWS * PIX),
            bf16(CP, C),
            bf16(CP, C),
            f32(136, CP),
            f32(25, 8, 128),
            f32(HROWS, WIDE, SUB, 128),
            f32(ROWS, BLOCK, SUB, 128),
            bf16(TILES, HROWS, WIDE, SUB, 128),
            f32(TILES, ROWS, BLOCK, SUB, 128),
            f32(TILES, 8, 128),
            f32(5, 8, 128),
            f32(NS, 5, 8, 128),
            f32(8, CP + 128),
            f32(8, 128),
            f32(8, CP),
            f32(ND, 8, 128),
            f32(ND, 8, 128),
            bf16(TILES, 2, 2, BLOCK, SUB, 128),
            bf16(TILES, 2, BLOCK, SUB, 128),
            bf16(TILES, 2, BLOCK, SUB, 128),
            bf16(ROWS * PIX, CP),
            bf16(ROWS * PIX, CP),
            f32(25, 8, 128),
            f32(EARLY, CP + 128),
            bf16(ND, EARLY, 128),
            bf16(ND, EARLY, 128),
            bf16(NS, EARLY, 128),
            bf16(ND, C, 128),
            bf16(ND, C, 128),
            bf16(NS, C, 128),
            sems(ND),
            sems(ND),
            sems(2),
            sems(2),
            one,
            one,
            sems(NS),
            sems(NS),
            sems(ND),
            sems(ND),
            sems(2, TILES),
            sems(2, TILES),
            sems(ND),
            sems(ND),
            sems(NS),
            sems(NS),
            sems(ND),
            sems(ND),
            sems(NS),
            sems(NS),
        ],
        compiler_params=pltpu.CompilerParams(
            collective_id=0, has_side_effects=True, vmem_limit_bytes=63 * 2**20
        ),
        name="block",
    )(*args)


def finish_kernel(
    early, late, mail, raw, raw_grad,
    gexp, gdepth, greduce, gexcite, gbex, gproj, gbred, out, out_grad, sem,
):
    moves = [
        pltpu.make_async_copy(raw, out, sem.at[0]),
        pltpu.make_async_copy(raw_grad, out_grad, sem.at[1]),
    ]
    for move in moves:
        move.start()
    gexp[...] = late[...].T[0:PART]
    gproj[...] = early[0:C].T[0:PART]
    gdepth[...] = early[C : C + 25, 0:PART]
    rows = [mail[d] for d in range(ND)]
    pool_all = jnp.concatenate([row[0:2] for row in rows], axis=0)
    dlog_all = jnp.concatenate([row[2:4] for row in rows], axis=0)
    sq_all = jnp.concatenate([row[4:6] for row in rows], axis=0)
    dsq_all = jnp.concatenate([row[6:8] for row in rows], axis=0)
    greduce[...] = dot_tn(dsq_all, pool_all, HIGH)[0:SE, 0:PART]
    gexcite[...] = dot_tn(sq_all, dlog_all, HIGH)[0:SE, 0:PART]
    gbex[...] = jnp.sum(dlog_all, axis=0, keepdims=True)[:, 0:PART]
    gbred[...] = jnp.sum(dsq_all, axis=0, keepdims=True)[:, 0:SE]
    for move in moves:
        move.wait()


def finish(early, late, mail, raw, raw_grad):
    return pl.pallas_call(
        finish_kernel,
        out_shape=(
            jax.ShapeDtypeStruct((PART, C), F32),
            jax.ShapeDtypeStruct((25, PART), F32),
            jax.ShapeDtypeStruct((SE, PART), F32),
            jax.ShapeDtypeStruct((SE, PART), F32),
            jax.ShapeDtypeStruct((1, PART), F32),
            jax.ShapeDtypeStruct((PART, C), F32),
            jax.ShapeDtypeStruct((1, SE), F32),
            jax.ShapeDtypeStruct((IMGS, ROWS, C, COLS), BF16),
            jax.ShapeDtypeStruct((IMGS, ROWS, C, COLS), BF16),
        ),
        in_specs=[VMEM, VMEM, VMEM, ANY, ANY],
        out_specs=(VMEM,) * 7 + (ANY, ANY),
        scratch_shapes=[pltpu.SemaphoreType.DMA((2,))],
        name="finish",
    )(early, late, mail, raw, raw_grad)


def on_device(
    features, w_expand, w_depth, w_reduce, b_reduce, w_excite, b_excite, w_project, cotangent
):
    raw, raw_grad, early, late, mail = block(
        w_expand.T,
        w_project,
        w_depth.reshape(25, PART),
        w_reduce.T,
        w_excite,
        b_excite[None, :],
        b_reduce[None, :],
        features.swapaxes(2, 3),
        cotangent.swapaxes(2, 3),
    )
    (
        s_expand, s_depth, s_reduce, s_excite, s_bexcite, s_project, s_breduce, output, grad,
    ) = finish(early, late, mail, raw, raw_grad)
    return (
        output.swapaxes(2, 3),
        grad.swapaxes(2, 3),
        s_expand.T,
        s_depth.reshape(5, 5, PART),
        s_reduce.T,
        s_excite,
        s_bexcite[0],
        s_project,
        s_breduce[0],
    )


def solution(mesh):
    return jax.shard_map(
        on_device,
        mesh=mesh,
        in_specs=(
            P("dp", "space", None, None),
            P(None, "dp"),
            P(None, None, "dp"),
            P("dp", None),
            P(),
            P(None, "dp"),
            P("dp"),
            P("dp", None),
            P("dp", "space", None, None),
        ),
        out_specs=(
            P("dp", "space", None, None),
            P("dp", "space", None, None),
            P(None, "dp"),
            P(None, None, "dp"),
            P("dp", None),
            P(None, "dp"),
            P("dp"),
            P("dp", None),
            P(),
        ),
        check_vma=False,
    )
```

time: 739 us -> 232 us (0.31)
  blocking collectives: 238 us -> 0 us
  Pallas kernels: 0 us -> 229 us
  other arithmetic: 221 us -> 0 us
  matrix products: 113 us -> 0 us
  waiting for transfers between devices: 83.6 us -> 0 us
  local copies, waits for them, and re-layouts: 44.6 us -> 2.64 us
  starting transfers between devices: 18.9 us -> 0 us
  between operations: 15.4 us -> 0.66 us
    pallas_call x0 -> x2, Pallas kernels: none -> 229 us  [the longest x1 160 us: block(): pl.pallas_call(block_kernel, out_shape=(jax.ShapeDtypeStruct((IMGS, ROWS,...]
    convert_element_type x5 -> x0, other arithmetic: 147 us -> none  [the longest x2 84.8 us: depthwise(): total = total + padded[:, i:i + rows, j:j + cols, :].astype(jnp.float32)...]
    psum x2 -> x0, blocking collectives: 113 us -> none  [the longest x1 64.9 us: on_device(): lax.psum((g_expand, g_depth, g_reduce, g_excite, g_bexcite, g_project, g_...]
    dot_general x12 -> x0, matrix products: 113 us -> none  [the longest x1 74.7 us: on_device(): jnp.dot(dflat, full_project.T, preferred_element_type=jnp.float32)]
    all_gather x5 -> x0, blocking collectives: 93.9 us -> none  [the longest x1 22.8 us: on_device(): lax.all_gather(w_depth, 'dp', axis=2, tiled=True)]
    psum x1 -> x0, waiting for transfers between devices: 79.5 us -> none  [on_device(): lax.psum((g_expand, g_depth, g_reduce, g_excite, g_bexcite, g_project, g_...]
    reduce_sum x2 -> x0, other arithmetic: 55.2 us -> none  [kernel_grad(): jnp.sum(ddepth.astype(jnp.float32) * padded[:, i:i + rows, j:j + cols, :]...]
    unnamed x1 -> x0, blocking collectives: 30.9 us -> none
  transfers between devices with their start and end apart: 5 -> 0, of which waited for: 3 -> 0; matrix products, arithmetic and copies ran while one was open for 14% -> 0% of each run, Pallas kernels for 0% -> 0%
where the time goes in v5:
time: 232 us
  Pallas kernels  229 us (99%)
  local copies, waits for them, and re-layouts  2.64 us (1%)
    pallas_call x1, Pallas kernels, block(): pl.pallas_call(block_kernel, out_shape=(jax.ShapeDtypeStruct((IMGS, ROWS,...  160 us
    pallas_call x1, Pallas kernels, finish(): pl.pallas_call(finish_kernel, out_shape=(jax.ShapeDtypeStruct((PART, C),...  68.3 us

profile of v5, /device:TPU:1, one launch (start us, length us, event | category | flops | bytes accessed | tf_op | source)
XLA Modules:
  0.0 231.9 jit_solution(2796499017026814665)
XLA Ops:
  0.6 1.3 reshape.24.taps
  2.0 160.3 %block.1 = (bf16[2,12,176,100]{3,2,1,0:T(8,128)(2,1)}, bf16[2,12,176,100]{3,2,1,0:T(8,128)(2,1)}, f32[208,128]{1,0:T(8,128)}, f32[176,128]{1,0:T(8,128)}, f32[16,8,128]{2,1,0:T(8,128)}) custom-call(bf16[66,176]{1,0:T(8,128)(2,1)} %bitcast.14, bf16[66,176]{1,0:T(8,128)(2,1)} %wpr.1, bf16[25,66]{1,0:T(8,128)(2,1)} %reshape.24.taps, bf16[44,66]{1,0:T(8,128)(2,1)} %bitcast.15, ...), custom_call_target="tpu_custom_call" | custom-call | tf_op jit(solution)/shard_map/block/pallas_call | solution.py:542
  162.3 68.3 %finish.1 = (f32[66,176]{1,0:T(8,128)}, f32[25,66]{1,0:T(8,128)}, f32[44,66]{1,0:T(8,128)}, f32[44,66]{1,0:T(8,128)}, f32[1,66]{1,0:T(1,128)}, /*index=5*/f32[66...) custom-call(f32[208,128]{1,0:T(8,128)} %get-tuple-element.23.early, ...), custom_call_target="tpu_custom_call" | custom-call | tf_op jit(solution)/shard_map/finish/pallas_call | solution.py:648
  230.5 1.3 reshape.25

commit v6 on v5

--- a/solution.py
+++ b/solution.py
@@ -620,47 +620,41 @@
 
 def finish_kernel(
     early, late, mail, raw, raw_grad,
-    gexp, gdepth, greduce, gexcite, gbex, gproj, gbred, out, out_grad, sem,
+    gexp, gdepth, greduce, gexcite, gbex, gproj, gbred, out, out_grad,
 ):
-    moves = [
-        pltpu.make_async_copy(raw, out, sem.at[0]),
-        pltpu.make_async_copy(raw_grad, out_grad, sem.at[1]),
-    ]
-    for move in moves:
-        move.start()
-    gexp[...] = late[...].T[0:PART]
-    gproj[...] = early[0:C].T[0:PART]
-    gdepth[...] = early[C : C + 25, 0:PART]
-    rows = [mail[d] for d in range(ND)]
-    pool_all = jnp.concatenate([row[0:2] for row in rows], axis=0)
-    dlog_all = jnp.concatenate([row[2:4] for row in rows], axis=0)
-    sq_all = jnp.concatenate([row[4:6] for row in rows], axis=0)
-    dsq_all = jnp.concatenate([row[6:8] for row in rows], axis=0)
-    greduce[...] = dot_tn(dsq_all, pool_all, HIGH)[0:SE, 0:PART]
-    gexcite[...] = dot_tn(sq_all, dlog_all, HIGH)[0:SE, 0:PART]
-    gbex[...] = jnp.sum(dlog_all, axis=0, keepdims=True)[:, 0:PART]
-    gbred[...] = jnp.sum(dsq_all, axis=0, keepdims=True)[:, 0:SE]
-    for move in moves:
-        move.wait()
+    out[...] = raw[...]
+    out_grad[...] = raw_grad[...]
+
+    @pl.when(pl.program_id(0) == 0)
+    def _():
+        gexp[...] = late[...].T[0:PART]
+        gproj[...] = early[0:C].T[0:PART]
+        gdepth[...] = early[C : C + 25, 0:PART]
+        rows = [mail[d] for d in range(ND)]
+        pool_all = jnp.concatenate([row[0:2] for row in rows], axis=0)
+        dlog_all = jnp.concatenate([row[2:4] for row in rows], axis=0)
+        sq_all = jnp.concatenate([row[4:6] for row in rows], axis=0)
+        dsq_all = jnp.concatenate([row[6:8] for row in rows], axis=0)
+        greduce[...] = dot_tn(dsq_all, pool_all, HIGH)[0:SE, 0:PART]
+        gexcite[...] = dot_tn(sq_all, dlog_all, HIGH)[0:SE, 0:PART]
+        gbex[...] = jnp.sum(dlog_all, axis=0, keepdims=True)[:, 0:PART]
+        gbred[...] = jnp.sum(dsq_all, axis=0, keepdims=True)[:, 0:SE]
 
 
 def finish(early, late, mail, raw, raw_grad):
+    def whole(*shape):
+        zeros = (0,) * len(shape)
+        return pl.BlockSpec(shape, lambda n: zeros)
+
+    part = pl.BlockSpec((IMGS, 3, C, COLS), lambda n: (0, n, 0, 0))
+    shapes = ((PART, C), (25, PART), (SE, PART), (SE, PART), (1, PART), (PART, C), (1, SE))
     return pl.pallas_call(
         finish_kernel,
-        out_shape=(
-            jax.ShapeDtypeStruct((PART, C), F32),
-            jax.ShapeDtypeStruct((25, PART), F32),
-            jax.ShapeDtypeStruct((SE, PART), F32),
-            jax.ShapeDtypeStruct((SE, PART), F32),
-            jax.ShapeDtypeStruct((1, PART), F32),
-            jax.ShapeDtypeStruct((PART, C), F32),
-            jax.ShapeDtypeStruct((1, SE), F32),
-            jax.ShapeDtypeStruct((IMGS, ROWS, C, COLS), BF16),
-            jax.ShapeDtypeStruct((IMGS, ROWS, C, COLS), BF16),
-        ),
-        in_specs=[VMEM, VMEM, VMEM, ANY, ANY],
-        out_specs=(VMEM,) * 7 + (ANY, ANY),
-        scratch_shapes=[pltpu.SemaphoreType.DMA((2,))],
+        grid=(ROWS // 3,),
+        out_shape=tuple(jax.ShapeDtypeStruct(shape, F32) for shape in shapes)
+        + (jax.ShapeDtypeStruct((IMGS, ROWS, C, COLS), BF16),) * 2,
+        in_specs=[whole(EARLY, 128), whole(C, 128), whole(ND, 8, 128), part, part],
+        out_specs=tuple(whole(*shape) for shape in shapes) + (part, part),
         name="finish",
     )(early, late, mail, raw, raw_grad)
 

time: 232 us -> 168 us (0.72)
  Pallas kernels: 229 us -> 165 us
    pallas_call x1, Pallas kernels: 68.3 us -> 4.39 us  [finish(): pl.pallas_call(finish_kernel, grid=(ROWS // 3,), out_shape=tuple((jax.Sha...]
where the time goes in v6:
time: 168 us
  Pallas kernels  165 us (98%)
  local copies, waits for them, and re-layouts  2.64 us (2%)
    pallas_call x1, Pallas kernels, block(): pl.pallas_call(block_kernel, out_shape=(jax.ShapeDtypeStruct((IMGS, ROWS,...  160 us
    pallas_call x1, Pallas kernels, finish(): pl.pallas_call(finish_kernel, grid=(ROWS // 3,), out_shape=tuple((jax.Sha...  4.39 us

profile of v6, /device:TPU:1, one launch (start us, length us, event | category | flops | bytes accessed | tf_op | source)
XLA Modules:
  0.0 168.0 jit_solution(16458051540069330879)
XLA Ops:
  0.6 1.3 reshape.24.taps
  2.0 160.3 %block.1 = (bf16[2,12,176,100]{3,2,1,0:T(8,128)(2,1)}, bf16[2,12,176,100]{3,2,1,0:T(8,128)(2,1)}, f32[208,128]{1,0:T(8,128)}, f32[176,128]{1,0:T(8,128)}, f32[16,8,128]{2,1,0:T(8,128)}) custom-call(bf16[66,176]{1,0:T(8,128)(2,1)} %bitcast.14, bf16[66,176]{1,0:T(8,128)(2,1)} %wpr.1, bf16[25,66]{1,0:T(8,128)(2,1)} %reshape.24.taps, bf16[44,66]{1,0:T(8,128)(2,1)} %bitcast.15, ...), custom_call_target="tpu_custom_call" | custom-call | tf_op jit(solution)/shard_map/block/pallas_call | solution.py:542
  162.3 4.4 %finish.1 = (f32[66,176]{1,0:T(8,128)}, f32[25,66]{1,0:T(8,128)}, f32[44,66]{1,0:T(8,128)}, f32[44,66]{1,0:T(8,128)}, f32[1,66]{1,0:T(1,128)}, /*index=5*/f32[66...) custom-call(f32[208,128]{1,0:T(8,128)} %get-tuple-element.23.early, ...), custom_call_target="tpu_custom_call" | custom-call | tf_op jit(solution)/shard_map/finish/pallas_call | solution.py:651
  166.7 1.3 reshape.25

commit v7 on v6

--- a/solution.py
+++ b/solution.py
@@ -67,9 +67,83 @@
     return jnp.where(place == wanted, 1.0, 0.0).astype(BF16)
 
 
-def spread_taps(taps, wide_taps):
-    for k in range(25):
-        wide_taps[k] = jnp.broadcast_to(taps[k : k + 1, :], (8, 128))
+def point_taps(taps):
+    w0, w1, w2, w3, w4 = taps
+    even, odd = w0 + w2 + w4, w1 + w3
+    even2, odd2 = w0 + 4.0 * w2 + 16.0 * w4, 2.0 * w1 + 8.0 * w3
+    even3, odd3 = w0 + 0.25 * w2 + 0.0625 * w4, 0.5 * w1 + 0.125 * w3
+    return [
+        w0,
+        (even + odd) * (-2.0 / 9.0),
+        (even - odd) * (-2.0 / 9.0),
+        (even2 + odd2) * (1.0 / 360.0),
+        (even2 - odd2) * (1.0 / 360.0),
+        (even3 + odd3) * (32.0 / 45.0),
+        (even3 - odd3) * (32.0 / 45.0),
+        w4,
+    ]
+
+
+def taps_from_points(g):
+    s1, d1 = (g[1] + g[2]) * (-2.0 / 9.0), (g[1] - g[2]) * (-2.0 / 9.0)
+    s2, d2 = (g[3] + g[4]) * (1.0 / 360.0), (g[3] - g[4]) * (1.0 / 360.0)
+    s3, d3 = (g[5] + g[6]) * (32.0 / 45.0), (g[5] - g[6]) * (32.0 / 45.0)
+    return [
+        g[0] + s1 + s2 + s3,
+        d1 + 2.0 * d2 + 0.5 * d3,
+        s1 + 4.0 * s2 + 0.25 * s3,
+        d1 + 8.0 * d2 + 0.125 * d3,
+        s1 + 16.0 * s2 + 0.0625 * s3 + g[7],
+    ]
+
+
+def to_points(x):
+    x0, x1, x2, x3, x4, x5, x6, x7 = x
+    f3, f4 = 5.0 * x3, 5.0 * x4
+    e1, o1 = (x6 + x2) - 4.25 * x4, (x5 + x1) - 4.25 * x3
+    e2, o2 = (x2 - f4) + 4.0 * x6, (x1 - f3) + 4.0 * x5
+    e3, o3 = (4.0 * x2 - f4) + x6, (4.0 * x1 - f3) + x5
+    o2, o3 = o2 + o2, 0.5 * o3
+    return [
+        (x0 - x6) + 5.25 * (x4 - x2),
+        e1 + o1,
+        e1 - o1,
+        e2 + o2,
+        e2 - o2,
+        e3 + o3,
+        e3 - o3,
+        (x7 - x1) + 5.25 * (x3 - x5),
+    ]
+
+
+def from_points(m):
+    s1, d1 = m[1] + m[2], m[1] - m[2]
+    s2, d2 = m[3] + m[4], m[3] - m[4]
+    s3, d3 = m[5] + m[6], m[5] - m[6]
+    return [
+        (m[0] + s1) + (s2 + s3),
+        (d1 + 2.0 * d2) + 0.5 * d3,
+        (s1 + 4.0 * s2) + 0.25 * s3,
+        ((d1 + 8.0 * d2) + 0.125 * d3) + m[7],
+    ]
+
+
+def outputs_to_points(y):
+    y0, y1, y2, y3 = y
+    a, b = y0 + y2, y1 + y3
+    c, d = y0 + 4.0 * y2, 2.0 * y1 + 8.0 * y3
+    e, f = y0 + 0.25 * y2, 0.5 * y1 + 0.125 * y3
+    return [y0, a + b, a - b, c + d, c - d, e + f, e - f, y3]
+
+
+def spread_taps(taps, wide_taps, flip):
+    for j in range(5):
+        column = [taps[5 * i + j : 5 * i + j + 1, :] for i in range(5)]
+        if flip:
+            column = column[::-1]
+        place = 4 - j if flip else j
+        for p, value in enumerate(point_taps(column)):
+            wide_taps[5 * p + place] = jnp.broadcast_to(value, (8, 128))
 
 
 def edge_columns(value):
@@ -87,14 +161,15 @@
     ref[r, 2 + BLOCK :] = right
 
 
-def conv_row(ref, r, h, wide_taps, flip):
-    total = jnp.zeros((BLOCK, 8, 128), F32)
-    for i in range(5):
-        source = ref[r + i, :, 8 * h : 8 * h + 8, :]
-        for j in range(5):
-            k = (4 - i) * 5 + 4 - j if flip else i * 5 + j
-            total = total + source[j : j + BLOCK] * wide_taps[k][None]
-    return total
+def conv_rows(ref, q, h, wide_taps):
+    points = to_points([ref[4 * q + n, :, 8 * h : 8 * h + 8, :] for n in range(8)])
+    totals = []
+    for p in range(8):
+        total = points[p][0:BLOCK] * wide_taps[5 * p][None]
+        for j in range(1, 5):
+            total = total + points[p][j : j + BLOCK] * wide_taps[5 * p + j][None]
+        totals.append(total)
+    return from_points(totals)
 
 
 def pad_mask():
@@ -220,9 +295,11 @@
     out, out_grad, early, late, mail_out,
     stage, pack, full, top, bottom, flatw, fp, cp, fpt, cpt, we, wp, misc,
     wide_taps, ex, dgs, saved, depth, sums, packed, landed, lanes, vecs, gates, msgs, mail,
-    edge, above, below, gated, dpre, acc, flat, epiece, egot, espace, lpiece, lgot, lspace,
+    edge, above, below, gated, dpre, acc, held, flat, flat_taps,
+    epiece, egot, espace, lpiece, lgot, lspace, tpiece, tgot, tspace,
     wsend, wrecv, hsend, hrecv, csend, crecv, ssend, srecv, msend, mrecv,
     dsend, drecv, esend, erecv, fsend, frecv, lsend, lrecv, gsend, grecv,
+    tsend, trecv, usend, urecv,
 ):
     me_s, me_d = lax.axis_index("space"), lax.axis_index("dp")
     core = lax.rem(me_s, 2)
@@ -240,7 +317,8 @@
     stage[0, 0:PART, 0:C] = wet[...].astype(F32)
     stage[1, 0:PART, 0:C] = wpr[...].astype(F32)
     side = slice(C, C + PART)
-    stage[0, 0:25, side] = taps[...].astype(F32)
+    for i in range(5):
+        stage[0, 5 * i : 5 * i + 5, side] = taps[i].astype(F32)
     stage[0, 32 : 32 + SE, side] = wrt[...].astype(F32)
     stage[1, 0:SE, side] = wx_own[...].astype(F32)
     stage[1, 48:49, side] = bex[...].astype(F32)
@@ -330,7 +408,7 @@
         lax.fori_loop(0, 2, chunk, 0)
 
     def first(t, carry):
-        spread_taps(misc[0:32, lane_of(t)], wide_taps)
+        spread_taps(misc[0:32, lane_of(t)], wide_taps, False)
 
         def expand(q, carry):
             pre = dot_nt(fp[pl.ds(8 * q, 8)].reshape(8 * PIX, C), we[lane_of(t), :])
@@ -342,20 +420,22 @@
         lax.fori_loop(0, 2, expand, 0)
         cot_matmul(t)
 
-        def conv(r, carry):
+        def conv(q, carry):
             pools, grads = list(carry[:2]), list(carry[2:])
             for h in range(2):
-                total = conv_row(ex, r, h, wide_taps, False)
-                depth[t, r, :, 8 * h : 8 * h + 8, :] = total
-                act = swish(total)
-                dgated = dgs[r, :, 8 * h : 8 * h + 8, :]
-                grads[h] = grads[h] + jnp.sum(act * dgated, axis=0)
-                pools[h] = pools[h] + jnp.sum(act[:9], axis=0) + jnp.sum(act[9:] * keep, axis=0)
-            saved[t, r] = ex[r].astype(BF16)
+                rows = slice(8 * h, 8 * h + 8)
+                for n, total in enumerate(conv_rows(ex, q, h, wide_taps)):
+                    depth[t, 4 * q + n, :, rows, :] = total
+                    act = swish(total)
+                    grads[h] = grads[h] + jnp.sum(act * dgs[4 * q + n, :, rows, :], axis=0)
+                    pools[h] = pools[h] + jnp.sum(act[:9], axis=0)
+                    pools[h] = pools[h] + jnp.sum(act[9:] * keep, axis=0)
+            for n in range(4):
+                saved[t, 4 * q + n] = ex[4 * q + n].astype(BF16)
             return (*pools, *grads)
 
         zero = jnp.zeros((8, 128), F32)
-        parts = lax.fori_loop(0, ROWS, conv, (zero,) * 4)
+        parts = lax.fori_loop(0, ROWS // 4, conv, (zero,) * 4)
         for r in range(ROWS, HROWS):
             saved[t, r] = ex[r].astype(BF16)
         for k in range(4):
@@ -438,35 +518,19 @@
 
     lax.fori_loop(0, TILES, second, 0)
 
-    def tap_grads(t, carry):
-        acc[...] = jnp.zeros_like(acc)
-
-        def row(r, carry):
-            for h in range(2):
-                rows = slice(8 * h, 8 * h + 8)
-                mine = depth[t, r, :, rows, :]
-                for i in range(5):
-                    source = saved[t, r + i].astype(F32)[:, rows, :]
-                    for j in range(5):
-                        k = 5 * i + j
-                        acc[k] = acc[k] + jnp.sum(mine * source[j : j + BLOCK], axis=0)
-            return carry
-
-        lax.fori_loop(0, ROWS, row, 0)
-        for k in range(25):
-            flat[C + k : C + k + 1, lane_of(t)] = jnp.sum(acc[k], axis=0, keepdims=True)
-        return carry
-
-    flat[...] = jnp.zeros_like(flat)
-    lax.fori_loop(0, TILES, tap_grads, 0)
-    all_channels_grad(gated, cpt, flat.at[0:C])
-    for d in range(ND):
-        epiece[d] = flat[:, SLOT * d : SLOT * d + 128].astype(BF16)
+    def pieces_of(source, rows, piece):
+        for d in range(ND):
+            piece[d] = source[0:rows, SLOT * d : SLOT * d + 128].astype(BF16)
+
+    flat[:, CP:] = jnp.zeros((C, 128), F32)
+    flat_taps[...] = jnp.zeros_like(flat_taps)
+    all_channels_grad(gated, cpt, flat)
+    pieces_of(flat, C, epiece)
     for copy in to_dp(epiece, egot, esend, erecv):
         copy.start()
 
     def third(t, carry):
-        spread_taps(misc[0:32, lane_of(t)], wide_taps)
+        spread_taps(misc[0:32, lane_of(t)], wide_taps, True)
 
         def middle(r, carry):
             store_row(ex, r + 2, depth[t, r])
@@ -486,17 +550,19 @@
             store_row(ex, n, above[t, n].astype(F32) * has_top)
             store_row(ex, ROWS + 2 + n, below[t, n].astype(F32) * has_bottom)
 
-        def conv(r, carry):
+        def conv(q, carry):
             both = []
             for h in range(2):
-                slope = dgs[r, :, 8 * h : 8 * h + 8, :]
-                both.append(conv_row(ex, r, h, wide_taps, True) * slope)
-            dpre[pl.ds(pl.multiple_of(r * PIX, PIX), PIX), lane_of(t)] = (
-                jnp.concatenate(both, axis=1).reshape(PIX, 128).astype(BF16)
-            )
+                rows = slice(8 * h, 8 * h + 8)
+                values = conv_rows(ex, q, h, wide_taps)
+                both.append([value * dgs[4 * q + n, :, rows, :] for n, value in enumerate(values)])
+            for n in range(4):
+                value = jnp.concatenate([both[0][n], both[1][n]], axis=1)
+                span = pl.ds(pl.multiple_of((4 * q + n) * PIX, PIX), PIX)
+                dpre[span, lane_of(t)] = value.reshape(PIX, 128).astype(BF16)
             return carry
 
-        lax.fori_loop(0, ROWS, conv, 0)
+        lax.fori_loop(0, ROWS // 4, conv, 0)
 
         @pl.when(t == TILES // 2)
         def _():
@@ -509,23 +575,64 @@
 
     lax.fori_loop(0, TILES, third, 0)
 
-    all_channels_grad(dpre, fpt, flat.at[0:C])
-    for d in range(ND):
-        lpiece[d] = flat[0:C, SLOT * d : SLOT * d + 128].astype(BF16)
-    copies = to_dp(lpiece, lgot, lsend, lrecv)
+    all_channels_grad(dpre, fpt, flat)
+    pieces_of(flat, C, lpiece)
+    for copy in to_dp(lpiece, lgot, lsend, lrecv):
+        copy.start()
+
+    def tap_grads(t, carry):
+        acc[...] = jnp.zeros_like(acc)
+
+        def window(q, carry):
+            for h in range(2):
+                rows = slice(8 * h, 8 * h + 8)
+                for low, high in ((0, 9), (9, WIDE)):
+                    points = to_points(
+                        [saved[t, 4 * q + n].astype(F32)[low:high, rows, :] for n in range(8)]
+                    )
+                    for p in range(8):
+                        held[p, low:high] = points[p]
+                mine = outputs_to_points([depth[t, 4 * q + n, :, rows, :] for n in range(4)])
+                for p in range(8):
+                    source = held[p]
+                    for j in range(5):
+                        k = 5 * p + j
+                        acc[k] = acc[k] + jnp.sum(mine[p] * source[j : j + BLOCK], axis=0)
+            return carry
+
+        lax.fori_loop(0, ROWS // 4, window, 0)
+        for j in range(5):
+            sums_at = [jnp.sum(acc[5 * p + j], axis=0, keepdims=True) for p in range(8)]
+            for i, value in enumerate(taps_from_points(sums_at)):
+                flat_taps[5 * i + j : 5 * i + j + 1, lane_of(t)] = value
+
+        @pl.when(t == TILES // 2)
+        def _():
+            total = dp_sum(to_dp(lpiece, lgot, lsend, lrecv), lpiece, lgot)
+            lspace[me_s] = total.astype(BF16)
+            for copy in to_space(lspace, gsend, grecv):
+                copy.start()
+
+        return carry
+
+    lax.fori_loop(0, TILES, tap_grads, 0)
+    pieces_of(flat_taps, 32, tpiece)
+    copies = to_dp(tpiece, tgot, tsend, trecv)
     for copy in copies:
         copy.start()
+
     all_channels_out(dpre, we, cp, 0, out_grad)
-    early[...] = space_sum(to_space(espace, fsend, frecv), espace)
+    tspace[me_s] = dp_sum(copies, tpiece, tgot).astype(BF16)
+    copies = to_space(tspace, usend, urecv)
+    for copy in copies:
+        copy.start()
+    all_channels_out(gated, wp, fp, 2, out)
     for copy in small:
         copy.wait()
     mail_out[...] = mail[...]
-    lspace[me_s] = dp_sum(copies, lpiece, lgot).astype(BF16)
-    copies = to_space(lspace, gsend, grecv)
-    for copy in copies:
-        copy.start()
-    all_channels_out(gated, wp, fp, 2, out)
-    late[...] = space_sum(copies, lspace)
+    early[0:C] = space_sum(to_space(espace, fsend, frecv), espace)
+    late[...] = space_sum(to_space(lspace, gsend, grecv), lspace)
+    early[C:] = space_sum(copies, tspace)
 
 
 def block(*args):
@@ -564,7 +671,7 @@
             bf16(CP, C),
             bf16(CP, C),
             f32(136, CP),
-            f32(25, 8, 128),
+            f32(40, 8, 128),
             f32(HROWS, WIDE, SUB, 128),
             f32(ROWS, BLOCK, SUB, 128),
             bf16(TILES, HROWS, WIDE, SUB, 128),
@@ -582,14 +689,19 @@
             bf16(TILES, 2, BLOCK, SUB, 128),
             bf16(ROWS * PIX, CP),
             bf16(ROWS * PIX, CP),
-            f32(25, 8, 128),
-            f32(EARLY, CP + 128),
-            bf16(ND, EARLY, 128),
-            bf16(ND, EARLY, 128),
-            bf16(NS, EARLY, 128),
+            f32(40, 8, 128),
+            f32(8, WIDE, 8, 128),
+            f32(C, CP + 128),
+            f32(32, CP + 128),
             bf16(ND, C, 128),
             bf16(ND, C, 128),
             bf16(NS, C, 128),
+            bf16(ND, C, 128),
+            bf16(ND, C, 128),
+            bf16(NS, C, 128),
+            bf16(ND, 32, 128),
+            bf16(ND, 32, 128),
+            bf16(NS, 32, 128),
             sems(ND),
             sems(ND),
             sems(2),
@@ -602,6 +714,10 @@
             sems(ND),
             sems(2, TILES),
             sems(2, TILES),
+            sems(ND),
+            sems(ND),
+            sems(NS),
+            sems(NS),
             sems(ND),
             sems(ND),
             sems(NS),
@@ -629,7 +745,8 @@
     def _():
         gexp[...] = late[...].T[0:PART]
         gproj[...] = early[0:C].T[0:PART]
-        gdepth[...] = early[C : C + 25, 0:PART]
+        for i in range(5):
+            gdepth[i] = early[C + 5 * i : C + 5 * i + 5, 0:PART]
         rows = [mail[d] for d in range(ND)]
         pool_all = jnp.concatenate([row[0:2] for row in rows], axis=0)
         dlog_all = jnp.concatenate([row[2:4] for row in rows], axis=0)
@@ -647,7 +764,7 @@
         return pl.BlockSpec(shape, lambda n: zeros)
 
     part = pl.BlockSpec((IMGS, 3, C, COLS), lambda n: (0, n, 0, 0))
-    shapes = ((PART, C), (25, PART), (SE, PART), (SE, PART), (1, PART), (PART, C), (1, SE))
+    shapes = ((PART, C), (5, 5, PART), (SE, PART), (SE, PART), (1, PART), (PART, C), (1, SE))
     return pl.pallas_call(
         finish_kernel,
         grid=(ROWS // 3,),
@@ -665,7 +782,7 @@
     raw, raw_grad, early, late, mail = block(
         w_expand.T,
         w_project,
-        w_depth.reshape(25, PART),
+        w_depth,
         w_reduce.T,
         w_excite,
         b_excite[None, :],
@@ -680,7 +797,7 @@
         output.swapaxes(2, 3),
         grad.swapaxes(2, 3),
         s_expand.T,
-        s_depth.reshape(5, 5, PART),
+        s_depth,
         s_reduce.T,
         s_excite,
         s_bexcite[0],

time: 168 us -> 140 us (0.83)
  Pallas kernels: 165 us -> 139 us
  local copies, waits for them, and re-layouts: 2.64 us -> 0 us
    pallas_call x1, Pallas kernels: 160 us -> 135 us  [block(): pl.pallas_call(block_kernel, out_shape=(jax.ShapeDtypeStruct((IMGS, ROWS,...]
    reshape x2 -> x0, local copies, waits for them, and re-layouts: 2.64 us -> none  [the longest x1 1.32 us: on_device(): s_depth.reshape(5, 5, PART)]
where the time goes in v7:
time: 140 us
  Pallas kernels  139 us (99%)
    pallas_call x1, Pallas kernels, block(): pl.pallas_call(block_kernel, out_shape=(jax.ShapeDtypeStruct((IMGS, ROWS,...  135 us
    pallas_call x1, Pallas kernels, finish(): pl.pallas_call(finish_kernel, grid=(ROWS // 3,), out_shape=tuple((jax.Sha...  4.39 us

profile of v7, /device:TPU:1, one launch (start us, length us, event | category | flops | bytes accessed | tf_op | source)
XLA Modules:
  0.0 140.2 jit_solution(16930148044619594589)
XLA Ops:
  0.6 135.1 %block.1 = (bf16[2,12,176,100]{3,2,1,0:T(8,128)(2,1)}, bf16[2,12,176,100]{3,2,1,0:T(8,128)(2,1)}, f32[208,128]{1,0:T(8,128)}, f32[176,128]{1,0:T(8,128)}, f32[16,8,128]{2,1,0:T(8,128)}) custom-call(bf16[66,176]{1,0:T(8,128)(2,1)} %bitcast.14, bf16[66,176]{1,0:T(8,128)(2,1)} %wpr.1, bf16[5,5,66]{2,1,0:T(8,128)(2,1)} %taps.1, bf16[44,66]{1,0:T(8,128)(2,1)} %bitcast.15, ...), custom_call_target="tpu_custom_call" | custom-call | tf_op jit(solution)/shard_map/block/pallas_call | solution.py:649
  135.8 4.4 %finish.1 = (f32[66,176]{1,0:T(8,128)}, f32[5,5,66]{2,1,0:T(8,128)}, f32[44,66]{1,0:T(8,128)}, f32[44,66]{1,0:T(8,128)}, f32[1,66]{1,0:T(1,128)}, /*index=5*/f32...) custom-call(f32[208,128]{1,0:T(8,128)} %get-tuple-element.23.early, ...), custom_call_target="tpu_custom_call" | custom-call | tf_op jit(solution)/shard_map/finish/pallas_call | solution.py:768

commit v8 on v7

--- a/solution.py
+++ b/solution.py
@@ -32,7 +32,8 @@
 
 
 def swish(value):
-    return value * sigmoid(value)
+    half = 0.5 * value
+    return half + half * jnp.tanh(half)
 
 
 def swish_grad(value):
@@ -291,15 +292,15 @@
 
 
 def block_kernel(
-    wet, wpr, taps, wrt, wx_own, bex, bred, feats, cot,
+    wet, wpr, taps, wrt, wx_own, bex, bred, feats_in, cot_in,
     out, out_grad, early, late, mail_out,
-    stage, pack, full, top, bottom, flatw, fp, cp, fpt, cpt, we, wp, misc,
-    wide_taps, ex, dgs, saved, depth, sums, packed, landed, lanes, vecs, gates, msgs, mail,
+    feats, cot, stage, pack, full, top, bottom, flatw, fp, cp, fpt, cpt, we, wp, misc,
+    wide_taps, ex, dgs, coming_pre, coming_dg, saved, depth, sums, packed, landed, lanes, vecs, gates, msgs, mail,
     edge, above, below, gated, dpre, acc, held, flat, flat_taps,
     epiece, egot, espace, lpiece, lgot, lspace, tpiece, tgot, tspace,
     wsend, wrecv, hsend, hrecv, csend, crecv, ssend, srecv, msend, mrecv,
     dsend, drecv, esend, erecv, fsend, frecv, lsend, lrecv, gsend, grecv,
-    tsend, trecv, usend, urecv,
+    tsend, trecv, usend, urecv, insem,
 ):
     me_s, me_d = lax.axis_index("space"), lax.axis_index("dp")
     core = lax.rem(me_s, 2)
@@ -312,6 +313,13 @@
         pl.semaphore_signal(
             barrier, inc=1, device_id=(lax.rem(me_s + k, NS), me_d), device_id_type=MESH
         )
+
+    arrive = [
+        pltpu.make_async_copy(feats_in, feats, insem.at[0]),
+        pltpu.make_async_copy(cot_in, cot, insem.at[1]),
+    ]
+    for copy in arrive:
+        copy.start()
 
     stage[...] = jnp.zeros_like(stage)
     stage[0, 0:PART, 0:C] = wet[...].astype(F32)
@@ -336,6 +344,8 @@
         )
         copy.start()
         copies.append(copy)
+    for copy in arrive:
+        copy.wait()
     halo = to_neighbours(
         feats.at[:, pl.ds(ROWS - 2, 2)],
         top,
@@ -398,27 +408,35 @@
     def lane_of(t):
         return pl.ds(pl.multiple_of(128 * t, 128), 128)
 
-    def cot_matmul(t):
-        def chunk(q, carry):
-            rows = pl.ds(6 * q, 6)
-            product = dot_nt(cp[rows].reshape(6 * PIX, C), wp[lane_of(t), :])
-            dgs[rows] = product.reshape(6, BLOCK, SUB, 128)
+    def pre_rows(t, start, count):
+        product = dot_nt(fp[pl.ds(start, count)].reshape(count * PIX, C), we[lane_of(t), :])
+        coming_pre[pl.ds(start, count)] = product.reshape(count, BLOCK, SUB, 128)
+
+    def cot_rows(t, start, count):
+        product = dot_nt(cp[pl.ds(start, count)].reshape(count * PIX, C), wp[lane_of(t), :])
+        coming_dg[pl.ds(start, count)] = product.reshape(count, BLOCK, SUB, 128)
+
+    def next_tile(t):
+        return jnp.minimum(t + 1, TILES - 1)
+
+    def take_dg():
+        def row(r, carry):
+            dgs[r] = coming_dg[r]
             return carry
 
-        lax.fori_loop(0, 2, chunk, 0)
+        lax.fori_loop(0, ROWS, row, 0)
 
     def first(t, carry):
         spread_taps(misc[0:32, lane_of(t)], wide_taps, False)
 
         def expand(q, carry):
-            pre = dot_nt(fp[pl.ds(8 * q, 8)].reshape(8 * PIX, C), we[lane_of(t), :])
-            value = swish(pre).astype(BF16).astype(F32).reshape(8, BLOCK, SUB, 128)
-            for n in range(8):
-                store_row(ex, 8 * q + n, value[n])
+            for n in range(4):
+                value = swish(coming_pre[4 * q + n]).astype(BF16).astype(F32)
+                store_row(ex, 4 * q + n, value)
             return carry
 
-        lax.fori_loop(0, 2, expand, 0)
-        cot_matmul(t)
+        lax.fori_loop(0, HROWS // 4, expand, 0)
+        take_dg()
 
         def conv(q, carry):
             pools, grads = list(carry[:2]), list(carry[2:])
@@ -432,6 +450,8 @@
                     pools[h] = pools[h] + jnp.sum(act[9:] * keep, axis=0)
             for n in range(4):
                 saved[t, 4 * q + n] = ex[4 * q + n].astype(BF16)
+            pre_rows(next_tile(t), jnp.minimum(6 * q, HROWS - 6), 6)
+            cot_rows(next_tile(t), 4 * q, 4)
             return (*pools, *grads)
 
         zero = jnp.zeros((8, 128), F32)
@@ -442,6 +462,12 @@
             sums[t, k : k + 1, :] = jnp.sum(parts[k], axis=0, keepdims=True)
         return carry
 
+    def begin(q, carry):
+        pre_rows(0, 8 * q, 8)
+        cot_rows(0, 6 * q, 6)
+        return carry
+
+    lax.fori_loop(0, 2, begin, 0)
     lax.fori_loop(0, TILES, first, 0)
 
     packed[...] = jnp.zeros_like(packed)
@@ -451,6 +477,12 @@
     copies = to_space(landed, ssend, srecv)
     for copy in copies:
         copy.start()
+
+    def begin_again(q, carry):
+        cot_rows(0, 6 * q, 6)
+        return carry
+
+    lax.fori_loop(0, 2, begin_again, 0)
     total = space_sum(copies, landed)
     for t in range(TILES):
         lanes[0:4, 128 * t : 128 * (t + 1)] = total[t // 2, 4 * (t % 2) : 4 * (t % 2) + 4]
@@ -492,23 +524,30 @@
         )
 
     def second(t, carry):
-        cot_matmul(t)
-
-        def pointwise(r, carry):
-            both = []
-            for h in range(2):
-                rows = slice(8 * h, 8 * h + 8)
-                value, ddepth = gate_row(
-                    depth[t, r, :, rows, :], dgs[r, :, rows, :], gates.at[:, lane_of(t)], h, keep
+        take_dg()
+
+        def pointwise(q, carry):
+            for n in range(4):
+                r = 4 * q + n
+                both = []
+                for h in range(2):
+                    rows = slice(8 * h, 8 * h + 8)
+                    value, ddepth = gate_row(
+                        depth[t, r, :, rows, :],
+                        dgs[r, :, rows, :],
+                        gates.at[:, lane_of(t)],
+                        h,
+                        keep,
+                    )
+                    depth[t, r, :, rows, :] = ddepth.astype(BF16).astype(F32)
+                    both.append(value)
+                gated[pl.ds(pl.multiple_of(r * PIX, PIX), PIX), lane_of(t)] = (
+                    jnp.concatenate(both, axis=1).reshape(PIX, 128).astype(BF16)
                 )
-                depth[t, r, :, rows, :] = ddepth.astype(BF16).astype(F32)
-                both.append(value)
-            gated[pl.ds(pl.multiple_of(r * PIX, PIX), PIX), lane_of(t)] = (
-                jnp.concatenate(both, axis=1).reshape(PIX, 128).astype(BF16)
-            )
+            cot_rows(next_tile(t), 4 * q, 4)
             return carry
 
-        lax.fori_loop(0, ROWS, pointwise, 0)
+        lax.fori_loop(0, ROWS // 4, pointwise, 0)
         for n in range(2):
             edge[t, 0, n] = depth[t, n].astype(BF16)
             edge[t, 1, n] = depth[t, ROWS - 2 + n].astype(BF16)
@@ -538,12 +577,12 @@
 
         lax.fori_loop(0, ROWS, middle, 0)
 
-        def chunk(q, carry):
-            pre = dot_nt(fp[pl.ds(6 * q + 2, 6)].reshape(6 * PIX, C), we[lane_of(t), :])
-            dgs[pl.ds(6 * q, 6)] = swish_grad(pre).reshape(6, BLOCK, SUB, 128)
+        def slopes(q, carry):
+            for n in range(4):
+                dgs[4 * q + n] = swish_grad(coming_pre[4 * q + n + 2])
             return carry
 
-        lax.fori_loop(0, 2, chunk, 0)
+        lax.fori_loop(0, ROWS // 4, slopes, 0)
         for copy in edge_copies(t):
             copy.wait()
         for n in range(2):
@@ -560,6 +599,7 @@
                 value = jnp.concatenate([both[0][n], both[1][n]], axis=1)
                 span = pl.ds(pl.multiple_of((4 * q + n) * PIX, PIX), PIX)
                 dpre[span, lane_of(t)] = value.reshape(PIX, 128).astype(BF16)
+            pre_rows(next_tile(t), 4 * q + 2, 4)
             return carry
 
         lax.fori_loop(0, ROWS // 4, conv, 0)
@@ -573,6 +613,11 @@
 
         return carry
 
+    def begin_third(q, carry):
+        pre_rows(0, 6 * q + 2, 6)
+        return carry
+
+    lax.fori_loop(0, 2, begin_third, 0)
     lax.fori_loop(0, TILES, third, 0)
 
     all_channels_grad(dpre, fpt, flat)
@@ -655,9 +700,11 @@
             jax.ShapeDtypeStruct((C, 128), F32),
             jax.ShapeDtypeStruct((ND, 8, 128), F32),
         ),
-        in_specs=[VMEM] * 9,
+        in_specs=[VMEM] * 7 + [ANY] * 2,
         out_specs=(VMEM,) * 5,
         scratch_shapes=[
+            bf16(IMGS, ROWS, C, COLS),
+            bf16(IMGS, ROWS, C, COLS),
             f32(2, 80, 256),
             bf16(2, 80, 256),
             bf16(2, ND, 80, 256),
@@ -673,6 +720,8 @@
             f32(136, CP),
             f32(40, 8, 128),
             f32(HROWS, WIDE, SUB, 128),
+            f32(ROWS, BLOCK, SUB, 128),
+            f32(HROWS, BLOCK, SUB, 128),
             f32(ROWS, BLOCK, SUB, 128),
             bf16(TILES, HROWS, WIDE, SUB, 128),
             f32(TILES, ROWS, BLOCK, SUB, 128),
@@ -726,6 +775,7 @@
             sems(ND),
             sems(NS),
             sems(NS),
+            sems(2),
         ],
         compiler_params=pltpu.CompilerParams(
             collective_id=0, has_side_effects=True, vmem_limit_bytes=63 * 2**20
@@ -763,11 +813,11 @@
         zeros = (0,) * len(shape)
         return pl.BlockSpec(shape, lambda n: zeros)
 
-    part = pl.BlockSpec((IMGS, 3, C, COLS), lambda n: (0, n, 0, 0))
+    part = pl.BlockSpec((IMGS, 6, C, COLS), lambda n: (0, n, 0, 0))
     shapes = ((PART, C), (5, 5, PART), (SE, PART), (SE, PART), (1, PART), (PART, C), (1, SE))
     return pl.pallas_call(
         finish_kernel,
-        grid=(ROWS // 3,),
+        grid=(ROWS // 6,),
         out_shape=tuple(jax.ShapeDtypeStruct(shape, F32) for shape in shapes)
         + (jax.ShapeDtypeStruct((IMGS, ROWS, C, COLS), BF16),) * 2,
         in_specs=[whole(EARLY, 128), whole(C, 128), whole(ND, 8, 128), part, part],

time: 140 us -> 136 us (0.971)
  Pallas kernels: 139 us -> 135 us
    pallas_call x1, Pallas kernels: 135 us -> 132 us  [block(): pl.pallas_call(block_kernel, out_shape=(jax.ShapeDtypeStruct((IMGS, ROWS,...]
where the time goes in v8:
time: 136 us
  Pallas kernels  135 us (99%)
    pallas_call x1, Pallas kernels, block(): pl.pallas_call(block_kernel, out_shape=(jax.ShapeDtypeStruct((IMGS, ROWS,...  132 us
    pallas_call x1, Pallas kernels, finish(): pl.pallas_call(finish_kernel, grid=(ROWS // 6,), out_shape=tuple((jax.Sha...  3.22 us

profile of v8, /device:TPU:1, one launch (start us, length us, event | category | flops | bytes accessed | tf_op | source)
XLA Modules:
  0.0 135.7 jit_solution(7505567056743415634)
XLA Ops:
  0.6 131.9 %block.1 = (bf16[2,12,176,100]{3,2,1,0:T(8,128)(2,1)}, bf16[2,12,176,100]{3,2,1,0:T(8,128)(2,1)}, f32[208,128]{1,0:T(8,128)}, f32[176,128]{1,0:T(8,128)}, f32[16,8,128]{2,1,0:T(8,128)}) custom-call(bf16[66,176]{1,0:T(8,128)(2,1)} %bitcast.14, bf16[66,176]{1,0:T(8,128)(2,1)} %wpr.1, bf16[5,5,66]{2,1,0:T(8,128)(2,1)} %taps.1, bf16[44,66]{1,0:T(8,128)(2,1)} %bitcast.15, ...), custom_call_target="tpu_custom_call" | custom-call | tf_op jit(solution)/shard_map/block/pallas_call | solution.py:694
  132.5 3.2 %finish.1 = (f32[66,176]{1,0:T(8,128)}, f32[5,5,66]{2,1,0:T(8,128)}, f32[44,66]{1,0:T(8,128)}, f32[44,66]{1,0:T(8,128)}, f32[1,66]{1,0:T(1,128)}, /*index=5*/f32...) custom-call(f32[208,128]{1,0:T(8,128)} %get-tuple-element.23.early, ...), custom_call_target="tpu_custom_call" | custom-call | tf_op jit(solution)/shard_map/finish/pallas_call | solution.py:818

commit v9 on v8

--- a/solution.py
+++ b/solution.py
@@ -137,6 +137,19 @@
     return [y0, a + b, a - b, c + d, c - d, e + f, e - f, y3]
 
 
+def dot_split(left, right, dims):
+    high = left.astype(BF16)
+    rest = left - high.astype(F32)
+    middle = rest.astype(BF16)
+    low = (rest - middle.astype(F32)).astype(BF16)
+    parts = jnp.concatenate([high.astype(F32), middle.astype(F32), low.astype(F32)], axis=0)
+    product = lax.dot_general(
+        parts.astype(BF16), right.astype(BF16), (dims, ((), ())), preferred_element_type=F32
+    )
+    count = left.shape[0]
+    return (product[2 * count :] + product[count : 2 * count]) + product[:count]
+
+
 def spread_taps(taps, wide_taps, flip):
     for j in range(5):
         column = [taps[5 * i + j : 5 * i + j + 1, :] for i in range(5)]
@@ -147,28 +160,21 @@
             wide_taps[5 * p + place] = jnp.broadcast_to(value, (8, 128))
 
 
-def edge_columns(value):
-    split = value.reshape(BLOCK, 2, 8, 128)
-    block = lax.broadcasted_iota(jnp.int32, (2, 2, 8, 128), 2)
-    left = jnp.where(block > 0, pltpu.roll(split[BLOCK - 2 :], 1, 2), 0.0)
-    right = jnp.where(block < 7, pltpu.roll(split[:2], 7, 2), 0.0)
-    return left.reshape(2, SUB, 128), right.reshape(2, SUB, 128)
-
-
-def store_row(ref, r, value):
-    left, right = edge_columns(value)
-    ref[r, 0:2] = left
-    ref[r, 2 : 2 + BLOCK] = value
-    ref[r, 2 + BLOCK :] = right
+def with_edges(value):
+    block = lax.broadcasted_iota(jnp.int32, (2, 8, 128), 1)
+    left = jnp.where(block > 0, pltpu.roll(value[BLOCK - 2 :], 1, 1), 0.0)
+    right = jnp.where(block < 7, pltpu.roll(value[:2], 7, 1), 0.0)
+    return jnp.concatenate([left, value, right], axis=0)
 
 
 def conv_rows(ref, q, h, wide_taps):
     points = to_points([ref[4 * q + n, :, 8 * h : 8 * h + 8, :] for n in range(8)])
     totals = []
     for p in range(8):
-        total = points[p][0:BLOCK] * wide_taps[5 * p][None]
+        source = with_edges(points[p])
+        total = source[0:BLOCK] * wide_taps[5 * p][None]
         for j in range(1, 5):
-            total = total + points[p][j : j + BLOCK] * wide_taps[5 * p + j][None]
+            total = total + source[j : j + BLOCK] * wide_taps[5 * p + j][None]
         totals.append(total)
     return from_points(totals)
 
@@ -293,8 +299,8 @@
 
 def block_kernel(
     wet, wpr, taps, wrt, wx_own, bex, bred, feats_in, cot_in,
-    out, out_grad, early, late, mail_out,
-    feats, cot, stage, pack, full, top, bottom, flatw, fp, cp, fpt, cpt, we, wp, misc,
+    out, out_grad_to, early, late, mail_out,
+    out_grad, feats, cot, stage, pack, full, top, bottom, flatw, fp, cp, fpt, cpt, we, wp, misc,
     wide_taps, ex, dgs, coming_pre, coming_dg, saved, depth, sums, packed, landed, lanes, vecs, gates, msgs, mail,
     edge, above, below, gated, dpre, acc, held, flat, flat_taps,
     epiece, egot, espace, lpiece, lgot, lspace, tpiece, tgot, tspace,
@@ -432,7 +438,7 @@
         def expand(q, carry):
             for n in range(4):
                 value = swish(coming_pre[4 * q + n]).astype(BF16).astype(F32)
-                store_row(ex, 4 * q + n, value)
+                ex[4 * q + n] = value
             return carry
 
         lax.fori_loop(0, HROWS // 4, expand, 0)
@@ -491,12 +497,12 @@
     wx = misc[80 : 80 + SE, :]
     pooled = lanes[0:2, 0:CP] / AREA
     dgate = lanes[2:4, 0:CP]
-    squeeze_pre = dot_nt(pooled, wr, HIGH) + bred[...].astype(F32)
+    squeeze_pre = dot_split(pooled, wr, ((1,), (1,))) + bred[...].astype(F32)
     squeeze = swish(squeeze_pre)
-    gate = sigmoid(dot_nn(squeeze, wx, HIGH) + misc[128:129, :])
+    gate = sigmoid(dot_split(squeeze, wx, ((1,), (0,))) + misc[128:129, :])
     dlogit = dgate * gate * (1.0 - gate)
-    dsq = dot_nt(dlogit, wx, HIGH) * swish_grad(squeeze_pre)
-    dpooled = dot_nn(dsq, wr, HIGH)
+    dsq = dot_split(dlogit, wx, ((1,), (1,))) * swish_grad(squeeze_pre)
+    dpooled = dot_split(dsq, wr, ((1,), (0,)))
     gates[0:2, :] = gate
     gates[2:4, :] = dpooled / AREA
     gates[4:8, :] = jnp.zeros((4, CP), F32)
@@ -572,7 +578,7 @@
         spread_taps(misc[0:32, lane_of(t)], wide_taps, True)
 
         def middle(r, carry):
-            store_row(ex, r + 2, depth[t, r])
+            ex[r + 2] = depth[t, r]
             return carry
 
         lax.fori_loop(0, ROWS, middle, 0)
@@ -586,8 +592,8 @@
         for copy in edge_copies(t):
             copy.wait()
         for n in range(2):
-            store_row(ex, n, above[t, n].astype(F32) * has_top)
-            store_row(ex, ROWS + 2 + n, below[t, n].astype(F32) * has_bottom)
+            ex[n] = above[t, n].astype(F32) * has_top
+            ex[ROWS + 2 + n] = below[t, n].astype(F32) * has_bottom
 
         def conv(q, carry):
             both = []
@@ -631,12 +637,9 @@
         def window(q, carry):
             for h in range(2):
                 rows = slice(8 * h, 8 * h + 8)
-                for low, high in ((0, 9), (9, WIDE)):
-                    points = to_points(
-                        [saved[t, 4 * q + n].astype(F32)[low:high, rows, :] for n in range(8)]
-                    )
-                    for p in range(8):
-                        held[p, low:high] = points[p]
+                points = to_points([saved[t, 4 * q + n].astype(F32)[:, rows, :] for n in range(8)])
+                for p in range(8):
+                    held[p] = with_edges(points[p])
                 mine = outputs_to_points([depth[t, 4 * q + n, :, rows, :] for n in range(4)])
                 for p in range(8):
                     source = held[p]
@@ -667,6 +670,8 @@
         copy.start()
 
     all_channels_out(dpre, we, cp, 0, out_grad)
+    leave = pltpu.make_async_copy(out_grad, out_grad_to, insem.at[0])
+    leave.start()
     tspace[me_s] = dp_sum(copies, tpiece, tgot).astype(BF16)
     copies = to_space(tspace, usend, urecv)
     for copy in copies:
@@ -678,6 +683,7 @@
     early[0:C] = space_sum(to_space(espace, fsend, frecv), espace)
     late[...] = space_sum(to_space(lspace, gsend, grecv), lspace)
     early[C:] = space_sum(copies, tspace)
+    leave.wait()
 
 
 def block(*args):
@@ -701,8 +707,9 @@
             jax.ShapeDtypeStruct((ND, 8, 128), F32),
         ),
         in_specs=[VMEM] * 7 + [ANY] * 2,
-        out_specs=(VMEM,) * 5,
+        out_specs=(VMEM, ANY, VMEM, VMEM, VMEM),
         scratch_shapes=[
+            bf16(IMGS, ROWS, C, COLS),
             bf16(IMGS, ROWS, C, COLS),
             bf16(IMGS, ROWS, C, COLS),
             f32(2, 80, 256),
@@ -719,11 +726,11 @@
             bf16(CP, C),
             f32(136, CP),
             f32(40, 8, 128),
-            f32(HROWS, WIDE, SUB, 128),
+            f32(HROWS, BLOCK, SUB, 128),
             f32(ROWS, BLOCK, SUB, 128),
             f32(HROWS, BLOCK, SUB, 128),
             f32(ROWS, BLOCK, SUB, 128),
-            bf16(TILES, HROWS, WIDE, SUB, 128),
+            bf16(TILES, HROWS, BLOCK, SUB, 128),
             f32(TILES, ROWS, BLOCK, SUB, 128),
             f32(TILES, 8, 128),
             f32(5, 8, 128),

time: 136 us -> 130 us (0.956)
  Pallas kernels: 135 us -> 129 us
    pallas_call x1, Pallas kernels: 132 us -> 126 us  [block(): pl.pallas_call(block_kernel, out_shape=(jax.ShapeDtypeStruct((IMGS, ROWS,...]
where the time goes in v9:
time: 130 us
  Pallas kernels  129 us (99%)
    pallas_call x1, Pallas kernels, block(): pl.pallas_call(block_kernel, out_shape=(jax.ShapeDtypeStruct((IMGS, ROWS,...  126 us
    pallas_call x1, Pallas kernels, finish(): pl.pallas_call(finish_kernel, grid=(ROWS // 6,), out_shape=tuple((jax.Sha...  3.22 us

profile of v9, /device:TPU:1, one launch (start us, length us, event | category | flops | bytes accessed | tf_op | source)
XLA Modules:
  0.0 130.0 jit_solution(7323457273231576763)
XLA Ops:
  0.6 126.1 %block.1 = (bf16[2,12,176,100]{3,2,1,0:T(8,128)(2,1)}, bf16[2,12,176,100]{3,2,1,0:T(8,128)(2,1)}, f32[208,128]{1,0:T(8,128)}, f32[176,128]{1,0:T(8,128)}, f32[16,8,128]{2,1,0:T(8,128)}) custom-call(bf16[66,176]{1,0:T(8,128)(2,1)} %bitcast.14, bf16[66,176]{1,0:T(8,128)(2,1)} %wpr.1, bf16[5,5,66]{2,1,0:T(8,128)(2,1)} %taps.1, bf16[44,66]{1,0:T(8,128)(2,1)} %bitcast.15, ...), custom_call_target="tpu_custom_call" | custom-call | tf_op jit(solution)/shard_map/block/pallas_call | solution.py:700
  126.8 3.2 %finish.1 = (f32[66,176]{1,0:T(8,128)}, f32[5,5,66]{2,1,0:T(8,128)}, f32[44,66]{1,0:T(8,128)}, f32[44,66]{1,0:T(8,128)}, f32[1,66]{1,0:T(1,128)}, /*index=5*/f32...) custom-call(f32[208,128]{1,0:T(8,128)} %get-tuple-element.23.early, ...), custom_call_target="tpu_custom_call" | custom-call | tf_op jit(solution)/shard_map/finish/pallas_call | solution.py:825

commit v10 on v9

--- a/solution.py
+++ b/solution.py
@@ -40,6 +40,12 @@
     sig = sigmoid(value)
     act = value * sig
     return sig + act - act * sig
+
+
+def twice_swish_grad(value):
+    half = 0.5 * value
+    twice = 1.0 + jnp.tanh(half)
+    return twice * ((value - half * twice) + 1.0)
 
 
 def dot_nt(left, right, precision=None):
@@ -154,7 +160,7 @@
     for j in range(5):
         column = [taps[5 * i + j : 5 * i + j + 1, :] for i in range(5)]
         if flip:
-            column = column[::-1]
+            column = [0.5 * value for value in column[::-1]]
         place = 4 - j if flip else j
         for p, value in enumerate(point_taps(column)):
             wide_taps[5 * p + place] = jnp.broadcast_to(value, (8, 128))
@@ -186,11 +192,13 @@
 
 def gate_row(depth, dgated, gates, h, keep):
     gate = gates[h : h + 1, :][None]
-    pull = gates[2 + h : 3 + h, :][None]
-    sig = sigmoid(depth)
-    act = depth * sig
+    half_gate = gates[2 + h : 3 + h, :][None]
+    half_pull = gates[4 + h : 5 + h, :][None]
+    half = 0.5 * depth
+    twice = 1.0 + jnp.tanh(half)
+    act = half * twice
     gated = act * gate
-    ddepth = (dgated * gate + pull) * (sig + act - act * sig)
+    ddepth = (dgated * half_gate + half_pull) * (twice * ((depth - act) + 1.0))
     ddepth = jnp.concatenate([ddepth[:9], ddepth[9:] * keep], axis=0)
     return gated, ddepth
 
@@ -299,8 +307,8 @@
 
 def block_kernel(
     wet, wpr, taps, wrt, wx_own, bex, bred, feats_in, cot_in,
-    out, out_grad_to, early, late, mail_out,
-    out_grad, feats, cot, stage, pack, full, top, bottom, flatw, fp, cp, fpt, cpt, we, wp, misc,
+    out_to, out_grad_to, early, late, mail_out,
+    out, out_grad, feats, cot, stage, pack, full, top, bottom, flatw, fp, cp, fpt, cpt, we, wp, misc,
     wide_taps, ex, dgs, coming_pre, coming_dg, saved, depth, sums, packed, landed, lanes, vecs, gates, msgs, mail,
     edge, above, below, gated, dpre, acc, held, flat, flat_taps,
     epiece, egot, espace, lpiece, lgot, lspace, tpiece, tgot, tspace,
@@ -362,7 +370,8 @@
     )
     for copy in halo:
         copy.start()
-    full[core, me_d] = pack[core]
+    full[0, me_d] = pack[0]
+    full[1, me_d] = pack[1]
     spread = (one_hot(0, False), one_hot(1, False))
     gather_t = (one_hot(0, True), one_hot(1, True))
 
@@ -377,17 +386,20 @@
         for src, dst in ((feats, fpt), (cot, cpt)):
             value = dot_nn(src[0, r], gather_t[0]) + dot_nn(src[1, r], gather_t[1])
             dst[:, PIX * r : PIX * (r + 1)] = value.astype(BF16)
-    for copy in copies:
-        copy.wait()
-    share = pltpu.make_async_remote_copy(
-        src_ref=full.at[core],
-        dst_ref=full.at[core],
-        send_sem=csend,
-        recv_sem=crecv,
-        device_id=(me_s + 1 - 2 * core, me_d),
-        device_id_type=MESH,
-    )
-    share.start()
+    shares = []
+    for k, copy in enumerate(copies, 1):
+        copy.wait_recv()
+        sender = lax.rem(me_d + ND - k, ND)
+        share = pltpu.make_async_remote_copy(
+            src_ref=full.at[core, sender],
+            dst_ref=full.at[core, sender],
+            send_sem=csend.at[k],
+            recv_sem=crecv.at[k],
+            device_id=(me_s + 1 - 2 * core, me_d),
+            device_id_type=MESH,
+        )
+        share.start()
+        shares.append(share)
     for copy in halo:
         copy.wait()
     has_top = jnp.where(me_s > 0, 1.0, 0.0)
@@ -397,7 +409,10 @@
         fp[r] = (value * has_top).astype(BF16)
         value = dot_nt(spread[0], bottom[0, r]) + dot_nt(spread[1], bottom[1, r])
         fp[ROWS + 2 + r] = (value * has_bottom).astype(BF16)
-    share.wait()
+    for copy in copies:
+        copy.wait_send()
+    for share in shares:
+        share.wait()
     for half, whole in ((0, we), (1, wp)):
         for d in range(ND):
             part = full[half, d].astype(F32)
@@ -437,8 +452,7 @@
 
         def expand(q, carry):
             for n in range(4):
-                value = swish(coming_pre[4 * q + n]).astype(BF16).astype(F32)
-                ex[4 * q + n] = value
+                ex[4 * q + n] = swish(coming_pre[4 * q + n])
             return carry
 
         lax.fori_loop(0, HROWS // 4, expand, 0)
@@ -504,8 +518,9 @@
     dsq = dot_split(dlogit, wx, ((1,), (1,))) * swish_grad(squeeze_pre)
     dpooled = dot_split(dsq, wr, ((1,), (0,)))
     gates[0:2, :] = gate
-    gates[2:4, :] = dpooled / AREA
-    gates[4:8, :] = jnp.zeros((4, CP), F32)
+    gates[2:4, :] = 0.5 * gate
+    gates[4:6, :] = dpooled * (0.5 / AREA)
+    gates[6:8, :] = jnp.zeros((2, CP), F32)
     lanes[0:2, 0:CP] = pooled
     lanes[2:4, 0:CP] = dlogit
     vecs[...] = jnp.zeros((8, 128), F32)
@@ -545,7 +560,7 @@
                         h,
                         keep,
                     )
-                    depth[t, r, :, rows, :] = ddepth.astype(BF16).astype(F32)
+                    depth[t, r, :, rows, :] = ddepth
                     both.append(value)
                 gated[pl.ds(pl.multiple_of(r * PIX, PIX), PIX), lane_of(t)] = (
                     jnp.concatenate(both, axis=1).reshape(PIX, 128).astype(BF16)
@@ -585,7 +600,7 @@
 
         def slopes(q, carry):
             for n in range(4):
-                dgs[4 * q + n] = swish_grad(coming_pre[4 * q + n + 2])
+                dgs[4 * q + n] = twice_swish_grad(coming_pre[4 * q + n + 2])
             return carry
 
         lax.fori_loop(0, ROWS // 4, slopes, 0)
@@ -677,6 +692,8 @@
     for copy in copies:
         copy.start()
     all_channels_out(gated, wp, fp, 2, out)
+    leave_too = pltpu.make_async_copy(out, out_to, insem.at[1])
+    leave_too.start()
     for copy in small:
         copy.wait()
     mail_out[...] = mail[...]
@@ -684,6 +701,7 @@
     late[...] = space_sum(to_space(lspace, gsend, grecv), lspace)
     early[C:] = space_sum(copies, tspace)
     leave.wait()
+    leave_too.wait()
 
 
 def block(*args):
@@ -696,7 +714,6 @@
     def sems(*shape):
         return pltpu.SemaphoreType.DMA(shape)
 
-    one = pltpu.SemaphoreType.DMA
     return pl.pallas_call(
         block_kernel,
         out_shape=(
@@ -707,8 +724,9 @@
             jax.ShapeDtypeStruct((ND, 8, 128), F32),
         ),
         in_specs=[VMEM] * 7 + [ANY] * 2,
-        out_specs=(VMEM, ANY, VMEM, VMEM, VMEM),
+        out_specs=(ANY, ANY, VMEM, VMEM, VMEM),
         scratch_shapes=[
+            bf16(IMGS, ROWS, C, COLS),
             bf16(IMGS, ROWS, C, COLS),
             bf16(IMGS, ROWS, C, COLS),
             bf16(IMGS, ROWS, C, COLS),
@@ -762,8 +780,8 @@
             sems(ND),
             sems(2),
             sems(2),
-            one,
-            one,
+            sems(ND),
+            sems(ND),
             sems(NS),
             sems(NS),
             sems(ND),

time: 130 us -> 129 us (level)
    pallas_call x1, Pallas kernels: 126 us -> 125 us  [block(): pl.pallas_call(block_kernel, out_shape=(jax.ShapeDtypeStruct((IMGS, ROWS,...]
where the time goes in v10:
time: 129 us
  Pallas kernels  128 us (99%)
    pallas_call x1, Pallas kernels, block(): pl.pallas_call(block_kernel, out_shape=(jax.ShapeDtypeStruct((IMGS, ROWS,...  125 us
    pallas_call x1, Pallas kernels, finish(): pl.pallas_call(finish_kernel, grid=(ROWS // 6,), out_shape=tuple((jax.Sha...  3.22 us

profile of v10, /device:TPU:1, one launch (start us, length us, event | category | flops | bytes accessed | tf_op | source)
XLA Modules:
  0.0 128.6 jit_solution(15084752193655224917)
XLA Ops:
  0.6 124.7 %block.1 = (bf16[2,12,176,100]{3,2,1,0:T(8,128)(2,1)}, bf16[2,12,176,100]{3,2,1,0:T(8,128)(2,1)}, f32[208,128]{1,0:T(8,128)}, f32[176,128]{1,0:T(8,128)}, f32[16,8,128]{2,1,0:T(8,128)}) custom-call(bf16[66,176]{1,0:T(8,128)(2,1)} %bitcast.14, bf16[66,176]{1,0:T(8,128)(2,1)} %wpr.1, bf16[5,5,66]{2,1,0:T(8,128)(2,1)} %taps.1, bf16[44,66]{1,0:T(8,128)(2,1)} %bitcast.15, ...), custom_call_target="tpu_custom_call" | custom-call | tf_op jit(solution)/shard_map/block/pallas_call | solution.py:717
  125.4 3.2 %finish.1 = (f32[66,176]{1,0:T(8,128)}, f32[5,5,66]{2,1,0:T(8,128)}, f32[44,66]{1,0:T(8,128)}, f32[44,66]{1,0:T(8,128)}, f32[1,66]{1,0:T(1,128)}, /*index=5*/f32...) custom-call(f32[208,128]{1,0:T(8,128)} %get-tuple-element.23.early, ...), custom_call_target="tpu_custom_call" | custom-call | tf_op jit(solution)/shard_map/finish/pallas_call | solution.py:843

commit v11 on v10

--- a/solution.py
+++ b/solution.py
@@ -229,11 +229,24 @@
     lax.fori_loop(0, 3, lanes, 0)
 
 
+OFFSETS = sorted(
+    ((x, y) for x in range(4) for y in range(4) if x or y),
+    key=lambda at: -(min(at[0], 4 - at[0]) + min(at[1], 4 - at[1])),
+)
+
+
+def dp_peer(k, sign):
+    me_d = lax.axis_index("dp")
+    x, y = OFFSETS[k - 1]
+    column = lax.rem(lax.div(me_d, 4) + (x if sign > 0 else 4 - x), 4)
+    return 4 * column + lax.rem(lax.rem(me_d, 4) + (y if sign > 0 else 4 - y), 4)
+
+
 def to_dp(src, dst, send, recv, by_sender=False):
     me_s, me_d = lax.axis_index("space"), lax.axis_index("dp")
     copies = []
     for k in range(1, ND):
-        target = lax.rem(me_d + k, ND)
+        target = dp_peer(k, 1)
         copies.append(
             pltpu.make_async_remote_copy(
                 src_ref=src.at[target],
@@ -321,7 +334,7 @@
     barrier = pltpu.get_barrier_semaphore()
     for k in range(1, ND):
         pl.semaphore_signal(
-            barrier, inc=1, device_id=(me_s, lax.rem(me_d + k, ND)), device_id_type=MESH
+            barrier, inc=1, device_id=(me_s, dp_peer(k, 1)), device_id_type=MESH
         )
     for k in range(1, NS):
         pl.semaphore_signal(
@@ -353,7 +366,7 @@
             dst_ref=full.at[core, me_d],
             send_sem=wsend.at[k],
             recv_sem=wrecv.at[k],
-            device_id=(me_s, lax.rem(me_d + k, ND)),
+            device_id=(me_s, dp_peer(k, 1)),
             device_id_type=MESH,
         )
         copy.start()
@@ -389,7 +402,7 @@
     shares = []
     for k, copy in enumerate(copies, 1):
         copy.wait_recv()
-        sender = lax.rem(me_d + ND - k, ND)
+        sender = dp_peer(k, -1)
         share = pltpu.make_async_remote_copy(
             src_ref=full.at[core, sender],
             dst_ref=full.at[core, sender],
@@ -560,7 +573,7 @@
                         h,
                         keep,
                     )
-                    depth[t, r, :, rows, :] = ddepth
+                    depth[t, r, :, rows, :] = ddepth.astype(BF16).astype(F32)
                     both.append(value)
                 gated[pl.ds(pl.multiple_of(r * PIX, PIX), PIX), lane_of(t)] = (
                     jnp.concatenate(both, axis=1).reshape(PIX, 128).astype(BF16)

time: 129 us -> 126 us (0.977)
  Pallas kernels: 128 us -> 125 us
    pallas_call x1, Pallas kernels: 125 us -> 121 us  [block(): pl.pallas_call(block_kernel, out_shape=(jax.ShapeDtypeStruct((IMGS, ROWS,...]
where the time goes in v11:
time: 126 us; the launch traced here: 125 us
  Pallas kernels  125 us (99%)
    pallas_call x1, Pallas kernels, block(): pl.pallas_call(block_kernel, out_shape=(jax.ShapeDtypeStruct((IMGS, ROWS,...  121 us
    pallas_call x1, Pallas kernels, finish(): pl.pallas_call(finish_kernel, grid=(ROWS // 6,), out_shape=tuple((jax.Sha...  3.22 us

profile of v11, /device:TPU:1, one launch (start us, length us, event | category | flops | bytes accessed | tf_op | source)
XLA Modules:
  0.0 125.2 jit_solution(4152363827633174607)
XLA Ops:
  0.6 121.3 %block.1 = (bf16[2,12,176,100]{3,2,1,0:T(8,128)(2,1)}, bf16[2,12,176,100]{3,2,1,0:T(8,128)(2,1)}, f32[208,128]{1,0:T(8,128)}, f32[176,128]{1,0:T(8,128)}, f32[16,8,128]{2,1,0:T(8,128)}) custom-call(bf16[66,176]{1,0:T(8,128)(2,1)} %bitcast.14, bf16[66,176]{1,0:T(8,128)(2,1)} %wpr.1, bf16[5,5,66]{2,1,0:T(8,128)(2,1)} %taps.1, bf16[44,66]{1,0:T(8,128)(2,1)} %bitcast.15, ...), custom_call_target="tpu_custom_call" | custom-call | tf_op jit(solution)/shard_map/block/pallas_call | solution.py:730
  121.9 3.2 %finish.1 = (f32[66,176]{1,0:T(8,128)}, f32[5,5,66]{2,1,0:T(8,128)}, f32[44,66]{1,0:T(8,128)}, f32[44,66]{1,0:T(8,128)}, f32[1,66]{1,0:T(1,128)}, /*index=5*/f32...) custom-call(f32[208,128]{1,0:T(8,128)} %get-tuple-element.23.early, ...), custom_call_target="tpu_custom_call" | custom-call | tf_op jit(solution)/shard_map/finish/pallas_call | solution.py:856

commit v12 on v11

--- a/solution.py
+++ b/solution.py
@@ -263,7 +263,7 @@
 def to_space(ref, send, recv):
     me_s, me_d = lax.axis_index("space"), lax.axis_index("dp")
     copies = []
-    for k in range(1, NS):
+    for k in (4, 5, 3, 6, 2, 7, 1):
         copies.append(
             pltpu.make_async_remote_copy(
                 src_ref=ref.at[me_s],
@@ -539,13 +539,6 @@
     vecs[...] = jnp.zeros((8, 128), F32)
     vecs[4:6, 0:SE] = squeeze
     vecs[6:8, 0:SE] = dsq
-    for d in range(ND):
-        msgs[d, 0:4, :] = lanes[0:4, SLOT * d : SLOT * d + 128]
-        msgs[d, 4:8, :] = vecs[4:8, :]
-    mail[me_d] = msgs[me_d]
-    small = to_dp(msgs, mail, msend, mrecv, True)
-    for copy in small:
-        copy.start()
 
     def edge_copies(t):
         return to_neighbours(
@@ -695,6 +688,13 @@
     pieces_of(flat_taps, 32, tpiece)
     copies = to_dp(tpiece, tgot, tsend, trecv)
     for copy in copies:
+        copy.start()
+    for d in range(ND):
+        msgs[d, 0:4, :] = lanes[0:4, SLOT * d : SLOT * d + 128]
+        msgs[d, 4:8, :] = vecs[4:8, :]
+    mail[me_d] = msgs[me_d]
+    small = to_dp(msgs, mail, msend, mrecv, True)
+    for copy in small:
         copy.start()
 
     all_channels_out(dpre, we, cp, 0, out_grad)

time: 126 us -> 125 us (level)
  no operation moved by 1% of the time
where the time goes in v12:
time: 125 us
  Pallas kernels  124 us (99%)
    pallas_call x1, Pallas kernels, block(): pl.pallas_call(block_kernel, out_shape=(jax.ShapeDtypeStruct((IMGS, ROWS,...  121 us
    pallas_call x1, Pallas kernels, finish(): pl.pallas_call(finish_kernel, grid=(ROWS // 6,), out_shape=tuple((jax.Sha...  3.22 us

profile of v12, /device:TPU:1, one launch (start us, length us, event | category | flops | bytes accessed | tf_op | source)
XLA Modules:
  0.0 124.9 jit_solution(14022386450403865651)
XLA Ops:
  0.6 121.0 %block.1 = (bf16[2,12,176,100]{3,2,1,0:T(8,128)(2,1)}, bf16[2,12,176,100]{3,2,1,0:T(8,128)(2,1)}, f32[208,128]{1,0:T(8,128)}, f32[176,128]{1,0:T(8,128)}, f32[16,8,128]{2,1,0:T(8,128)}) custom-call(bf16[66,176]{1,0:T(8,128)(2,1)} %bitcast.14, bf16[66,176]{1,0:T(8,128)(2,1)} %wpr.1, bf16[5,5,66]{2,1,0:T(8,128)(2,1)} %taps.1, bf16[44,66]{1,0:T(8,128)(2,1)} %bitcast.15, ...), custom_call_target="tpu_custom_call" | custom-call | tf_op jit(solution)/shard_map/block/pallas_call | solution.py:730
  121.7 3.2 %finish.1 = (f32[66,176]{1,0:T(8,128)}, f32[5,5,66]{2,1,0:T(8,128)}, f32[44,66]{1,0:T(8,128)}, f32[44,66]{1,0:T(8,128)}, f32[1,66]{1,0:T(1,128)}, /*index=5*/f32...) custom-call(f32[208,128]{1,0:T(8,128)} %get-tuple-element.23.early, ...), custom_call_target="tpu_custom_call" | custom-call | tf_op jit(solution)/shard_map/finish/pallas_call | solution.py:856

commit v13 on v12

--- a/solution.py
+++ b/solution.py
@@ -465,7 +465,7 @@
 
         def expand(q, carry):
             for n in range(4):
-                ex[4 * q + n] = swish(coming_pre[4 * q + n])
+                ex[4 * q + n] = swish(coming_pre[4 * q + n]).astype(BF16).astype(F32)
             return carry
 
         lax.fori_loop(0, HROWS // 4, expand, 0)

time: 125 us -> 126 us (level)
  no operation moved by 1% of the time
where the time goes in v13:
time: 126 us; the launch traced here: 125 us
  Pallas kernels  125 us (99%)
    pallas_call x1, Pallas kernels, block(): pl.pallas_call(block_kernel, out_shape=(jax.ShapeDtypeStruct((IMGS, ROWS,...  122 us
    pallas_call x1, Pallas kernels, finish(): pl.pallas_call(finish_kernel, grid=(ROWS // 6,), out_shape=tuple((jax.Sha...  3.22 us

profile of v13, /device:TPU:1, one launch (start us, length us, event | category | flops | bytes accessed | tf_op | source)
XLA Modules:
  0.0 125.4 jit_solution(6425840291036385185)
XLA Ops:
  0.6 121.5 %block.1 = (bf16[2,12,176,100]{3,2,1,0:T(8,128)(2,1)}, bf16[2,12,176,100]{3,2,1,0:T(8,128)(2,1)}, f32[208,128]{1,0:T(8,128)}, f32[176,128]{1,0:T(8,128)}, f32[16,8,128]{2,1,0:T(8,128)}) custom-call(bf16[66,176]{1,0:T(8,128)(2,1)} %bitcast.14, bf16[66,176]{1,0:T(8,128)(2,1)} %wpr.1, bf16[5,5,66]{2,1,0:T(8,128)(2,1)} %taps.1, bf16[44,66]{1,0:T(8,128)(2,1)} %bitcast.15, ...), custom_call_target="tpu_custom_call" | custom-call | tf_op jit(solution)/shard_map/block/pallas_call | solution.py:730
  122.2 3.2 %finish.1 = (f32[66,176]{1,0:T(8,128)}, f32[5,5,66]{2,1,0:T(8,128)}, f32[44,66]{1,0:T(8,128)}, f32[44,66]{1,0:T(8,128)}, f32[1,66]{1,0:T(1,128)}, /*index=5*/f32...) custom-call(f32[208,128]{1,0:T(8,128)} %get-tuple-element.23.early, ...), custom_call_target="tpu_custom_call" | custom-call | tf_op jit(solution)/shard_map/finish/pallas_call | solution.py:856
